TPU v7x, 32 devices: a whole 2x2x4 slice. The times are simulated.
32 devices in a mesh: doc: 8 (over y, x, core), lab: 4 (over z).
Axes of the slice: x: 2, y: 2, z: 4, core: 2. Of those that a mesh axis runs over, the one named last changes fastest.
Arguments:
- embeddings: bfloat16 [16384, 768], P(('doc', 'lab')), may hold values from -6 to 6
- positives: int32 [16384, 16], P(('doc', 'lab')), may hold values from 0 to 4095, as said below
- weights: float32 [8192, 768], P(('doc', 'lab')), may hold values from -6 to 6
- parents: int32 [8192], replicated, may hold values from 0 to 254, as said below
- owners: int32 [4, 8], replicated, may hold values from 0 to 3
- shortlist: int32 [4, 32, 4], replicated, may hold values from 0 to 3, as said below
- counts: int32 [4, 32], replicated, may hold values from 1 to 4, as said below
Outputs:
- trained: float32 [8192, 768], P(('doc', 'lab'))
- momentum: float32 [8192, 768], P(('doc', 'lab'))
Inputs may be any that keep to these rules, and one draw needn't show every extreme that they name: `positives`: each positive code is (s * 4 + j) * 256 + l with s < 4, j < 4, l < 256; repeats allowed. parents[l] is a row of l's own block below l's row; row 0 of a block is its own parent. `shortlist`: the 4 tile numbers of one step and block are distinct. `counts`: in every step some block has all 4 slots live.
All inputs are finite; a program needn't handle non-finite values.
Results may differ from a plain program's by a relative error of at most 0.0003.
Values may be sent and summed in bfloat16 or wider, within the bound.
No kernel may reach another device: no remote copies, remote signals or barrier semaphores. Data moves between devices by JAX's collectives and lax.ppermute only.
A program may use at most 64 MiB of HBM per device.

v0:
```python
import jax
import jax.numpy as jnp
from jax import lax
from jax.sharding import PartitionSpec as P

TILE = 128
STEPS = 4


learning_rate = 0.1
beta_rate = 0.9
pull_rate = 1.0


def from_root(value, axis, source):
    kept = jnp.where(lax.axis_index(axis) == source, value, 0).astype(value.dtype)
    return lax.psum(kept, axis)


def from_behind(value, axis, by):
    length = lax.axis_size(axis)
    return lax.ppermute(value, axis, [(i, (i + by) % length) for i in range(length)])


def pick_rows(panel, labels, tiles, tile_rows):
    width = panel.shape[1]
    shaped = panel.reshape(panel.shape[0] // tile_rows, tile_rows, width)
    lshaped = labels.reshape(labels.shape[0] // tile_rows, tile_rows, labels.shape[1])
    rows = jnp.take(shaped, tiles, axis=0).reshape(tiles.shape[0] * tile_rows, width)
    picked = jnp.take(lshaped, tiles, axis=0).reshape(tiles.shape[0] * tile_rows, labels.shape[1])
    return (rows, picked)


def block_update(weight, moment, rows, picked, base, parent_rows, live):
    scale = 1.0 / jnp.sqrt(jnp.float32(rows.shape[1]))
    rows32 = rows.astype(jnp.float32)
    scores = (
        jnp.dot(
            rows32, weight.T, precision=lax.Precision.HIGHEST, preferred_element_type=jnp.float32
        )
        * scale
    )
    label_ids = base + jnp.arange(weight.shape[0], dtype=jnp.int32)
    target = jnp.any(picked[:, :, None] == label_ids[None, None, :], axis=1).astype(jnp.float32)
    resid = (jax.nn.sigmoid(scores) - target) * live[:, None]
    grad = (
        jnp.dot(
            resid.T, rows32, precision=lax.Precision.HIGHEST, preferred_element_type=jnp.float32
        )
        * scale
    )
    grad = grad + pull_rate * (weight - jnp.take(weight, parent_rows, axis=0))
    moment = beta_rate * moment + grad
    return (weight - learning_rate * moment, moment)


def local(embeddings, positives, weights, parents, owners, shortlist, counts):
    doc_index = lax.axis_index("doc")
    lab_index = lax.axis_index("lab")
    doc_count = lax.axis_size("doc")
    lab_count = lax.axis_size("lab")
    block_rows = weights.shape[0]
    tile_rows = TILE
    slots = shortlist.shape[2]
    slot_of_row = jnp.arange(slots * tile_rows, dtype=jnp.int32) // tile_rows
    weight = weights
    moment = jnp.zeros_like(weights)
    for step in range(STEPS):
        root = owners[step, doc_index]
        panel = from_root(embeddings, "lab", root)
        labels = from_root(positives, "lab", root)
        met_block = (doc_index - step) % doc_count * lab_count + lab_index
        if step > 0:
            weight, moment = from_behind((weight, moment), "doc", 1)
        tiles = lax.dynamic_index_in_dim(shortlist[step], met_block, 0, keepdims=False)
        rows, picked = pick_rows(panel, labels, tiles, tile_rows)
        live = (slot_of_row < counts[step, met_block]).astype(jnp.float32)
        parent_rows = lax.dynamic_slice_in_dim(parents, met_block * block_rows, block_rows, 0)
        code_base = (step * lab_count + lab_index) * block_rows
        weight, moment = block_update(weight, moment, rows, picked, code_base, parent_rows, live)
    weight, moment = from_behind((weight, moment), "doc", -(STEPS - 1))
    return (weight, moment)


def solution(mesh):
    return jax.shard_map(
        local,
        mesh=mesh,
        in_specs=(
            P(("doc", "lab"), None),
            P(("doc", "lab"), None),
            P(("doc", "lab"), None),
            P(),
            P(),
            P(),
            P(),
        ),
        out_specs=(P(("doc", "lab"), None), P(("doc", "lab"), None)),
        check_vma=False,
    )
```

profile of v0, /device:TPU:3, one launch (start us, length us, event | category | flops | bytes accessed | tf_op | source)
XLA Modules:
  0.0 292.1 jit_solution(11844188458083857288)
XLA Ops:
  7.2 1.4 constant_dynamic-slice_fusion.5
  13.3 2.8 broadcast_select_fusion.4
  23.0 24.6 %all-reduce.5.cloned.1.call-done = (s32[4,128,16]{1,2,0:T(8,128)}, s32[4,128,16]{1,2,0:T(8,128)}, s32[4,128,16]{1,2,0:T(8,128)}, s32[4,128,16]{1,2,0:T(8,128)}) async-done(((s32[4,128,16]{1,2,0:T(8,128)}, s32[4,128,16]{1,2,0:T(8,128)}, s32[4,128,16]{1,2,0:T(8,128)}, s32[4,128,16]{1,2,0:T(8,128)}), (s32[4,128,16]{1,2,0:T(8,128)}, s32[4,128,16]{1,2,0:T(8,128)}, s32[4,128,16]{1,2,0:T(8,128)}, ...) | async-done | bytes 131088 | tf_op jit(solution)/shard_map/psum | solution.py:17
  49.0 5.9 %compare_reduce_fusion.3 = pred[512,256]{1,0:T(8,128)(4,1)S(1)} fusion(s32[256]{0:T(256)S(1)} %iota_add_fusion.3, s32[512,16]{1,0:T(8,128)S(1)} %bitcast.64), kind=kLoop, calls=%fused_computation.15 | loop fusion | flops 4063232 | bytes 164864 | tf_op jit(solution)/shard_map/reduce_or | solution.py:44
  54.9 119.6 %all-reduce.7.cloned.1.call-done = (bf16[4,128,768]{2,1,0:T(8,128)(2,1)}, bf16[4,128,768]{2,1,0:T(8,128)(2,1)}, bf16[4,128,768]{2,1,0:T(8,128)(2,1)}, bf16[4,128,768]{2,1,0:T(8,128)(2,1)}) async-done(((bf16[4,128,768]{2,1,0:T(8,128)(2,1)}, bf16[4,128,768]{2,1,0:T(8,128)(2,1)}, bf16[4,128,768]{2,1,0:T(8,128)(2,1)}, bf16[4,128,768]{2,1,0:T(8,128)(2,1)}), (bf16[4,128,768]{2,1,0:T(8,128)(2,1)}, ...) | async-done | bytes 3145744 | tf_op jit(solution)/shard_map/psum | solution.py:17
  174.6 1.7 gather_fusion
  177.4 1.8 multiply_subtract_fusion.3
  179.2 1.8 collective-permute-start
  181.8 5.9 %compare_reduce_fusion.2 = pred[512,256]{1,0:T(8,128)(4,1)S(1)} fusion(s32[256]{0:T(256)S(1)} %iota_add_fusion.2, s32[512,16]{1,0:T(8,128)S(1)} %bitcast.65), kind=kLoop, calls=%fused_computation.14 | loop fusion | flops 4063232 | bytes 164864 | tf_op jit(solution)/shard_map/reduce_or | solution.py:44
  187.7 1.7 gather_fusion.3
  193.2 5.4 %collective-permute-done.1 = f32[256,768]{1,0:T(8,128)} collective-permute-done((f32[256,768]{1,0:T(8,128)S(1)}, f32[256,768]{1,0:T(8,128)}, u32[]{:S(2)}, u32[]{:S(2)}) %collective-permute-start.1) | collective-permute-done | bytes 786464 | tf_op jit(solution)/shard_map/ppermute | solution.py:22
  198.6 2.3 multiply_subtract_fusion.2
  200.9 3.5 %collective-permute-start.2 = (f32[256,768]{1,0:T(8,128)}, f32[256,768]{1,0:T(8,128)S(1)}, u32[]{:S(2)}, u32[]{:S(2)}) collective-permute-start(f32[256,768]{1,0:T(8,128)} %get-tuple-element.21), channel_id=1, source_target_pairs={{0,4},{4,8},{8,12},{12,16},{16,20},{20,24},{24,28},{28,0},{1,5},{5... | collective-permute-start | bytes 2359304 | tf_op jit(solution)/shard_map/ppermute | solution.py:22
  205.2 5.9 %compare_reduce_fusion.1 = pred[512,256]{1,0:T(8,128)(4,1)S(1)} fusion(s32[256]{0:T(256)S(1)} %iota_add_fusion.1, s32[512,16]{1,0:T(8,128)S(1)} %bitcast.66), kind=kLoop, calls=%fused_computation.13 | loop fusion | flops 4063232 | bytes 164864 | tf_op jit(solution)/shard_map/reduce_or | solution.py:44
  212.1 1.6 collective-permute-done.2
  216.6 5.4 %collective-permute-done.3 = f32[256,768]{1,0:T(8,128)} collective-permute-done((f32[256,768]{1,0:T(8,128)S(1)}, f32[256,768]{1,0:T(8,128)}, u32[]{:S(2)}, u32[]{:S(2)}) %collective-permute-start.3) | collective-permute-done | bytes 786464 | tf_op jit(solution)/shard_map/ppermute | solution.py:22
  222.0 2.3 multiply_subtract_fusion.1
  224.3 3.5 %collective-permute-start.4 = (f32[256,768]{1,0:T(8,128)}, f32[256,768]{1,0:T(8,128)S(1)}, u32[]{:S(2)}, u32[]{:S(2)}) collective-permute-start(f32[256,768]{1,0:T(8,128)} %get-tuple-element.17), channel_id=1, source_target_pairs={{0,4},{4,8},{8,12},{12,16},{16,20},{20,24},{24,28},{28,0},{1,5},{5... | collective-permute-start | bytes 2359304 | tf_op jit(solution)/shard_map/ppermute | solution.py:22
  228.6 5.9 %compare_reduce_fusion = pred[512,256]{1,0:T(8,128)(4,1)S(1)} fusion(s32[256]{0:T(256)S(1)} %iota_add_fusion, s32[512,16]{1,0:T(8,128)S(1)} %bitcast.67), kind=kLoop, calls=%fused_computation.12 | loop fusion | flops 4063232 | bytes 164864 | tf_op jit(solution)/shard_map/reduce_or | solution.py:44
  235.3 1.8 collective-permute-done.4
  240.0 5.4 %collective-permute-done.5 = f32[256,768]{1,0:T(8,128)} collective-permute-done((f32[256,768]{1,0:T(8,128)S(1)}, f32[256,768]{1,0:T(8,128)}, u32[]{:S(2)}, u32[]{:S(2)}) %collective-permute-start.5) | collective-permute-done | bytes 786464 | tf_op jit(solution)/shard_map/ppermute | solution.py:22
  246.8 2.6 collective-permute-start.6
  249.5 25.5 %collective-permute-done.6 = f32[256,768]{1,0:T(8,128)S(1)} collective-permute-done((f32[256,768]{1,0:T(8,128)S(1)}, f32[256,768]{1,0:T(8,128)S(1)}, u32[]{:S(2)}, u32[]{:S(2)}) %collective-permute-start.6) | collective-permute-done | bytes 786464 | tf_op jit(solution)/shard_map/ppermute | solution.py:22
  275.1 8.4 %collective-permute-done.7 = f32[256,768]{1,0:T(8,128)S(1)} collective-permute-done((f32[256,768]{1,0:T(8,128)S(1)}, f32[256,768]{1,0:T(8,128)S(1)}, u32[]{:S(2)}, u32[]{:S(2)}) %collective-permute-start.7) | collective-permute-done | bytes 786464 | tf_op jit(solution)/shard_map/ppermute | solution.py:22
  (87 shorter events, 28.1 us)
Async XLA Ops:
  7.2 40.4 %all-reduce.5.cloned.1.call-start = ((), (), s32[]{:S(2)}) async-start(), calls=%async_computation | async-start | bytes 262144 | tf_op jit(solution)/shard_map/psum | solution.py:17
  13.2 161.3 %all-reduce.7.cloned.1.call-start = ((), (), s32[]{:S(2)}) async-start(), calls=%async_computation.1 | async-start | bytes 6291456 | tf_op jit(solution)/shard_map/psum | solution.py:17
  16.1 0.7 copy-start.6
  16.1 1.9 copy-start
  18.1 1.5 copy-start.7
  177.4 3.6 %copy-start.3 = (s32[4,128,16]{1,2,0:T(8,128)S(1)}, s32[4,128,16]{1,2,0:T(8,128)}, u32[]{:S(2)}) copy-start(s32[4,128,16]{1,2,0:T(8,128)} %get-tuple-element.6) | copy-start | bytes 98308
  179.2 11.0 %collective-permute-start = (f32[256,768]{1,0:T(8,128)}, f32[256,768]{1,0:T(8,128)S(1)}, u32[]{:S(2)}, u32[]{:S(2)}) collective-permute-start(f32[256,768]{1,0:T(8,128)} %get-tuple-element.53), channel_id=1, source_target_pairs={{0,4},{4,8},{8,12},{12,16},{16,20},{20,24},{24,28},{28,0},{1,5},{5... | collective-permute-start | bytes 2359304 | tf_op jit(solution)/shard_map/ppermute | solution.py:22
  189.4 9.2 %collective-permute-start.1 = (f32[256,768]{1,0:T(8,128)S(1)}, f32[256,768]{1,0:T(8,128)}, u32[]{:S(2)}, u32[]{:S(2)}) collective-permute-start(f32[256,768]{1,0:T(8,128)S(1)} %get-tuple-element.54), channel_id=1, source_target_pairs={{0,4},{4,8},{8,12},{12,16},{16,20},{20,24},{24,28},{28,0},{1,5},{5... | collective-permute-start | bytes 2359304 | tf_op jit(solution)/shard_map/ppermute | solution.py:22
  198.6 5.8 %copy-start.2 = (s32[4,128,16]{1,2,0:T(8,128)S(1)}, s32[4,128,16]{1,2,0:T(8,128)}, u32[]{:S(2)}) copy-start(s32[4,128,16]{1,2,0:T(8,128)} %get-tuple-element.7) | copy-start | bytes 98308
  200.9 10.2 %copy-start.5 = (bf16[4,128,768]{2,1,0:T(8,128)(2,1)S(1)}, bf16[4,128,768]{2,1,0:T(8,128)(2,1)}, u32[]{:S(2)}) copy-start(bf16[4,128,768]{2,1,0:T(8,128)(2,1)} %get-tuple-element.11) | copy-start | bytes 2359300
  200.9 12.7 %collective-permute-start.2 = (f32[256,768]{1,0:T(8,128)}, f32[256,768]{1,0:T(8,128)S(1)}, u32[]{:S(2)}, u32[]{:S(2)}) collective-permute-start(f32[256,768]{1,0:T(8,128)} %get-tuple-element.21), channel_id=1, source_target_pairs={{0,4},{4,8},{8,12},{12,16},{16,20},{20,24},{24,28},{28,0},{1,5},{5... | collective-permute-start | bytes 2359304 | tf_op jit(solution)/shard_map/ppermute | solution.py:22
  211.7 10.3 %collective-permute-start.3 = (f32[256,768]{1,0:T(8,128)S(1)}, f32[256,768]{1,0:T(8,128)}, u32[]{:S(2)}, u32[]{:S(2)}) collective-permute-start(f32[256,768]{1,0:T(8,128)S(1)} %get-tuple-element.22), channel_id=1, source_target_pairs={{0,4},{4,8},{8,12},{12,16},{16,20},{20,24},{24,28},{28,0},{1,5},{5... | collective-permute-start | bytes 2359304 | tf_op jit(solution)/shard_map/ppermute | solution.py:22
  222.0 5.8 %copy-start.1 = (s32[4,128,16]{1,2,0:T(8,128)S(1)}, s32[4,128,16]{1,2,0:T(8,128)}, u32[]{:S(2)}) copy-start(s32[4,128,16]{1,2,0:T(8,128)} %get-tuple-element.8) | copy-start | bytes 98308
  224.3 10.2 %copy-start.4 = (bf16[4,128,768]{2,1,0:T(8,128)(2,1)S(1)}, bf16[4,128,768]{2,1,0:T(8,128)(2,1)}, u32[]{:S(2)}) copy-start(bf16[4,128,768]{2,1,0:T(8,128)(2,1)} %get-tuple-element.12) | copy-start | bytes 2359300
  224.3 12.7 %collective-permute-start.4 = (f32[256,768]{1,0:T(8,128)}, f32[256,768]{1,0:T(8,128)S(1)}, u32[]{:S(2)}, u32[]{:S(2)}) collective-permute-start(f32[256,768]{1,0:T(8,128)} %get-tuple-element.17), channel_id=1, source_target_pairs={{0,4},{4,8},{8,12},{12,16},{16,20},{20,24},{24,28},{28,0},{1,5},{5... | collective-permute-start | bytes 2359304 | tf_op jit(solution)/shard_map/ppermute | solution.py:22
  235.1 10.3 %collective-permute-start.5 = (f32[256,768]{1,0:T(8,128)S(1)}, f32[256,768]{1,0:T(8,128)}, u32[]{:S(2)}, u32[]{:S(2)}) collective-permute-start(f32[256,768]{1,0:T(8,128)S(1)} %get-tuple-element.18), channel_id=1, source_target_pairs={{0,4},{4,8},{8,12},{12,16},{16,20},{20,24},{24,28},{28,0},{1,5},{5... | collective-permute-start | bytes 2359304 | tf_op jit(solution)/shard_map/ppermute | solution.py:22
  246.8 28.2 %collective-permute-start.6 = (f32[256,768]{1,0:T(8,128)S(1)}, f32[256,768]{1,0:T(8,128)S(1)}, u32[]{:S(2)}, u32[]{:S(2)}) collective-permute-start(f32[256,768]{1,0:T(8,128)S(1)} %get-tuple-element.13), channel_id=1, source_target_pairs={{0,20},{4,24},{8,28},{12,0},{16,4},{20,8},{24,12},{28,16},{1,21},{... | collective-permute-start | bytes 2359304 | tf_op jit(solution)/shard_map/ppermute | solution.py:22
  249.4 34.0 %collective-permute-start.7 = (f32[256,768]{1,0:T(8,128)S(1)}, f32[256,768]{1,0:T(8,128)S(1)}, u32[]{:S(2)}, u32[]{:S(2)}) collective-permute-start(f32[256,768]{1,0:T(8,128)S(1)} %get-tuple-element.14), channel_id=1, source_target_pairs={{0,20},{4,24},{8,28},{12,0},{16,4},{20,8},{24,12},{28,16},{1,21},{... | collective-permute-start | bytes 2359304 | tf_op jit(solution)/shard_map/ppermute | solution.py:22
Sparse Core Ops, SparseCore 0:
  13.3 34.1 all-reduce.4
  50.9 123.6 all-reduce.6
where the time goes:
time: 293 us; the launch traced here: 292 us
  waiting for transfers between devices  198 us (68%)
  other arithmetic  37.6 us (13%)
  local copies, waits for them, and re-layouts  18.9 us (6%)
  between operations  17.1 us (6%)
  starting transfers between devices  11.9 us (4%)
  matrix products  8.22 us (3%)
    psum x2, waiting for transfers between devices, from_root(): return lax.psum(kept, axis)  144 us
    ppermute x8, waiting for transfers between devices, from_behind(): lax.ppermute(value, axis, [(i, (i + by) % length) for i in range(length)])  54.1 us
    reduce_or x4, other arithmetic, block_update(): jnp.any(picked[:, :, None] == label_ids[None, None, :], axis=1)  23.6 us
    ppermute x8, starting transfers between devices, from_behind(): lax.ppermute(value, axis, [(i, (i + by) % length) for i in range(length)])  11.8 us
    sub x3, other arithmetic, block_update(): return (weight - learning_rate * moment, moment)  6.09 us
  transfers between devices with their start and end apart: 10, of which 10 were waited for; matrix products, arithmetic and copies ran while one was open for 16% of the time, Pallas kernels for 0%

commit v1 on v0

v1 whole, which is shorter than its diff:
```python
import functools

import jax
import jax.numpy as jnp
from jax import lax
from jax.experimental import pallas as pl
from jax.experimental.pallas import tpu as pltpu
from jax.sharding import PartitionSpec as P

TILE = 128
STEPS = 4
CHUNKS = 2
CODE_ROWS = 16

learning_rate = 0.1
beta_rate = 0.9
pull_rate = 1.0

VMEM = pl.BlockSpec(memory_space=pltpu.VMEM)
SMEM = pl.BlockSpec(memory_space=pltpu.SMEM)
ANY = pl.BlockSpec(memory_space=pl.ANY)


def select_kernel(n, which_ref, *refs):
    sources, outs, sem = refs[:n], refs[n:-1], refs[-1]
    for k, out in enumerate(outs):
        for i, source in enumerate(sources):

            @pl.when(which_ref[k] == i)
            def _(source=source, out=out, k=k):
                pltpu.make_async_copy(source, out, sem.at[k]).start()

    for k, out in enumerate(outs):
        pltpu.make_async_copy(sources[0], out, sem.at[k]).wait()


def select(which, sources, count):
    shape = jax.ShapeDtypeStruct(sources[0].shape, sources[0].dtype)
    size = sources[0].size * sources[0].dtype.itemsize
    return pl.pallas_call(
        functools.partial(select_kernel, len(sources)),
        out_shape=[shape] * count,
        in_specs=[SMEM] + [ANY] * len(sources),
        out_specs=[ANY] * count,
        scratch_shapes=[pltpu.SemaphoreType.DMA((count,))],
        cost_estimate=pl.CostEstimate(flops=0, bytes_accessed=2 * count * size, transcendentals=0),
        name="select_panels",
    )(which, *sources)


def split(value):
    high = value.astype(jnp.bfloat16)
    return high, (value - high.astype(jnp.float32)).astype(jnp.bfloat16)


def product(pair, other, dims):
    dot = functools.partial(
        lax.dot_general, dimension_numbers=(dims, ((), ())), preferred_element_type=jnp.float32
    )
    return dot(pair[1], other) + dot(pair[0], other)


def update_kernel(first, rows, scale, flags_ref, *refs):
    panels, refs = refs[:CHUNKS], refs[CHUNKS:]
    if first:
        parents_ref, weight_ref, weight_out, moment_out = refs
    else:
        parents_ref, weight_ref, moment_ref, weight_out, moment_out = refs
    labels = weight_ref.shape[0]
    weight = weight_ref[...]
    pair = split(weight)
    label = lax.broadcasted_iota(jnp.int32, (labels, rows), 0).astype(jnp.float32)
    group = flags_ref[0].astype(jnp.float32)
    grad = jnp.zeros(weight.shape, jnp.float32)
    for c, panel_ref in enumerate(panels):
        panel = panel_ref[:rows, :]
        codes = panel_ref[rows:, :].astype(jnp.float32)
        own = jnp.where(codes[:, rows : 2 * rows] == group, codes[:, :rows], -1.0)
        hit = label == own[0:1, :]
        for k in range(1, CODE_ROWS):
            hit = hit | (label == own[k : k + 1, :])
        scores = product(pair, panel, ((1,), (1,))) * scale
        resid = jax.nn.sigmoid(scores) - jnp.where(hit, 1.0, 0.0)
        parts = []
        for t in range(rows // TILE):
            live = flags_ref[1 + c * (rows // TILE) + t].astype(jnp.float32)
            parts.append(resid[:, t * TILE : (t + 1) * TILE] * live)
        resid = jnp.concatenate(parts, axis=1)
        grad = grad + product(split(resid), panel, ((1,), (0,)))
    column = lax.broadcasted_iota(jnp.int32, (labels, labels), 1)
    pick = (column == parents_ref[...]).astype(jnp.bfloat16)
    rest = (weight - pair[0].astype(jnp.float32) - pair[1].astype(jnp.float32)).astype(jnp.bfloat16)
    dot = functools.partial(jnp.dot, preferred_element_type=jnp.float32)
    parent = dot(pick, rest) + dot(pick, pair[1]) + dot(pick, pair[0])
    grad = grad * scale + pull_rate * (weight - parent)
    moment = grad if first else beta_rate * moment_ref[...] + grad
    moment_out[...] = moment
    weight_out[...] = weight - learning_rate * moment


def update(flags, panels, rows, parents, weight, moment):
    labels, width = weight.shape
    first = moment is None
    state = [weight] if first else [weight, moment]
    shape = jax.ShapeDtypeStruct(weight.shape, jnp.float32)
    flops = 8 * labels * width * rows * CHUNKS
    size = 2 * rows * CHUNKS * width + 16 * labels * width
    return pl.pallas_call(
        functools.partial(update_kernel, first, rows, 1.0 / float(width) ** 0.5),
        out_shape=[shape, shape],
        in_specs=[SMEM] + [VMEM] * (len(panels) + 1 + len(state)),
        out_specs=[VMEM, VMEM],
        compiler_params=pltpu.CompilerParams(vmem_limit_bytes=32 * 1024 * 1024),
        cost_estimate=pl.CostEstimate(
            flops=flops, bytes_accessed=size, transcendentals=labels * rows * CHUNKS
        ),
        name="update_block",
    )(flags, *panels, parents, *state)


def gather_line(value, axis):
    n = lax.axis_size(axis)
    up, down = [value], [value]
    for r in range(1, n):
        up.append(lax.ppermute(up[-1], axis, [(i, i + 1) for i in range(r - 1, n - 1)]))
        down.append(lax.ppermute(down[-1], axis, [(i, i - 1) for i in range(1, n - r + 1)]))
    return up[:0:-1] + down


def local(embeddings, positives, weights, parents, owners, shortlist, counts):
    doc_index = lax.axis_index("doc")
    lab_index = lax.axis_index("lab")
    doc_count = lax.axis_size("doc")
    lab_count = lax.axis_size("lab")
    labels, width = weights.shape
    rows = embeddings.shape[0] // CHUNKS
    tiles = embeddings.shape[0] // TILE
    home = doc_index * lab_count + lab_index

    groups = positives // labels
    within = positives - groups * labels
    chunks = []
    for c in range(CHUNKS):
        part = slice(c * rows, (c + 1) * rows)
        codes = jnp.concatenate([within[part].T, groups[part].T], axis=1).astype(jnp.bfloat16)
        codes = jnp.pad(codes, ((0, 0), (0, width - 2 * rows)))
        chunks.append(jnp.concatenate([embeddings[part], codes], axis=0))

    which = lax.dynamic_index_in_dim(owners, doc_index, 1, keepdims=False) - lab_index + lab_count - 1
    lists = lax.dynamic_index_in_dim(shortlist, home, 1, keepdims=False)
    live = lax.dynamic_index_in_dim(counts, home, 1, keepdims=True)
    listed = lists[:, :, None] == jnp.arange(tiles, dtype=jnp.int32)
    used = jnp.arange(lists.shape[1], dtype=jnp.int32) < live
    on = jnp.any(listed & used[:, :, None], axis=1).astype(jnp.int32)
    group = jnp.arange(STEPS, dtype=jnp.int32)[:, None] * lab_count + lab_index
    flags = jnp.concatenate([group, on], axis=1)
    parent_rows = lax.dynamic_slice_in_dim(parents, home * labels, labels, 0)[:, None]

    panels = [[] for _ in range(STEPS)]
    for chunk in chunks:
        found = select(which, gather_line(chunk, "lab"), STEPS)
        for step in range(STEPS):
            got = found[step]
            if step > 0:
                pairs = [(i, (i - step) % doc_count) for i in range(doc_count)]
                got = lax.ppermute(got, "doc", pairs)
            panels[step].append(got)
    weight, moment = weights, None
    for step in range(STEPS):
        weight, moment = update(flags[step], panels[step], rows, parent_rows, weight, moment)
    return (weight, moment)


def solution(mesh):
    return jax.shard_map(
        local,
        mesh=mesh,
        in_specs=(
            P(("doc", "lab"), None),
            P(("doc", "lab"), None),
            P(("doc", "lab"), None),
            P(),
            P(),
            P(),
            P(),
        ),
        out_specs=(P(("doc", "lab"), None), P(("doc", "lab"), None)),
        check_vma=False,
    )
```

time: 293 us -> 211 us (0.72)
  the two profiles are of different devices: /device:TPU:3 before, /device:TPU:31 now
where the time goes in v1:
time: 211 us; the launch traced here: 210 us
  Pallas kernels  119 us (56%)
  waiting for transfers between devices  54.9 us (26%)
  starting transfers between devices  28.6 us (14%)
  local copies, waits for them, and re-layouts  4.7 us (2%)
    pallas_call x2, Pallas kernels, select(): pl.pallas_call(functools.partial(select_kernel, len(sources)), out_shape=...  105 us
    ppermute x6, waiting for transfers between devices, local(): got = lax.ppermute(got, 'doc', pairs)  27.2 us
    ppermute x6, waiting for transfers between devices, gather_line(): lax.ppermute(up[-1], axis, [(i, i + 1) for i in range(r - 1, n - 1)])  26.8 us
    pallas_call x4, Pallas kernels, update(): pl.pallas_call(functools.partial(update_kernel, first, rows, 1.0 / float(...  14.1 us
    ppermute x6, starting transfers between devices, gather_line(): lax.ppermute(down[-1], axis, [(i, i - 1) for i in range(1, n - r + 1)])  12.5 us
    ppermute x6, starting transfers between devices, local(): got = lax.ppermute(got, 'doc', pairs)  8.4 us
    ppermute x6, starting transfers between devices, gather_line(): lax.ppermute(up[-1], axis, [(i, i + 1) for i in range(r - 1, n - 1)])  7.71 us
  transfers between devices with their start and end apart: 18, of which 10 were waited for; matrix products, arithmetic and copies ran while one was open for 1% of the time, Pallas kernels for 55%

profile of v1, /device:TPU:31, one launch (start us, length us, event | category | flops | bytes accessed | tf_op | source)
XLA Modules:
  0.0 210.1 jit_solution(15279594721974989246)
XLA Ops:
  2.7 2.1 collective-permute-start.10
  4.8 1.3 collective-permute-start.7
  7.5 4.6 %collective-permute-start.3 = (bf16[272,768]{1,0:T(8,128)(2,1)S(1)}, bf16[272,768]{1,0:T(8,128)(2,1)S(1)}, u32[]{:S(2)}, u32[]{:S(2)}) collective-permute-start(bf16[272,768]{1,0:T(8,128)(2,1)S(1)} %pad_maximum_fusion.refs_3_), channel_id=1, source_target_pairs={{1,0},{2,1},{3,2},{5,4},{6,5},{7,6},{9,8},{10,9},{11,10},{13,12},{... | collective-permute-start | bytes 1253384 | tf_op jit(solution)/shard_map/ppermute | solution.py:126
  13.1 1.4 collective-permute-start.11
  14.5 2.4 %collective-permute-done.7.refs_2_ = bf16[272,768]{1,0:T(8,128)(2,1)S(1)} collective-permute-done((bf16[272,768]{1,0:T(8,128)(2,1)S(1)}, bf16[272,768]{1,0:T(8,128)(2,1)S(1)}, u32[]{:S(2)}, u32[]{:S(2)}) %collective-permute-start.7) | collective-permute-done | bytes 417824 | tf_op jit(solution)/shard_map/ppermute | solution.py:125
  18.2 7.7 %collective-permute-done.refs_2_ = bf16[272,768]{1,0:T(8,128)(2,1)S(1)} collective-permute-done((bf16[272,768]{1,0:T(8,128)(2,1)S(1)}, bf16[272,768]{1,0:T(8,128)(2,1)S(1)}, u32[]{:S(2)}, u32[]{:S(2)}) %collective-permute-start) | collective-permute-done | bytes 417824 | tf_op jit(solution)/shard_map/ppermute | solution.py:125
  27.1 1.4 collective-permute-start.4
  28.6 1.4 collective-permute-start.12
  30.0 4.8 %collective-permute-done.8.refs_1_ = bf16[272,768]{1,0:T(8,128)(2,1)S(1)} collective-permute-done((bf16[272,768]{1,0:T(8,128)(2,1)S(1)}, bf16[272,768]{1,0:T(8,128)(2,1)S(1)}, u32[]{:S(2)}, u32[]{:S(2)}) %collective-permute-start.8) | collective-permute-done | bytes 417824 | tf_op jit(solution)/shard_map/ppermute | solution.py:125
  36.1 7.7 %collective-permute-done.1.refs_1_ = bf16[272,768]{1,0:T(8,128)(2,1)S(1)} collective-permute-done((bf16[272,768]{1,0:T(8,128)(2,1)S(1)}, bf16[272,768]{1,0:T(8,128)(2,1)S(1)}, u32[]{:S(2)}, u32[]{:S(2)}) %collective-permute-start.1) | collective-permute-done | bytes 417824 | tf_op jit(solution)/shard_map/ppermute | solution.py:125
  45.0 1.4 collective-permute-start.5
  48.5 4.3 %collective-permute-done.9.refs_0_ = bf16[272,768]{1,0:T(8,128)(2,1)} collective-permute-done((bf16[272,768]{1,0:T(8,128)(2,1)S(1)}, bf16[272,768]{1,0:T(8,128)(2,1)}, u32[]{:S(2)}, u32[]{:S(2)}) %collective-permute-start.9) | collective-permute-done | bytes 417824 | tf_op jit(solution)/shard_map/ppermute | solution.py:125
  52.8 52.4 %select_panels.3 = (bf16[272,768]{1,0:T(8,128)(2,1)}, bf16[272,768]{1,0:T(8,128)(2,1)}, bf16[272,768]{1,0:T(8,128)(2,1)}, bf16[272,768]{1,0:T(8,128)(2,1)}) custom-call(s32[4]{0:T(128)} %add_reduce_fusion.which_ref, bf16[272,768]{1,0:T(8,128)(2,1)} %collective-permute-done.9.refs_0_, bf16[272,768]{1,0:T(8,128)(2,1)} %copy-done.11, ...), custom_call_target="tpu_custom_call" | custom-call | bytes 3342336 | tf_op jit(solution)/shard_map/select_panels/pallas_call | solution.py:40
  105.3 3.4 %collective-permute-start.17 = (bf16[272,768]{1,0:T(8,128)(2,1)}, bf16[272,768]{1,0:T(8,128)(2,1)S(1)}, u32[]{:S(2)}, u32[]{:S(2)}) collective-permute-start(bf16[272,768]{1,0:T(8,128)(2,1)} %get-tuple-element.21), channel_id=1, source_target_pairs={{0,28},{4,0},{8,4},{12,8},{16,12},{20,16},{24,20},{28,24},{1,29},{... | collective-permute-start | bytes 1253384 | tf_op jit(solution)/shard_map/ppermute | solution.py:166
  109.1 52.6 %select_panels.2 = (bf16[272,768]{1,0:T(8,128)(2,1)}, bf16[272,768]{1,0:T(8,128)(2,1)}, bf16[272,768]{1,0:T(8,128)(2,1)}, bf16[272,768]{1,0:T(8,128)(2,1)}) custom-call(s32[4]{0:T(128)} %add_reduce_fusion.which_ref, bf16[272,768]{1,0:T(8,128)(2,1)} %collective-permute-done.2.refs_0_, bf16[272,768]{1,0:T(8,128)(2,1)} %copy-done.10, ...), custom_call_target="tpu_custom_call" | custom-call | bytes 3342336 | tf_op jit(solution)/shard_map/select_panels/pallas_call | solution.py:40
  164.2 3.3 %collective-permute-start.13 = (bf16[272,768]{1,0:T(8,128)(2,1)S(1)}, bf16[272,768]{1,0:T(8,128)(2,1)S(1)}, u32[]{:S(2)}, u32[]{:S(2)}) collective-permute-start(bf16[272,768]{1,0:T(8,128)(2,1)S(1)} %copy-done.14), channel_id=1, source_target_pairs={{0,20},{4,24},{8,28},{12,0},{16,4},{20,8},{24,12},{28,16},{1,21},{... | collective-permute-start | bytes 1253384 | tf_op jit(solution)/shard_map/ppermute | solution.py:166
  168.7 3.2 %update_block.4 = (f32[256,768]{1,0:T(8,128)S(1)}, f32[256,768]{1,0:T(8,128)S(1)}) custom-call(s32[5]{0:T(128)S(1)} %get-tuple-element.38.flags_ref, bf16[272,768]{1,0:T(8,128)(2,1)S(1)} %copy-done.3, bf16[272,768]{1,0:T(8,128)(2,1)S(1)} %copy-done.2, s32[256,1]{1,0:T(8,128)S(1)} %copy.20.refs_2_, f32[256,768]{1,0:T(8,128)S(1)} %copy-done.1), custom_call_target="tpu_custom_call" | custom-call | flops 805306368 | bytes 3932160 | tf_op jit(solution)/shard_map/update_block/pallas_call | solution.py:108
  172.0 2.8 %collective-permute-done.16.refs_0_ = bf16[272,768]{1,0:T(8,128)(2,1)S(1)} collective-permute-done((bf16[272,768]{1,0:T(8,128)(2,1)}, bf16[272,768]{1,0:T(8,128)(2,1)S(1)}, u32[]{:S(2)}, u32[]{:S(2)}) %collective-permute-start.16) | collective-permute-done | bytes 417824 | tf_op jit(solution)/shard_map/ppermute | solution.py:166
  174.8 3.2 %update_block.5 = (f32[256,768]{1,0:T(8,128)S(1)}, f32[256,768]{1,0:T(8,128)S(1)}) custom-call(s32[5]{0:T(128)S(1)} %get-tuple-element.39.flags_ref, bf16[272,768]{1,0:T(8,128)(2,1)S(1)} %collective-permute-done.16.refs_0_, bf16[272,768]{1,0:T(8,128)(2,1)S(1)} %collective-permute-done.17.refs_1_, s32[256,1]{1,0:T(8,128)S(1)} %copy.20.refs_2_, ...), custom_call_target="tpu_custom_call" | custom-call | flops 805306368 | bytes 3932160 | tf_op jit(solution)/shard_map/update_block/pallas_call | solution.py:108
  178.1 5.1 %collective-permute-done.14.refs_0_ = bf16[272,768]{1,0:T(8,128)(2,1)S(1)} collective-permute-done((bf16[272,768]{1,0:T(8,128)(2,1)}, bf16[272,768]{1,0:T(8,128)(2,1)S(1)}, u32[]{:S(2)}, u32[]{:S(2)}) %collective-permute-start.14) | collective-permute-done | bytes 417824 | tf_op jit(solution)/shard_map/ppermute | solution.py:166
  183.2 3.2 %update_block.6 = (f32[256,768]{1,0:T(8,128)S(1)}, f32[256,768]{1,0:T(8,128)S(1)}) custom-call(s32[5]{0:T(128)S(1)} %get-tuple-element.40.flags_ref, bf16[272,768]{1,0:T(8,128)(2,1)S(1)} %collective-permute-done.14.refs_0_, bf16[272,768]{1,0:T(8,128)(2,1)S(1)} %collective-permute-done.15.refs_1_, s32[256,1]{1,0:T(8,128)S(1)} %copy.20.refs_2_, ...), custom_call_target="tpu_custom_call" | custom-call | flops 805306368 | bytes 3932160 | tf_op jit(solution)/shard_map/update_block/pallas_call | solution.py:108
  186.4 14.7 %collective-permute-done.13.refs_1_ = bf16[272,768]{1,0:T(8,128)(2,1)S(1)} collective-permute-done((bf16[272,768]{1,0:T(8,128)(2,1)S(1)}, bf16[272,768]{1,0:T(8,128)(2,1)S(1)}, u32[]{:S(2)}, u32[]{:S(2)}) %collective-permute-start.13) | collective-permute-done | bytes 417824 | tf_op jit(solution)/shard_map/ppermute | solution.py:166
  201.2 4.5 %collective-permute-done.6.refs_0_ = bf16[272,768]{1,0:T(8,128)(2,1)S(1)} collective-permute-done((bf16[272,768]{1,0:T(8,128)(2,1)}, bf16[272,768]{1,0:T(8,128)(2,1)S(1)}, u32[]{:S(2)}, u32[]{:S(2)}) %collective-permute-start.6) | collective-permute-done | bytes 417824 | tf_op jit(solution)/shard_map/ppermute | solution.py:166
  205.6 4.4 %update_block.7 = (f32[256,768]{1,0:T(8,128)}, f32[256,768]{1,0:T(8,128)}) custom-call(s32[5]{0:T(128)S(1)} %get-tuple-element.41.flags_ref, bf16[272,768]{1,0:T(8,128)(2,1)S(1)} %collective-permute-done.6.refs_0_, bf16[272,768]{1,0:T(8,128)(2,1)S(1)} %collective-permute-done.13.refs_1_, s32[256,1]{1,0:T(8,128)S(1)} %copy.20.refs_2_, ...), custom_call_target="tpu_custom_call" | custom-call | flops 805306368 | bytes 3932160 | tf_op jit(solution)/shard_map/update_block/pallas_call | solution.py:108
  (66 shorter events, 15.6 us)
Async XLA Ops:
  0.6 108.1 %copy-start = (s32[4,32,4]{1,2,0:T(4,128)S(1)}, s32[4,32,4]{1,2,0:T(4,128)}, u32[]{:S(2)}) copy-start(s32[4,32,4]{1,2,0:T(4,128)} %param.12) | copy-start | bytes 6148
  2.7 10.4 %collective-permute-start.10 = (bf16[272,768]{1,0:T(8,128)(2,1)S(1)}, bf16[272,768]{1,0:T(8,128)(2,1)S(1)}, u32[]{:S(2)}, u32[]{:S(2)}) collective-permute-start(bf16[272,768]{1,0:T(8,128)(2,1)S(1)} %pad_maximum_fusion.1.refs_3_), channel_id=1, source_target_pairs={{1,0},{2,1},{3,2},{5,4},{6,5},{7,6},{9,8},{10,9},{11,10},{13,12},{... | collective-permute-start | bytes 1253384 | tf_op jit(solution)/shard_map/ppermute | solution.py:126
  4.8 12.1 %collective-permute-start.7 = (bf16[272,768]{1,0:T(8,128)(2,1)S(1)}, bf16[272,768]{1,0:T(8,128)(2,1)S(1)}, u32[]{:S(2)}, u32[]{:S(2)}) collective-permute-start(bf16[272,768]{1,0:T(8,128)(2,1)S(1)} %pad_maximum_fusion.1.refs_3_), channel_id=1, source_target_pairs={{0,1},{1,2},{2,3},{4,5},{5,6},{6,7},{8,9},{9,10},{10,11},{12,13},{... | collective-permute-start | bytes 1253384 | tf_op jit(solution)/shard_map/ppermute | solution.py:125
  6.2 99.1 %copy-start.4 = (bf16[272,768]{1,0:T(8,128)(2,1)}, bf16[272,768]{1,0:T(8,128)(2,1)S(1)}, u32[]{:S(2)}) copy-start(bf16[272,768]{1,0:T(8,128)(2,1)S(1)} %pad_maximum_fusion.refs_3_) | copy-start | bytes 1253380
  6.2 19.7 %collective-permute-start = (bf16[272,768]{1,0:T(8,128)(2,1)S(1)}, bf16[272,768]{1,0:T(8,128)(2,1)S(1)}, u32[]{:S(2)}, u32[]{:S(2)}) collective-permute-start(bf16[272,768]{1,0:T(8,128)(2,1)S(1)} %pad_maximum_fusion.refs_3_), channel_id=1, source_target_pairs={{0,1},{1,2},{2,3},{4,5},{5,6},{6,7},{8,9},{9,10},{10,11},{12,13},{... | collective-permute-start | bytes 1253384 | tf_op jit(solution)/shard_map/ppermute | solution.py:125
  7.5 19.7 %collective-permute-start.3 = (bf16[272,768]{1,0:T(8,128)(2,1)S(1)}, bf16[272,768]{1,0:T(8,128)(2,1)S(1)}, u32[]{:S(2)}, u32[]{:S(2)}) collective-permute-start(bf16[272,768]{1,0:T(8,128)(2,1)S(1)} %pad_maximum_fusion.refs_3_), channel_id=1, source_target_pairs={{1,0},{2,1},{3,2},{5,4},{6,5},{7,6},{9,8},{10,9},{11,10},{13,12},{... | collective-permute-start | bytes 1253384 | tf_op jit(solution)/shard_map/ppermute | solution.py:126
  13.1 15.5 %collective-permute-start.11 = (bf16[272,768]{1,0:T(8,128)(2,1)S(1)}, bf16[272,768]{1,0:T(8,128)(2,1)}, u32[]{:S(2)}, u32[]{:S(2)}) collective-permute-start(bf16[272,768]{1,0:T(8,128)(2,1)S(1)} %collective-permute-done.10.refs_4_), channel_id=1, source_target_pairs={{1,0},{2,1},{5,4},{6,5},{9,8},{10,9},{13,12},{14,13},{17,16},{18,1... | collective-permute-start | bytes 1253384 | tf_op jit(solution)/shard_map/ppermute | solution.py:126
  16.9 17.9 %collective-permute-start.8 = (bf16[272,768]{1,0:T(8,128)(2,1)S(1)}, bf16[272,768]{1,0:T(8,128)(2,1)S(1)}, u32[]{:S(2)}, u32[]{:S(2)}) collective-permute-start(bf16[272,768]{1,0:T(8,128)(2,1)S(1)} %collective-permute-done.7.refs_2_), channel_id=1, source_target_pairs={{1,2},{2,3},{5,6},{6,7},{9,10},{10,11},{13,14},{14,15},{17,18},{18... | collective-permute-start | bytes 1253384 | tf_op jit(solution)/shard_map/ppermute | solution.py:125
  25.8 79.4 %copy-start.6 = (bf16[272,768]{1,0:T(8,128)(2,1)}, bf16[272,768]{1,0:T(8,128)(2,1)S(1)}, u32[]{:S(2)}) copy-start(bf16[272,768]{1,0:T(8,128)(2,1)S(1)} %collective-permute-done.refs_2_) | copy-start | bytes 1253380
  25.8 17.9 %collective-permute-start.1 = (bf16[272,768]{1,0:T(8,128)(2,1)S(1)}, bf16[272,768]{1,0:T(8,128)(2,1)S(1)}, u32[]{:S(2)}, u32[]{:S(2)}) collective-permute-start(bf16[272,768]{1,0:T(8,128)(2,1)S(1)} %collective-permute-done.refs_2_), channel_id=1, source_target_pairs={{1,2},{2,3},{5,6},{6,7},{9,10},{10,11},{13,14},{14,15},{17,18},{18... | collective-permute-start | bytes 1253384 | tf_op jit(solution)/shard_map/ppermute | solution.py:125
  27.1 78.1 %copy-start.7 = (bf16[272,768]{1,0:T(8,128)(2,1)}, bf16[272,768]{1,0:T(8,128)(2,1)S(1)}, u32[]{:S(2)}) copy-start(bf16[272,768]{1,0:T(8,128)(2,1)S(1)} %collective-permute-done.3.refs_4_) | copy-start | bytes 1253380
  27.1 17.9 %collective-permute-start.4 = (bf16[272,768]{1,0:T(8,128)(2,1)S(1)}, bf16[272,768]{1,0:T(8,128)(2,1)}, u32[]{:S(2)}, u32[]{:S(2)}) collective-permute-start(bf16[272,768]{1,0:T(8,128)(2,1)S(1)} %collective-permute-done.3.refs_4_), channel_id=1, source_target_pairs={{1,0},{2,1},{5,4},{6,5},{9,8},{10,9},{13,12},{14,13},{17,16},{18,1... | collective-permute-start | bytes 1253384 | tf_op jit(solution)/shard_map/ppermute | solution.py:126
  28.6 19.9 %collective-permute-start.12 = (bf16[272,768]{1,0:T(8,128)(2,1)}, bf16[272,768]{1,0:T(8,128)(2,1)}, u32[]{:S(2)}, u32[]{:S(2)}) collective-permute-start(bf16[272,768]{1,0:T(8,128)(2,1)} %collective-permute-done.11.refs_5_), channel_id=1, source_target_pairs={{1,0},{5,4},{9,8},{13,12},{17,16},{21,20},{25,24},{29,28}} | collective-permute-start | bytes 1253384 | tf_op jit(solution)/shard_map/ppermute | solution.py:126
  34.8 18.0 %collective-permute-start.9 = (bf16[272,768]{1,0:T(8,128)(2,1)S(1)}, bf16[272,768]{1,0:T(8,128)(2,1)}, u32[]{:S(2)}, u32[]{:S(2)}) collective-permute-start(bf16[272,768]{1,0:T(8,128)(2,1)S(1)} %collective-permute-done.8.refs_1_), channel_id=1, source_target_pairs={{2,3},{6,7},{10,11},{14,15},{18,19},{22,23},{26,27},{30,31}} | collective-permute-start | bytes 1253384 | tf_op jit(solution)/shard_map/ppermute | solution.py:125
  43.7 61.5 %copy-start.10 = (bf16[272,768]{1,0:T(8,128)(2,1)}, bf16[272,768]{1,0:T(8,128)(2,1)S(1)}, u32[]{:S(2)}) copy-start(bf16[272,768]{1,0:T(8,128)(2,1)S(1)} %collective-permute-done.1.refs_1_) | copy-start | bytes 1253380
  43.7 65.3 %collective-permute-start.2 = (bf16[272,768]{1,0:T(8,128)(2,1)S(1)}, bf16[272,768]{1,0:T(8,128)(2,1)}, u32[]{:S(2)}, u32[]{:S(2)}) collective-permute-start(bf16[272,768]{1,0:T(8,128)(2,1)S(1)} %collective-permute-done.1.refs_1_), channel_id=1, source_target_pairs={{2,3},{6,7},{10,11},{14,15},{18,19},{22,23},{26,27},{30,31}} | collective-permute-start | bytes 1253384 | tf_op jit(solution)/shard_map/ppermute | solution.py:125
  45.0 64.1 %collective-permute-start.5 = (bf16[272,768]{1,0:T(8,128)(2,1)}, bf16[272,768]{1,0:T(8,128)(2,1)}, u32[]{:S(2)}, u32[]{:S(2)}) collective-permute-start(bf16[272,768]{1,0:T(8,128)(2,1)} %collective-permute-done.4.refs_5_), channel_id=1, source_target_pairs={{1,0},{5,4},{9,8},{13,12},{17,16},{21,20},{25,24},{29,28}} | collective-permute-start | bytes 1253384 | tf_op jit(solution)/shard_map/ppermute | solution.py:126
  105.3 62.2 %collective-permute-start.17 = (bf16[272,768]{1,0:T(8,128)(2,1)}, bf16[272,768]{1,0:T(8,128)(2,1)S(1)}, u32[]{:S(2)}, u32[]{:S(2)}) collective-permute-start(bf16[272,768]{1,0:T(8,128)(2,1)} %get-tuple-element.21), channel_id=1, source_target_pairs={{0,28},{4,0},{8,4},{12,8},{16,12},{20,16},{24,20},{28,24},{1,29},{... | collective-permute-start | bytes 1253384 | tf_op jit(solution)/shard_map/ppermute | solution.py:166
  109.1 58.7 %copy-start.1 = (f32[256,768]{1,0:T(8,128)S(1)}, f32[256,768]{1,0:T(8,128)}, u32[]{:S(2)}) copy-start(f32[256,768]{1,0:T(8,128)} %refs_3_.1) | copy-start | bytes 2359300
  161.7 13.1 %collective-permute-start.16 = (bf16[272,768]{1,0:T(8,128)(2,1)}, bf16[272,768]{1,0:T(8,128)(2,1)S(1)}, u32[]{:S(2)}, u32[]{:S(2)}) collective-permute-start(bf16[272,768]{1,0:T(8,128)(2,1)} %get-tuple-element.20), channel_id=1, source_target_pairs={{0,28},{4,0},{8,4},{12,8},{16,12},{20,16},{24,20},{28,24},{1,29},{... | collective-permute-start | bytes 1253384 | tf_op jit(solution)/shard_map/ppermute | solution.py:166
  161.8 16.3 %collective-permute-start.15 = (bf16[272,768]{1,0:T(8,128)(2,1)}, bf16[272,768]{1,0:T(8,128)(2,1)S(1)}, u32[]{:S(2)}, u32[]{:S(2)}) collective-permute-start(bf16[272,768]{1,0:T(8,128)(2,1)} %get-tuple-element.19), channel_id=1, source_target_pairs={{0,24},{4,28},{8,0},{12,4},{16,8},{20,12},{24,16},{28,20},{1,25},{... | collective-permute-start | bytes 1253384 | tf_op jit(solution)/shard_map/ppermute | solution.py:166
  162.1 21.1 %collective-permute-start.14 = (bf16[272,768]{1,0:T(8,128)(2,1)}, bf16[272,768]{1,0:T(8,128)(2,1)S(1)}, u32[]{:S(2)}, u32[]{:S(2)}) collective-permute-start(bf16[272,768]{1,0:T(8,128)(2,1)} %get-tuple-element.18), channel_id=1, source_target_pairs={{0,24},{4,28},{8,0},{12,4},{16,8},{20,12},{24,16},{28,20},{1,25},{... | collective-permute-start | bytes 1253384 | tf_op jit(solution)/shard_map/ppermute | solution.py:166
  164.2 37.0 %collective-permute-start.13 = (bf16[272,768]{1,0:T(8,128)(2,1)S(1)}, bf16[272,768]{1,0:T(8,128)(2,1)S(1)}, u32[]{:S(2)}, u32[]{:S(2)}) collective-permute-start(bf16[272,768]{1,0:T(8,128)(2,1)S(1)} %copy-done.14), channel_id=1, source_target_pairs={{0,20},{4,24},{8,28},{12,0},{16,4},{20,8},{24,12},{28,16},{1,21},{... | collective-permute-start | bytes 1253384 | tf_op jit(solution)/shard_map/ppermute | solution.py:166
  167.5 38.2 %collective-permute-start.6 = (bf16[272,768]{1,0:T(8,128)(2,1)}, bf16[272,768]{1,0:T(8,128)(2,1)S(1)}, u32[]{:S(2)}, u32[]{:S(2)}) collective-permute-start(bf16[272,768]{1,0:T(8,128)(2,1)} %get-tuple-element.16), channel_id=1, source_target_pairs={{0,20},{4,24},{8,28},{12,0},{16,4},{20,8},{24,12},{28,16},{1,21},{... | collective-permute-start | bytes 1253384 | tf_op jit(solution)/shard_map/ppermute | solution.py:166
  (9 other events, 213.3 us)

commit v2 on v1

v2 whole, which is shorter than its diff:
```python
import functools

import jax
import jax.numpy as jnp
from jax import lax
from jax.experimental import pallas as pl
from jax.experimental.pallas import tpu as pltpu
from jax.sharding import PartitionSpec as P

TILE = 128
STEPS = 4
POS = 16
LOWER = 6
GROUP = 2

learning_rate = 0.1
beta_rate = 0.9
pull_rate = 1.0

VMEM = pl.BlockSpec(memory_space=pltpu.VMEM)
SMEM = pl.BlockSpec(memory_space=pltpu.SMEM)
ANY = pl.BlockSpec(memory_space=pl.ANY)
MIB = 1024 * 1024


def select_kernel(n, which_ref, *refs):
    sources, outs = refs[:n], refs[n:]
    for k, out in enumerate(outs):
        for i, source in enumerate(sources):

            @pl.when(which_ref[k] == i)
            def _(source=source, out=out):
                out[...] = source[...]


def select(which, sources):
    size = sources[0].size * sources[0].dtype.itemsize
    return pl.pallas_call(
        functools.partial(select_kernel, len(sources)),
        out_shape=[pltpu.VMEM(sources[0].shape, sources[0].dtype)] * which.shape[0],
        in_specs=[SMEM] + [VMEM] * len(sources),
        out_specs=[VMEM] * which.shape[0],
        compiler_params=pltpu.CompilerParams(vmem_limit_bytes=12 * MIB),
        cost_estimate=pl.CostEstimate(
            flops=0, bytes_accessed=2 * which.shape[0] * size, transcendentals=0
        ),
        name="select_panels",
    )(which, *sources)


def pack_kernel(start, size, lab_ref, source, *refs):
    outs, sem = refs[:-1], refs[-1]
    n = len(outs)
    copies = []
    for k, out in enumerate(outs):
        piece = lax.rem(lab_ref[0] + k, n)
        row = pl.multiple_of(start + piece * size, 16)
        copies.append(pltpu.make_async_copy(source.at[pl.ds(row, size)], out, sem.at[k]))
    for copy in copies:
        copy.start()
    for copy in copies:
        copy.wait()


def pack(source, start, n, lab):
    size = (source.shape[0] - start) // n
    shape = (size, source.shape[1])
    return pl.pallas_call(
        functools.partial(pack_kernel, start, size),
        out_shape=[pltpu.VMEM(shape, source.dtype)] * n,
        in_specs=[SMEM, ANY],
        out_specs=[VMEM] * n,
        scratch_shapes=[pltpu.SemaphoreType.DMA((n,))],
        compiler_params=pltpu.CompilerParams(vmem_limit_bytes=8 * MIB),
        name="pack_pieces",
    )(lab, source)


def split(value):
    high = value.astype(jnp.bfloat16)
    return high, (value - high.astype(jnp.float32)).astype(jnp.bfloat16)


def product(pair, other, dims):
    dot = functools.partial(
        lax.dot_general, dimension_numbers=(dims, ((), ())), preferred_element_type=jnp.float32
    )
    return dot(pair[1], other) + dot(pair[0], other)


def update_kernel(first, top, size, offset, scale, group_ref, places_ref, panel_ref, *refs):
    n = places_ref.shape[0]
    pieces, refs = refs[:n], refs[n:]
    if first:
        live_ref, parents_ref, weight_ref, weight_out, moment_out, rows_ref = refs
    else:
        live_ref, parents_ref, weight_ref, moment_ref, weight_out, moment_out, rows_ref = refs
    labels, width = weight_ref.shape
    count = rows_ref.shape[0]
    rows_ref[:top, :] = panel_ref[:top, :]
    for k, piece in enumerate(pieces):
        row = pl.multiple_of(top + places_ref[k] * size, 16)
        rows_ref[pl.ds(row, size), :] = piece[offset : offset + size, :]
    rows = rows_ref[...]
    weight = weight_ref[...]
    pair = split(weight)
    group = group_ref[0].astype(jnp.bfloat16)
    within = panel_ref[top : top + POS, :count]
    own = jnp.where(panel_ref[top + POS :, :count] == group, within, jnp.bfloat16(-1.0))
    label = lax.broadcasted_iota(jnp.int32, (labels, count), 0)
    label = label.astype(jnp.float32).astype(jnp.bfloat16)
    target = jnp.zeros(label.shape, jnp.bfloat16)
    for k in range(POS):
        target = jnp.where(label == own[k : k + 1, :], jnp.bfloat16(1.0), target)
    scores = product(pair, rows, ((1,), (1,))) * scale
    resid = (jax.nn.sigmoid(scores) - target.astype(jnp.float32)) * live_ref[...]
    grad = product(split(resid), rows, ((1,), (0,)))
    column = lax.broadcasted_iota(jnp.int32, (labels, labels), 1)
    pick = (column == parents_ref[...]).astype(jnp.bfloat16)
    dot = functools.partial(jnp.dot, preferred_element_type=jnp.float32)
    parent = dot(pick, pair[1]) + dot(pick, pair[0])
    grad = grad * scale + pull_rate * (weight - parent)
    moment = grad if first else beta_rate * moment_ref[...] + grad
    moment_out[...] = moment
    weight_out[...] = weight - learning_rate * moment


def update(group, places, panel, pieces, offset, live, parents, weight, moment, last):
    labels, width = weight.shape
    count = live.shape[1]
    top = panel.shape[0] - 2 * POS
    size = (count - top) // len(pieces)
    first = moment is None
    state = [weight] if first else [weight, moment]
    shape = (jax.ShapeDtypeStruct if last else pltpu.VMEM)(weight.shape, jnp.float32)
    scale = 1.0 / float(width) ** 0.5
    return pl.pallas_call(
        functools.partial(update_kernel, first, top, size, offset, scale),
        out_shape=[shape, shape],
        in_specs=[SMEM, SMEM] + [VMEM] * (len(pieces) + 3 + len(state)),
        out_specs=[VMEM, VMEM],
        scratch_shapes=[pltpu.VMEM((count, width), panel.dtype)],
        compiler_params=pltpu.CompilerParams(vmem_limit_bytes=12 * MIB),
        cost_estimate=pl.CostEstimate(
            flops=8 * labels * width * count,
            bytes_accessed=2 * count * width + 16 * labels * width,
            transcendentals=labels * count,
        ),
        name="update_block",
    )(group, places, panel, *pieces, live, parents, *state)


def after(value, *earlier):
    return lax.optimization_barrier((value, *earlier))[0]


def circle(n):
    return [*range(0, 1), *range(1, n, 2), *reversed(range(2, n, 2))]


def send(what, value, axis, pairs, *earlier):
    value = after(value, *earlier) if earlier else value
    with jax.named_scope(what):
        return lax.ppermute(value, axis, pairs)


def local(embeddings, positives, weights, parents, owners, shortlist, counts):
    doc_index = lax.axis_index("doc")
    lab_index = lax.axis_index("lab")
    doc_count = lax.axis_size("doc")
    lab_count = lax.axis_size("lab")
    labels, width = weights.shape
    rows = embeddings.shape[0]
    home = doc_index * lab_count + lab_index
    unit = 16 * lab_count
    size = max(1, rows * LOWER // unit // 8) * 16
    top = rows - size * lab_count

    mine = pack(embeddings, top, lab_count, lab_index[None])

    groups = positives // labels
    codes = jnp.concatenate([positives - groups * labels, groups], axis=1).T
    codes = jnp.pad(codes, ((0, 0), (0, width - rows))).astype(jnp.bfloat16)
    upper = jnp.concatenate([embeddings[:top], codes], axis=0)

    order = circle(lab_count)
    order_of = jnp.array(order, jnp.int32)
    place_of = jnp.array([order.index(i) for i in range(lab_count)], jnp.int32)
    owner = lax.dynamic_index_in_dim(owners, doc_index, 1, keepdims=False)
    which_upper = (place_of[lab_index] - place_of[owner]) % lab_count
    which_lower = (lab_index - owner) % lab_count
    places = order_of[(place_of[lab_index] - jnp.arange(lab_count, dtype=jnp.int32)) % lab_count]
    lists = lax.dynamic_index_in_dim(shortlist, home, 1, keepdims=False)
    used = lax.dynamic_index_in_dim(counts, home, 1, keepdims=True)
    listed = lists[:, :, None] == jnp.arange(rows, dtype=jnp.int32) // TILE
    listed = listed & (jnp.arange(lists.shape[1], dtype=jnp.int32) < used)[:, :, None]
    live = jnp.any(listed, axis=1).astype(jnp.float32)
    group = jnp.arange(STEPS, dtype=jnp.int32)[:, None] * lab_count + lab_index
    parent_rows = lax.dynamic_slice_in_dim(parents, home * labels, labels, 0)[:, None]
    prepared = (which_upper, places, live, group, parent_rows)

    around = [(order[i], order[(i + 1) % lab_count]) for i in range(lab_count)]

    def shift(what, step, value, *earlier):
        pairs = [(i, (i - step) % doc_count) for i in range(doc_count)]
        return send(f"{what}_doc_shift_{step}", value, "doc", pairs, *earlier)

    met = [mine[0]]
    for k in range(1, lab_count):
        pairs = [(i, (i + k) % lab_count) for i in range(lab_count)]
        met.append(send(f"lower_lab_shift_{k}", mine[k], "lab", pairs))
    held = [upper]

    def hop(*earlier):
        held.append(send(f"upper_lab_hop_{len(held)}", held[-1], "lab", around, *earlier))

    hop(mine[0])
    lower = select(which_lower, met)
    hop(*prepared, lower[0])
    lower = [lower[0]] + [shift("lower", s, lower[s]) for s in range(1, STEPS)]
    for r in range(3, lab_count):
        hop(lower[1])
    parts = []
    for g in range(0, STEPS, GROUP):
        parts.append([jnp.concatenate(lower[g : g + GROUP], axis=0)])

    def spread(g, *earlier):
        part = parts[g]
        part.append(send(f"part_{g}_lab_hop_{len(part)}", part[-1], "lab", around, *earlier))

    spread(0)
    found = select(which_upper, [after(held[0], parts[0][1], *lower), *held[1:]])
    found = [found[0]] + [shift("upper", s, found[s]) for s in range(1, STEPS)]
    spread(1, found[0])
    for r in range(2, lab_count):
        spread(0, found[min(2 * r - 3, STEPS - 1)])
        spread(1, found[min(2 * r - 2, STEPS - 1)])

    weight, moment = weights, None
    for s in range(STEPS):
        weight, moment = update(
            group[s],
            places,
            found[s],
            parts[s // GROUP],
            s % GROUP * size,
            live[s : s + 1],
            parent_rows,
            weight,
            moment,
            s == STEPS - 1,
        )
    return (weight, moment)


def solution(mesh):
    return jax.shard_map(
        local,
        mesh=mesh,
        in_specs=(
            P(("doc", "lab"), None),
            P(("doc", "lab"), None),
            P(("doc", "lab"), None),
            P(),
            P(),
            P(),
            P(),
        ),
        out_specs=(P(("doc", "lab"), None), P(("doc", "lab"), None)),
        check_vma=False,
    )
```

time: 211 us -> 92 us (0.44)
  the two profiles are of different devices: /device:TPU:31 before, /device:TPU:0 now
where the time goes in v2:
time: 92 us; the launch traced here: 91 us
  waiting for transfers between devices  43.5 us (47%)
  starting transfers between devices  21.9 us (24%)
  Pallas kernels  14.8 us (16%)
  local copies, waits for them, and re-layouts  8.1 us (9%)
  other arithmetic  1.88 us (2%)
    ppermute x18, waiting for transfers between devices, send(): return lax.ppermute(value, axis, pairs)  43.5 us
    ppermute x18, starting transfers between devices, send(): return lax.ppermute(value, axis, pairs)  21.9 us
    pallas_call x4, Pallas kernels, update(): pl.pallas_call(functools.partial(update_kernel, first, top, size, offset,...  12.6 us
    unnamed x16, local copies, waits for them, and re-layouts  4.31 us
  transfers between devices with their start and end apart: 18, of which 10 were waited for; matrix products, arithmetic and copies ran while one was open for 6% of the time, Pallas kernels for 7%

profile of v2, /device:TPU:0, one launch (start us, length us, event | category | flops | bytes accessed | tf_op | source)
XLA Modules:
  0.0 91.0 jit_solution(3698575054165667451)
XLA Ops:
  2.6 3.1 %collective-permute-start = (bf16[96,768]{1,0:T(8,128)(2,1)S(1)}, bf16[96,768]{1,0:T(8,128)(2,1)S(1)}, u32[]{:S(2)}, u32[]{:S(2)}) collective-permute-start(bf16[96,768]{1,0:T(8,128)(2,1)S(1)} %get-tuple-element.30), channel_id=1, source_target_pairs={{0,1},{1,2},{2,3},{3,0},{4,5},{5,6},{6,7},{7,4},{8,9},{9,10},{10,1... | collective-permute-start | bytes 442376 | tf_op jit(solution)/shard_map/lower_lab_shift_1/ppermute | solution.py:164
  5.6 2.6 %collective-permute-start.1 = (bf16[96,768]{1,0:T(8,128)(2,1)S(1)}, bf16[96,768]{1,0:T(8,128)(2,1)S(1)}, u32[]{:S(2)}, u32[]{:S(2)}) collective-permute-start(bf16[96,768]{1,0:T(8,128)(2,1)S(1)} %get-tuple-element.31), channel_id=1, source_target_pairs={{0,2},{1,3},{2,0},{3,1},{4,6},{5,7},{6,4},{7,5},{8,10},{9,11},{10,... | collective-permute-start | bytes 442376 | tf_op jit(solution)/shard_map/lower_lab_shift_2/ppermute | solution.py:164
  8.2 1.3 %collective-permute-start.2 = (bf16[96,768]{1,0:T(8,128)(2,1)S(1)}, bf16[96,768]{1,0:T(8,128)(2,1)S(1)}, u32[]{:S(2)}, u32[]{:S(2)}) collective-permute-start(bf16[96,768]{1,0:T(8,128)(2,1)S(1)} %get-tuple-element.32), channel_id=1, source_target_pairs={{0,3},{1,0},{2,1},{3,2},{4,7},{5,4},{6,5},{7,6},{8,11},{9,8},{10,9... | collective-permute-start | bytes 442376 | tf_op jit(solution)/shard_map/lower_lab_shift_3/ppermute | solution.py:164
  15.9 2.0 %collective-permute-done.1.refs_2_ = bf16[96,768]{1,0:T(8,128)(2,1)S(1)} collective-permute-done((bf16[96,768]{1,0:T(8,128)(2,1)S(1)}, bf16[96,768]{1,0:T(8,128)(2,1)S(1)}, u32[]{:S(2)}, u32[]{:S(2)}) %collective-permute-start.1) | collective-permute-done | bytes 147488 | tf_op jit(solution)/shard_map/lower_lab_shift_2/ppermute | solution.py:164
  18.6 2.0 %collective-permute-start.3 = (bf16[96,768]{1,0:T(8,128)(2,1)S(1)}, bf16[96,768]{1,0:T(8,128)(2,1)S(1)}, u32[]{:S(2)}, u32[]{:S(2)}) collective-permute-start(bf16[96,768]{1,0:T(8,128)(2,1)S(1)} %get-tuple-element.34), channel_id=1, source_target_pairs={{0,28},{4,0},{8,4},{12,8},{16,12},{20,16},{24,20},{28,24},{1,29},{... | collective-permute-start | bytes 442376 | tf_op jit(solution)/shard_map/lower_doc_shift_1/ppermute | solution.py:164
  22.6 3.7 %collective-permute-done.7.refs_1_ = bf16[160,768]{1,0:T(8,128)(2,1)S(1)} collective-permute-done((bf16[160,768]{1,0:T(8,128)(2,1)S(1)}, bf16[160,768]{1,0:T(8,128)(2,1)S(1)}, u32[]{:S(2)}, u32[]{:S(2)}) %collective-permute-start.7) | collective-permute-done | bytes 245792 | tf_op jit(solution)/shard_map/upper_lab_hop_1/ppermute | solution.py:164
  26.4 2.7 %collective-permute-start.4 = (bf16[192,768]{1,0:T(8,128)(2,1)S(1)}, bf16[192,768]{1,0:T(8,128)(2,1)S(1)}, u32[]{:S(2)}, u32[]{:S(2)}) collective-permute-start(bf16[192,768]{1,0:T(8,128)(2,1)S(1)} %constant_dynamic-update-slice_fusion.refs_0_), channel_id=1, source_target_pairs={{0,1},{1,3},{3,2},{2,0},{4,5},{5,7},{7,6},{6,4},{8,9},{9,11},{11,1... | collective-permute-start | bytes 884744 | tf_op jit(solution)/shard_map/part_0_lab_hop_1/ppermute | solution.py:164
  29.1 6.9 %collective-permute-done.8.refs_2_ = bf16[160,768]{1,0:T(8,128)(2,1)S(1)} collective-permute-done((bf16[160,768]{1,0:T(8,128)(2,1)S(1)}, bf16[160,768]{1,0:T(8,128)(2,1)S(1)}, u32[]{:S(2)}, u32[]{:S(2)}) %collective-permute-start.8) | collective-permute-done | bytes 245792 | tf_op jit(solution)/shard_map/upper_lab_hop_2/ppermute | solution.py:164
  36.0 6.3 %collective-permute-done.4.refs_1_ = bf16[192,768]{1,0:T(8,128)(2,1)S(1)} collective-permute-done((bf16[192,768]{1,0:T(8,128)(2,1)S(1)}, bf16[192,768]{1,0:T(8,128)(2,1)S(1)}, u32[]{:S(2)}, u32[]{:S(2)}) %collective-permute-start.4) | collective-permute-done | bytes 294944 | tf_op jit(solution)/shard_map/part_0_lab_hop_1/ppermute | solution.py:164
  42.3 4.3 %collective-permute-done.9.refs_3_ = bf16[160,768]{1,0:T(8,128)(2,1)S(1)} collective-permute-done((bf16[160,768]{1,0:T(8,128)(2,1)S(1)}, bf16[160,768]{1,0:T(8,128)(2,1)S(1)}, u32[]{:S(2)}, u32[]{:S(2)}) %collective-permute-start.9) | collective-permute-done | bytes 245792 | tf_op jit(solution)/shard_map/upper_lab_hop_3/ppermute | solution.py:164
  47.4 1.3 %collective-permute-start.15 = (bf16[160,768]{1,0:T(8,128)(2,1)S(1)}, bf16[160,768]{1,0:T(8,128)(2,1)S(1)}, u32[]{:S(2)}, u32[]{:S(2)}) collective-permute-start(bf16[160,768]{1,0:T(8,128)(2,1)S(1)} %get-tuple-element.47), channel_id=1, source_target_pairs={{0,28},{4,0},{8,4},{12,8},{16,12},{20,16},{24,20},{28,24},{1,29},{... | collective-permute-start | bytes 737288 | tf_op jit(solution)/shard_map/upper_doc_shift_1/ppermute | solution.py:164
  48.7 1.3 %collective-permute-start.12 = (bf16[160,768]{1,0:T(8,128)(2,1)S(1)}, bf16[160,768]{1,0:T(8,128)(2,1)S(1)}, u32[]{:S(2)}, u32[]{:S(2)}) collective-permute-start(bf16[160,768]{1,0:T(8,128)(2,1)S(1)} %get-tuple-element.44), channel_id=1, source_target_pairs={{0,24},{4,28},{8,0},{12,4},{16,8},{20,12},{24,16},{28,20},{1,25},{... | collective-permute-start | bytes 737288 | tf_op jit(solution)/shard_map/upper_doc_shift_2/ppermute | solution.py:164
  50.0 4.3 %collective-permute-done.15.panel_ref = bf16[160,768]{1,0:T(8,128)(2,1)S(1)} collective-permute-done((bf16[160,768]{1,0:T(8,128)(2,1)S(1)}, bf16[160,768]{1,0:T(8,128)(2,1)S(1)}, u32[]{:S(2)}, u32[]{:S(2)}) %collective-permute-start.15) | collective-permute-done | bytes 245792 | tf_op jit(solution)/shard_map/upper_doc_shift_1/ppermute | solution.py:164
  54.3 2.1 %collective-permute-start.16 = (bf16[192,768]{1,0:T(8,128)(2,1)S(1)}, bf16[192,768]{1,0:T(8,128)(2,1)S(1)}, u32[]{:S(2)}, u32[]{:S(2)}) collective-permute-start(bf16[192,768]{1,0:T(8,128)(2,1)S(1)} %collective-permute-done.4.refs_1_), channel_id=1, source_target_pairs={{0,1},{1,3},{3,2},{2,0},{4,5},{5,7},{7,6},{6,4},{8,9},{9,11},{11,1... | collective-permute-start | bytes 884744 | tf_op jit(solution)/shard_map/part_0_lab_hop_2/ppermute | solution.py:164
  56.4 2.0 %collective-permute-done.12.panel_ref = bf16[160,768]{1,0:T(8,128)(2,1)S(1)} collective-permute-done((bf16[160,768]{1,0:T(8,128)(2,1)S(1)}, bf16[160,768]{1,0:T(8,128)(2,1)S(1)}, u32[]{:S(2)}, u32[]{:S(2)}) %collective-permute-start.12) | collective-permute-done | bytes 245792 | tf_op jit(solution)/shard_map/upper_doc_shift_2/ppermute | solution.py:164
  58.4 2.1 %collective-permute-start.13 = (bf16[192,768]{1,0:T(8,128)(2,1)S(1)}, bf16[192,768]{1,0:T(8,128)(2,1)S(1)}, u32[]{:S(2)}, u32[]{:S(2)}) collective-permute-start(bf16[192,768]{1,0:T(8,128)(2,1)S(1)} %collective-permute-done.11.refs_1_), channel_id=1, source_target_pairs={{0,1},{1,3},{3,2},{2,0},{4,5},{5,7},{7,6},{6,4},{8,9},{9,11},{11,1... | collective-permute-start | bytes 884744 | tf_op jit(solution)/shard_map/part_1_lab_hop_2/ppermute | solution.py:164
  60.5 5.6 %collective-permute-done.10.panel_ref = bf16[160,768]{1,0:T(8,128)(2,1)S(1)} collective-permute-done((bf16[160,768]{1,0:T(8,128)(2,1)S(1)}, bf16[160,768]{1,0:T(8,128)(2,1)S(1)}, u32[]{:S(2)}, u32[]{:S(2)}) %collective-permute-start.10) | collective-permute-done | bytes 245792 | tf_op jit(solution)/shard_map/upper_doc_shift_3/ppermute | solution.py:164
  66.4 4.5 %collective-permute-done.13.refs_2_ = bf16[192,768]{1,0:T(8,128)(2,1)S(1)} collective-permute-done((bf16[192,768]{1,0:T(8,128)(2,1)S(1)}, bf16[192,768]{1,0:T(8,128)(2,1)S(1)}, u32[]{:S(2)}, u32[]{:S(2)}) %collective-permute-start.13) | collective-permute-done | bytes 294944 | tf_op jit(solution)/shard_map/part_1_lab_hop_2/ppermute | solution.py:164
  70.9 1.6 %collective-permute-start.14 = (bf16[192,768]{1,0:T(8,128)(2,1)S(1)}, bf16[192,768]{1,0:T(8,128)(2,1)S(1)}, u32[]{:S(2)}, u32[]{:S(2)}) collective-permute-start(bf16[192,768]{1,0:T(8,128)(2,1)S(1)} %collective-permute-done.13.refs_2_), channel_id=1, source_target_pairs={{0,1},{1,3},{3,2},{2,0},{4,5},{5,7},{7,6},{6,4},{8,9},{9,11},{11,1... | collective-permute-start | bytes 884744 | tf_op jit(solution)/shard_map/part_1_lab_hop_3/ppermute | solution.py:164
  73.3 3.9 %collective-permute-done.17.refs_3_ = bf16[192,768]{1,0:T(8,128)(2,1)S(1)} collective-permute-done((bf16[192,768]{1,0:T(8,128)(2,1)S(1)}, bf16[192,768]{1,0:T(8,128)(2,1)S(1)}, u32[]{:S(2)}, u32[]{:S(2)}) %collective-permute-start.17) | collective-permute-done | bytes 294944 | tf_op jit(solution)/shard_map/part_0_lab_hop_3/ppermute | solution.py:164
  78.4 2.9 %update_block.4 = (f32[256,768]{1,0:T(8,128)S(1)}, f32[256,768]{1,0:T(8,128)S(1)}) custom-call(s32[1]{0:T(128)} %bitcast.7.group_ref, s32[4]{0:T(128)S(1)} %gather_fusion, bf16[160,768]{1,0:T(8,128)(2,1)S(1)} %get-tuple-element.42.panel_ref, bf16[192,768]{1,0:T(8,128)(2,1)S(1)} %constant_dynamic-update-slice_fusion.refs_0_, ...), custom_call_target="tpu_custom_call" | custom-call | flops 805306368 | bytes 3932160 | tf_op jit(solution)/shard_map/update_block/pallas_call | solution.py:137
  81.3 2.9 %update_block.5 = (f32[256,768]{1,0:T(8,128)S(1)}, f32[256,768]{1,0:T(8,128)S(1)}) custom-call(s32[1]{0:T(128)} %bitcast.6.group_ref, s32[4]{0:T(128)S(1)} %gather_fusion, bf16[160,768]{1,0:T(8,128)(2,1)S(1)} %collective-permute-done.15.panel_ref, bf16[192,768]{1,0:T(8,128)(2,1)S(1)} %constant_dynamic-update-slice_fusion.refs_0_, ...), custom_call_target="tpu_custom_call" | custom-call | flops 805306368 | bytes 3932160 | tf_op jit(solution)/shard_map/update_block/pallas_call | solution.py:137
  84.2 2.9 %update_block.6 = (f32[256,768]{1,0:T(8,128)S(1)}, f32[256,768]{1,0:T(8,128)S(1)}) custom-call(s32[1]{0:T(128)} %bitcast.5.group_ref, s32[4]{0:T(128)S(1)} %gather_fusion, bf16[160,768]{1,0:T(8,128)(2,1)S(1)} %collective-permute-done.12.panel_ref, bf16[192,768]{1,0:T(8,128)(2,1)S(1)} %constant_dynamic-update-slice_fusion.2.refs_0_, ...), custom_call_target="tpu_custom_call" | custom-call | flops 805306368 | bytes 3932160 | tf_op jit(solution)/shard_map/update_block/pallas_call | solution.py:137
  87.1 4.0 %update_block.7 = (f32[256,768]{1,0:T(8,128)}, f32[256,768]{1,0:T(8,128)}) custom-call(s32[1]{0:T(128)} %bitcast.group_ref, s32[4]{0:T(128)S(1)} %gather_fusion, bf16[160,768]{1,0:T(8,128)(2,1)S(1)} %collective-permute-done.10.panel_ref, bf16[192,768]{1,0:T(8,128)(2,1)S(1)} %constant_dynamic-update-slice_fusion.2.refs_0_, ...), custom_call_target="tpu_custom_call" | custom-call | flops 805306368 | bytes 3932160 | tf_op jit(solution)/shard_map/update_block/pallas_call | solution.py:137
  (62 shorter events, 13.9 us)
Async XLA Ops:
  0.6 14.9 %copy-start = (s32[4,32,4]{1,2,0:T(4,128)S(1)}, s32[4,32,4]{1,2,0:T(4,128)}, u32[]{:S(2)}) copy-start(s32[4,32,4]{1,2,0:T(4,128)} %param.14) | copy-start | bytes 6148
  0.6 1.1 %copy-start.1 = (bf16[512,768]{1,0:T(8,128)(2,1)S(1)}, bf16[512,768]{1,0:T(8,128)(2,1)}, u32[]{:S(2)}) copy-start(bf16[512,768]{1,0:T(8,128)(2,1)} %source.1) | copy-start | bytes 2359300
  2.6 13.4 %collective-permute-start = (bf16[96,768]{1,0:T(8,128)(2,1)S(1)}, bf16[96,768]{1,0:T(8,128)(2,1)S(1)}, u32[]{:S(2)}, u32[]{:S(2)}) collective-permute-start(bf16[96,768]{1,0:T(8,128)(2,1)S(1)} %get-tuple-element.30), channel_id=1, source_target_pairs={{0,1},{1,2},{2,3},{3,0},{4,5},{5,6},{6,7},{7,4},{8,9},{9,10},{10,1... | collective-permute-start | bytes 442376 | tf_op jit(solution)/shard_map/lower_lab_shift_1/ppermute | solution.py:164
  5.6 12.3 %collective-permute-start.1 = (bf16[96,768]{1,0:T(8,128)(2,1)S(1)}, bf16[96,768]{1,0:T(8,128)(2,1)S(1)}, u32[]{:S(2)}, u32[]{:S(2)}) collective-permute-start(bf16[96,768]{1,0:T(8,128)(2,1)S(1)} %get-tuple-element.31), channel_id=1, source_target_pairs={{0,2},{1,3},{2,0},{3,1},{4,6},{5,7},{6,4},{7,5},{8,10},{9,11},{10,... | collective-permute-start | bytes 442376 | tf_op jit(solution)/shard_map/lower_lab_shift_2/ppermute | solution.py:164
  8.2 1.4 %copy-start.4 = (s32[512,16]{0,1:T(8,128)S(1)}, s32[512,16]{0,1:T(8,128)}, u32[]{:S(2)}) copy-start(s32[512,16]{0,1:T(8,128)} %param.10) | copy-start | bytes 98308
  8.2 1.4 %slice-start = ((bf16[512,768]{1,0:T(8,128)(2,1)}), bf16[128,768]{1,0:T(8,128)(2,1)S(1)}, s32[]{:S(2)}) async-start(bf16[512,768]{1,0:T(8,128)(2,1)} %source.1), calls=%async_computation | async-start | bytes 393216 | tf_op jit(solution)/shard_map/slice | solution.py:184
  8.2 9.7 %collective-permute-start.2 = (bf16[96,768]{1,0:T(8,128)(2,1)S(1)}, bf16[96,768]{1,0:T(8,128)(2,1)S(1)}, u32[]{:S(2)}, u32[]{:S(2)}) collective-permute-start(bf16[96,768]{1,0:T(8,128)(2,1)S(1)} %get-tuple-element.32), channel_id=1, source_target_pairs={{0,3},{1,0},{2,1},{3,2},{4,7},{5,4},{6,5},{7,6},{8,11},{9,8},{10,9... | collective-permute-start | bytes 442376 | tf_op jit(solution)/shard_map/lower_lab_shift_3/ppermute | solution.py:164
  9.7 16.6 %collective-permute-start.7 = (bf16[160,768]{1,0:T(8,128)(2,1)S(1)}, bf16[160,768]{1,0:T(8,128)(2,1)S(1)}, u32[]{:S(2)}, u32[]{:S(2)}) collective-permute-start(bf16[160,768]{1,0:T(8,128)(2,1)S(1)} %fusion.1.refs_0_), channel_id=1, source_target_pairs={{0,1},{1,3},{3,2},{2,0},{4,5},{5,7},{7,6},{6,4},{8,9},{9,11},{11,1... | collective-permute-start | bytes 737288 | tf_op jit(solution)/shard_map/upper_lab_hop_1/ppermute | solution.py:164
  11.3 0.7 copy-start.6
  18.6 7.7 %collective-permute-start.3 = (bf16[96,768]{1,0:T(8,128)(2,1)S(1)}, bf16[96,768]{1,0:T(8,128)(2,1)S(1)}, u32[]{:S(2)}, u32[]{:S(2)}) collective-permute-start(bf16[96,768]{1,0:T(8,128)(2,1)S(1)} %get-tuple-element.34), channel_id=1, source_target_pairs={{0,28},{4,0},{8,4},{12,8},{16,12},{20,16},{24,20},{28,24},{1,29},{... | collective-permute-start | bytes 442376 | tf_op jit(solution)/shard_map/lower_doc_shift_1/ppermute | solution.py:164
  22.1 13.9 %collective-permute-start.5 = (bf16[96,768]{1,0:T(8,128)(2,1)S(1)}, bf16[96,768]{1,0:T(8,128)(2,1)S(1)}, u32[]{:S(2)}, u32[]{:S(2)}) collective-permute-start(bf16[96,768]{1,0:T(8,128)(2,1)S(1)} %get-tuple-element.35), channel_id=1, source_target_pairs={{0,24},{4,28},{8,0},{12,4},{16,8},{20,12},{24,16},{28,20},{1,25},{... | collective-permute-start | bytes 442376 | tf_op jit(solution)/shard_map/lower_doc_shift_2/ppermute | solution.py:164
  26.3 9.7 %collective-permute-start.8 = (bf16[160,768]{1,0:T(8,128)(2,1)S(1)}, bf16[160,768]{1,0:T(8,128)(2,1)S(1)}, u32[]{:S(2)}, u32[]{:S(2)}) collective-permute-start(bf16[160,768]{1,0:T(8,128)(2,1)S(1)} %collective-permute-done.7.refs_1_), channel_id=1, source_target_pairs={{0,1},{1,3},{3,2},{2,0},{4,5},{5,7},{7,6},{6,4},{8,9},{9,11},{11,1... | collective-permute-start | bytes 737288 | tf_op jit(solution)/shard_map/upper_lab_hop_2/ppermute | solution.py:164
  26.4 15.9 %collective-permute-start.4 = (bf16[192,768]{1,0:T(8,128)(2,1)S(1)}, bf16[192,768]{1,0:T(8,128)(2,1)S(1)}, u32[]{:S(2)}, u32[]{:S(2)}) collective-permute-start(bf16[192,768]{1,0:T(8,128)(2,1)S(1)} %constant_dynamic-update-slice_fusion.refs_0_), channel_id=1, source_target_pairs={{0,1},{1,3},{3,2},{2,0},{4,5},{5,7},{7,6},{6,4},{8,9},{9,11},{11,1... | collective-permute-start | bytes 884744 | tf_op jit(solution)/shard_map/part_0_lab_hop_1/ppermute | solution.py:164
  29.1 6.9 %collective-permute-start.6 = (bf16[96,768]{1,0:T(8,128)(2,1)S(1)}, bf16[96,768]{1,0:T(8,128)(2,1)S(1)}, u32[]{:S(2)}, u32[]{:S(2)}) collective-permute-start(bf16[96,768]{1,0:T(8,128)(2,1)S(1)} %get-tuple-element.36), channel_id=1, source_target_pairs={{0,20},{4,24},{8,28},{12,0},{16,4},{20,8},{24,12},{28,16},{1,21},{... | collective-permute-start | bytes 442376 | tf_op jit(solution)/shard_map/lower_doc_shift_3/ppermute | solution.py:164
  36.0 10.6 %collective-permute-start.9 = (bf16[160,768]{1,0:T(8,128)(2,1)S(1)}, bf16[160,768]{1,0:T(8,128)(2,1)S(1)}, u32[]{:S(2)}, u32[]{:S(2)}) collective-permute-start(bf16[160,768]{1,0:T(8,128)(2,1)S(1)} %collective-permute-done.8.refs_2_), channel_id=1, source_target_pairs={{0,1},{1,3},{3,2},{2,0},{4,5},{5,7},{7,6},{6,4},{8,9},{9,11},{11,1... | collective-permute-start | bytes 737288 | tf_op jit(solution)/shard_map/upper_lab_hop_3/ppermute | solution.py:164
  47.3 11.1 %collective-permute-start.11 = (bf16[192,768]{1,0:T(8,128)(2,1)S(1)}, bf16[192,768]{1,0:T(8,128)(2,1)S(1)}, u32[]{:S(2)}, u32[]{:S(2)}) collective-permute-start(bf16[192,768]{1,0:T(8,128)(2,1)S(1)} %constant_dynamic-update-slice_fusion.2.refs_0_), channel_id=1, source_target_pairs={{0,1},{1,3},{3,2},{2,0},{4,5},{5,7},{7,6},{6,4},{8,9},{9,11},{11,1... | collective-permute-start | bytes 884744 | tf_op jit(solution)/shard_map/part_1_lab_hop_1/ppermute | solution.py:164
  47.4 6.9 %collective-permute-start.15 = (bf16[160,768]{1,0:T(8,128)(2,1)S(1)}, bf16[160,768]{1,0:T(8,128)(2,1)S(1)}, u32[]{:S(2)}, u32[]{:S(2)}) collective-permute-start(bf16[160,768]{1,0:T(8,128)(2,1)S(1)} %get-tuple-element.47), channel_id=1, source_target_pairs={{0,28},{4,0},{8,4},{12,8},{16,12},{20,16},{24,20},{28,24},{1,29},{... | collective-permute-start | bytes 737288 | tf_op jit(solution)/shard_map/upper_doc_shift_1/ppermute | solution.py:164
  48.7 9.7 %collective-permute-start.12 = (bf16[160,768]{1,0:T(8,128)(2,1)S(1)}, bf16[160,768]{1,0:T(8,128)(2,1)S(1)}, u32[]{:S(2)}, u32[]{:S(2)}) collective-permute-start(bf16[160,768]{1,0:T(8,128)(2,1)S(1)} %get-tuple-element.44), channel_id=1, source_target_pairs={{0,24},{4,28},{8,0},{12,4},{16,8},{20,12},{24,16},{28,20},{1,25},{... | collective-permute-start | bytes 737288 | tf_op jit(solution)/shard_map/upper_doc_shift_2/ppermute | solution.py:164
  54.3 11.8 %collective-permute-start.16 = (bf16[192,768]{1,0:T(8,128)(2,1)S(1)}, bf16[192,768]{1,0:T(8,128)(2,1)S(1)}, u32[]{:S(2)}, u32[]{:S(2)}) collective-permute-start(bf16[192,768]{1,0:T(8,128)(2,1)S(1)} %collective-permute-done.4.refs_1_), channel_id=1, source_target_pairs={{0,1},{1,3},{3,2},{2,0},{4,5},{5,7},{7,6},{6,4},{8,9},{9,11},{11,1... | collective-permute-start | bytes 884744 | tf_op jit(solution)/shard_map/part_0_lab_hop_2/ppermute | solution.py:164
  58.4 12.5 %collective-permute-start.13 = (bf16[192,768]{1,0:T(8,128)(2,1)S(1)}, bf16[192,768]{1,0:T(8,128)(2,1)S(1)}, u32[]{:S(2)}, u32[]{:S(2)}) collective-permute-start(bf16[192,768]{1,0:T(8,128)(2,1)S(1)} %collective-permute-done.11.refs_1_), channel_id=1, source_target_pairs={{0,1},{1,3},{3,2},{2,0},{4,5},{5,7},{7,6},{6,4},{8,9},{9,11},{11,1... | collective-permute-start | bytes 884744 | tf_op jit(solution)/shard_map/part_1_lab_hop_2/ppermute | solution.py:164
  60.5 5.6 %collective-permute-start.10 = (bf16[160,768]{1,0:T(8,128)(2,1)S(1)}, bf16[160,768]{1,0:T(8,128)(2,1)S(1)}, u32[]{:S(2)}, u32[]{:S(2)}) collective-permute-start(bf16[160,768]{1,0:T(8,128)(2,1)S(1)} %get-tuple-element.41), channel_id=1, source_target_pairs={{0,20},{4,24},{8,28},{12,0},{16,4},{20,8},{24,12},{28,16},{1,21},{... | collective-permute-start | bytes 737288 | tf_op jit(solution)/shard_map/upper_doc_shift_3/ppermute | solution.py:164
  66.1 11.1 %collective-permute-start.17 = (bf16[192,768]{1,0:T(8,128)(2,1)S(1)}, bf16[192,768]{1,0:T(8,128)(2,1)S(1)}, u32[]{:S(2)}, u32[]{:S(2)}) collective-permute-start(bf16[192,768]{1,0:T(8,128)(2,1)S(1)} %collective-permute-done.16.refs_2_), channel_id=1, source_target_pairs={{0,1},{1,3},{3,2},{2,0},{4,5},{5,7},{7,6},{6,4},{8,9},{9,11},{11,1... | collective-permute-start | bytes 884744 | tf_op jit(solution)/shard_map/part_0_lab_hop_3/ppermute | solution.py:164
  70.9 13.2 %collective-permute-start.14 = (bf16[192,768]{1,0:T(8,128)(2,1)S(1)}, bf16[192,768]{1,0:T(8,128)(2,1)S(1)}, u32[]{:S(2)}, u32[]{:S(2)}) collective-permute-start(bf16[192,768]{1,0:T(8,128)(2,1)S(1)} %collective-permute-done.13.refs_2_), channel_id=1, source_target_pairs={{0,1},{1,3},{3,2},{2,0},{4,5},{5,7},{7,6},{6,4},{8,9},{9,11},{11,1... | collective-permute-start | bytes 884744 | tf_op jit(solution)/shard_map/part_1_lab_hop_3/ppermute | solution.py:164
  77.2 1.1 %copy-start.2 = (f32[256,768]{1,0:T(8,128)S(1)}, f32[256,768]{1,0:T(8,128)}, u32[]{:S(2)}) copy-start(f32[256,768]{1,0:T(8,128)} %refs_6_.1) | copy-start | bytes 2359300
  (2 other events, 1.3 us)

commit v3 on v2

--- a/solution.py
+++ b/solution.py
@@ -11,7 +11,10 @@
 STEPS = 4
 POS = 16
 LOWER = 6
-GROUP = 2
+GROUPS = ((0, 1), (2, 3))
+LANES = 128
+UPDATE_MIB = 7
+PACK_MIB = 48
 
 learning_rate = 0.1
 beta_rate = 0.9
@@ -71,9 +74,16 @@
         in_specs=[SMEM, ANY],
         out_specs=[VMEM] * n,
         scratch_shapes=[pltpu.SemaphoreType.DMA((n,))],
-        compiler_params=pltpu.CompilerParams(vmem_limit_bytes=8 * MIB),
+        compiler_params=pltpu.CompilerParams(vmem_limit_bytes=PACK_MIB * MIB),
         name="pack_pieces",
     )(lab, source)
+
+
+def coded(high, low):
+    value = (low + 128).astype(jnp.float32) * 2.0**-64
+    for bit in range(7):
+        value = jnp.where((high >> bit) & 1 == 1, value * 2.0 ** (1 << bit), value)
+    return value
 
 
 def split(value):
@@ -88,14 +98,14 @@
     return dot(pair[1], other) + dot(pair[0], other)
 
 
-def update_kernel(first, top, size, offset, scale, group_ref, places_ref, panel_ref, *refs):
+def update_kernel(first, top, size, offset, scale, places_ref, panel_ref, *refs):
     n = places_ref.shape[0]
     pieces, refs = refs[:n], refs[n:]
     if first:
-        live_ref, parents_ref, weight_ref, weight_out, moment_out, rows_ref = refs
+        live_ref, pick_ref, weight_ref, weight_out, moment_out, rows_ref = refs
     else:
-        live_ref, parents_ref, weight_ref, moment_ref, weight_out, moment_out, rows_ref = refs
-    labels, width = weight_ref.shape
+        live_ref, pick_ref, weight_ref, moment_ref, weight_out, moment_out, rows_ref = refs
+    labels = weight_ref.shape[0]
     count = rows_ref.shape[0]
     rows_ref[:top, :] = panel_ref[:top, :]
     for k, piece in enumerate(pieces):
@@ -104,31 +114,29 @@
     rows = rows_ref[...]
     weight = weight_ref[...]
     pair = split(weight)
-    group = group_ref[0].astype(jnp.bfloat16)
-    within = panel_ref[top : top + POS, :count]
-    own = jnp.where(panel_ref[top + POS :, :count] == group, within, jnp.bfloat16(-1.0))
-    label = lax.broadcasted_iota(jnp.int32, (labels, count), 0)
-    label = label.astype(jnp.float32).astype(jnp.bfloat16)
+    label = lax.broadcasted_iota(jnp.int32, (labels, LANES), 0)
+    label = ((label & 127) + 128) << (label >> 7)
+    label = (label.astype(jnp.float32) * live_ref[:, count:]).astype(jnp.bfloat16)
+    label = jnp.concatenate([label] * (count // LANES), axis=1)
     target = jnp.zeros(label.shape, jnp.bfloat16)
     for k in range(POS):
-        target = jnp.where(label == own[k : k + 1, :], jnp.bfloat16(1.0), target)
+        code = panel_ref[top + k : top + k + 1, :count]
+        target = jnp.where(label == code, jnp.bfloat16(1.0), target)
     scores = product(pair, rows, ((1,), (1,))) * scale
-    resid = (jax.nn.sigmoid(scores) - target.astype(jnp.float32)) * live_ref[...]
+    resid = (jax.nn.sigmoid(scores) - target.astype(jnp.float32)) * live_ref[:, :count]
     grad = product(split(resid), rows, ((1,), (0,)))
-    column = lax.broadcasted_iota(jnp.int32, (labels, labels), 1)
-    pick = (column == parents_ref[...]).astype(jnp.bfloat16)
     dot = functools.partial(jnp.dot, preferred_element_type=jnp.float32)
-    parent = dot(pick, pair[1]) + dot(pick, pair[0])
+    parent = dot(pick_ref[...], pair[1]) + dot(pick_ref[...], pair[0])
     grad = grad * scale + pull_rate * (weight - parent)
     moment = grad if first else beta_rate * moment_ref[...] + grad
     moment_out[...] = moment
     weight_out[...] = weight - learning_rate * moment
 
 
-def update(group, places, panel, pieces, offset, live, parents, weight, moment, last):
+def update(places, panel, pieces, offset, live, pick, weight, moment, last):
     labels, width = weight.shape
-    count = live.shape[1]
-    top = panel.shape[0] - 2 * POS
+    count = live.shape[1] - LANES
+    top = panel.shape[0] - POS
     size = (count - top) // len(pieces)
     first = moment is None
     state = [weight] if first else [weight, moment]
@@ -137,17 +145,17 @@
     return pl.pallas_call(
         functools.partial(update_kernel, first, top, size, offset, scale),
         out_shape=[shape, shape],
-        in_specs=[SMEM, SMEM] + [VMEM] * (len(pieces) + 3 + len(state)),
+        in_specs=[SMEM] + [VMEM] * (len(pieces) + 3 + len(state)),
         out_specs=[VMEM, VMEM],
         scratch_shapes=[pltpu.VMEM((count, width), panel.dtype)],
-        compiler_params=pltpu.CompilerParams(vmem_limit_bytes=12 * MIB),
+        compiler_params=pltpu.CompilerParams(vmem_limit_bytes=UPDATE_MIB * MIB),
         cost_estimate=pl.CostEstimate(
             flops=8 * labels * width * count,
             bytes_accessed=2 * count * width + 16 * labels * width,
             transcendentals=labels * count,
         ),
         name="update_block",
-    )(group, places, panel, *pieces, live, parents, *state)
+    )(places, panel, *pieces, live, pick, *state)
 
 
 def after(value, *earlier):
@@ -172,15 +180,14 @@
     labels, width = weights.shape
     rows = embeddings.shape[0]
     home = doc_index * lab_count + lab_index
-    unit = 16 * lab_count
-    size = max(1, rows * LOWER // unit // 8) * 16
+    grain = 16 * lab_count
+    size = max(1, rows * LOWER // grain // 8) * 16
     top = rows - size * lab_count
 
     mine = pack(embeddings, top, lab_count, lab_index[None])
 
-    groups = positives // labels
-    codes = jnp.concatenate([positives - groups * labels, groups], axis=1).T
-    codes = jnp.pad(codes, ((0, 0), (0, width - rows))).astype(jnp.bfloat16)
+    codes = coded(positives.T >> 7, positives.T & 127).astype(jnp.bfloat16)
+    codes = jnp.pad(codes, ((0, 0), (0, width - rows)))
     upper = jnp.concatenate([embeddings[:top], codes], axis=0)
 
     order = circle(lab_count)
@@ -195,9 +202,13 @@
     listed = lists[:, :, None] == jnp.arange(rows, dtype=jnp.int32) // TILE
     listed = listed & (jnp.arange(lists.shape[1], dtype=jnp.int32) < used)[:, :, None]
     live = jnp.any(listed, axis=1).astype(jnp.float32)
-    group = jnp.arange(STEPS, dtype=jnp.int32)[:, None] * lab_count + lab_index
-    parent_rows = lax.dynamic_slice_in_dim(parents, home * labels, labels, 0)[:, None]
-    prepared = (which_upper, places, live, group, parent_rows)
+    base = (jnp.arange(STEPS, dtype=jnp.int32) * lab_count + lab_index) * labels
+    unit = jnp.broadcast_to(coded(base >> 7, jnp.zeros_like(base))[:, None], (STEPS, LANES))
+    live = jnp.concatenate([live, unit / 128.0], axis=1)
+    parent_rows = lax.dynamic_slice_in_dim(parents, home * labels, labels, 0)
+    pick = parent_rows[:, None] == jnp.arange(labels, dtype=jnp.int32)
+    pick = pick.astype(jnp.bfloat16)
+    prepared = (which_upper, places, live, pick)
 
     around = [(order[i], order[(i + 1) % lab_count]) for i in range(lab_count)]
 
@@ -219,33 +230,33 @@
     hop(*prepared, lower[0])
     lower = [lower[0]] + [shift("lower", s, lower[s]) for s in range(1, STEPS)]
     for r in range(3, lab_count):
-        hop(lower[1])
-    parts = []
-    for g in range(0, STEPS, GROUP):
-        parts.append([jnp.concatenate(lower[g : g + GROUP], axis=0)])
+        hop(*lower[1:])
+    parts = [[jnp.concatenate([lower[s] for s in steps], axis=0)] for steps in GROUPS]
 
     def spread(g, *earlier):
         part = parts[g]
         part.append(send(f"part_{g}_lab_hop_{len(part)}", part[-1], "lab", around, *earlier))
 
-    spread(0)
-    found = select(which_upper, [after(held[0], parts[0][1], *lower), *held[1:]])
+    spread(0, *lower)
+    found = select(which_upper, [after(held[0], parts[0][1]), *held[1:]])
     found = [found[0]] + [shift("upper", s, found[s]) for s in range(1, STEPS)]
-    spread(1, found[0])
+    spread(1)
     for r in range(2, lab_count):
-        spread(0, found[min(2 * r - 3, STEPS - 1)])
-        spread(1, found[min(2 * r - 2, STEPS - 1)])
+        if r == 2:
+            spread(0)
+        else:
+            spread(0, found[min(r - 2, STEPS - 1)])
+        spread(1, found[min(r - 1, STEPS - 1)])
 
     weight, moment = weights, None
     for s in range(STEPS):
         weight, moment = update(
-            group[s],
             places,
             found[s],
-            parts[s // GROUP],
-            s % GROUP * size,
+            parts[s in GROUPS[1]],
+            (s - GROUPS[s in GROUPS[1]][0]) * size,
             live[s : s + 1],
-            parent_rows,
+            pick,
             weight,
             moment,
             s == STEPS - 1,

time: 92 us -> 83 us (0.902)
  waiting for transfers between devices: 43.5 us -> 34.9 us
  starting transfers between devices: 21.9 us -> 26.5 us
  Pallas kernels: 14.8 us -> 12.2 us
  local copies, waits for them, and re-layouts: 8.1 us -> 6.3 us
    ppermute x18, waiting for transfers between devices: 43.5 us -> 34.9 us  [send(): return lax.ppermute(value, axis, pairs)]
    ppermute x18, starting transfers between devices: 21.9 us -> 26.5 us  [send(): return lax.ppermute(value, axis, pairs)]
    pallas_call x4, Pallas kernels: 12.6 us -> 10 us  [update(): pl.pallas_call(functools.partial(update_kernel, first, top, size, offset,...]
    unnamed x16, local copies, waits for them, and re-layouts: 4.31 us -> 3.18 us
  transfers between devices with their start and end apart: 18 -> 18, of which waited for: 10 -> 11; matrix products, arithmetic and copies ran while one was open for 6% -> 6% of each run, Pallas kernels for 7% -> 10%
where the time goes in v3:
time: 83 us; the launch traced here: 82.8 us
  waiting for transfers between devices  34.9 us (42%)
  starting transfers between devices  26.5 us (32%)
  Pallas kernels  12.2 us (15%)
  local copies, waits for them, and re-layouts  6.3 us (8%)
  other arithmetic  2.01 us (2%)
  between operations  0.85 us (1%)
    ppermute x18, waiting for transfers between devices, send(): return lax.ppermute(value, axis, pairs)  34.9 us
    ppermute x18, starting transfers between devices, send(): return lax.ppermute(value, axis, pairs)  26.5 us
    pallas_call x4, Pallas kernels, update(): pl.pallas_call(functools.partial(update_kernel, first, top, size, offset,...  10 us
    unnamed x16, local copies, waits for them, and re-layouts  3.18 us
  transfers between devices with their start and end apart: 18, of which 11 were waited for; matrix products, arithmetic and copies ran while one was open for 6% of the time, Pallas kernels for 10%

profile of v3, /device:TPU:0, one launch (start us, length us, event | category | flops | bytes accessed | tf_op | source)
XLA Modules:
  0.0 82.8 jit_solution(13595471877907867062)
XLA Ops:
  0.7 1.1 %copy-done.1 = bf16[512,768]{1,0:T(8,128)(2,1)S(1)} copy-done((bf16[512,768]{1,0:T(8,128)(2,1)S(1)}, bf16[512,768]{1,0:T(8,128)(2,1)}, u32[]{:S(2)}) %copy-start.1) | copy-done | bytes 786456
  2.6 3.1 %collective-permute-start = (bf16[96,768]{1,0:T(8,128)(2,1)S(1)}, bf16[96,768]{1,0:T(8,128)(2,1)S(1)}, u32[]{:S(2)}, u32[]{:S(2)}) collective-permute-start(bf16[96,768]{1,0:T(8,128)(2,1)S(1)} %get-tuple-element.29), channel_id=1, source_target_pairs={{0,1},{1,2},{2,3},{3,0},{4,5},{5,6},{6,7},{7,4},{8,9},{9,10},{10,1... | collective-permute-start | bytes 442376 | tf_op jit(solution)/shard_map/lower_lab_shift_1/ppermute | solution.py:172
  5.6 2.6 %collective-permute-start.1 = (bf16[96,768]{1,0:T(8,128)(2,1)S(1)}, bf16[96,768]{1,0:T(8,128)(2,1)S(1)}, u32[]{:S(2)}, u32[]{:S(2)}) collective-permute-start(bf16[96,768]{1,0:T(8,128)(2,1)S(1)} %get-tuple-element.30), channel_id=1, source_target_pairs={{0,2},{1,3},{2,0},{3,1},{4,6},{5,7},{6,4},{7,5},{8,10},{9,11},{10,... | collective-permute-start | bytes 442376 | tf_op jit(solution)/shard_map/lower_lab_shift_2/ppermute | solution.py:172
  8.2 1.3 %collective-permute-start.2 = (bf16[96,768]{1,0:T(8,128)(2,1)S(1)}, bf16[96,768]{1,0:T(8,128)(2,1)S(1)}, u32[]{:S(2)}, u32[]{:S(2)}) collective-permute-start(bf16[96,768]{1,0:T(8,128)(2,1)S(1)} %get-tuple-element.31), channel_id=1, source_target_pairs={{0,3},{1,0},{2,1},{3,2},{4,7},{5,4},{6,5},{7,6},{8,11},{9,8},{10,9... | collective-permute-start | bytes 442376 | tf_op jit(solution)/shard_map/lower_lab_shift_3/ppermute | solution.py:172
  15.5 2.4 %collective-permute-done.1.refs_2_ = bf16[96,768]{1,0:T(8,128)(2,1)S(1)} collective-permute-done((bf16[96,768]{1,0:T(8,128)(2,1)S(1)}, bf16[96,768]{1,0:T(8,128)(2,1)S(1)}, u32[]{:S(2)}, u32[]{:S(2)}) %collective-permute-start.1) | collective-permute-done | bytes 147488 | tf_op jit(solution)/shard_map/lower_lab_shift_2/ppermute | solution.py:172
  18.6 2.0 %collective-permute-start.3 = (bf16[96,768]{1,0:T(8,128)(2,1)S(1)}, bf16[96,768]{1,0:T(8,128)(2,1)S(1)}, u32[]{:S(2)}, u32[]{:S(2)}) collective-permute-start(bf16[96,768]{1,0:T(8,128)(2,1)S(1)} %get-tuple-element.33), channel_id=1, source_target_pairs={{0,28},{4,0},{8,4},{12,8},{16,12},{20,16},{24,20},{28,24},{1,29},{... | collective-permute-start | bytes 442376 | tf_op jit(solution)/shard_map/lower_doc_shift_1/ppermute | solution.py:172
  22.1 3.6 %collective-permute-done.7.refs_1_ = bf16[144,768]{1,0:T(8,128)(2,1)S(1)} collective-permute-done((bf16[144,768]{1,0:T(8,128)(2,1)S(1)}, bf16[144,768]{1,0:T(8,128)(2,1)S(1)}, u32[]{:S(2)}, u32[]{:S(2)}) %collective-permute-start.7) | collective-permute-done | bytes 221216 | tf_op jit(solution)/shard_map/upper_lab_hop_1/ppermute | solution.py:172
  25.9 2.2 %collective-permute-done.4 = bf16[96,768]{1,0:T(8,128)(2,1)S(1)} collective-permute-done((bf16[96,768]{1,0:T(8,128)(2,1)S(1)}, bf16[96,768]{1,0:T(8,128)(2,1)S(1)}, u32[]{:S(2)}, u32[]{:S(2)}) %collective-permute-start.4) | collective-permute-done | bytes 147488 | tf_op jit(solution)/shard_map/lower_doc_shift_2/ppermute | solution.py:172
  28.1 3.7 %collective-permute-start.6 = (bf16[192,768]{1,0:T(8,128)(2,1)S(1)}, bf16[192,768]{1,0:T(8,128)(2,1)S(1)}, u32[]{:S(2)}, u32[]{:S(2)}) collective-permute-start(bf16[192,768]{1,0:T(8,128)(2,1)S(1)} %constant_dynamic-update-slice_fusion.refs_0_), channel_id=1, source_target_pairs={{0,1},{1,3},{3,2},{2,0},{4,5},{5,7},{7,6},{6,4},{8,9},{9,11},{11,1... | collective-permute-start | bytes 884744 | tf_op jit(solution)/shard_map/part_0_lab_hop_1/ppermute | solution.py:172
  31.8 3.1 %collective-permute-done.8.refs_2_ = bf16[144,768]{1,0:T(8,128)(2,1)S(1)} collective-permute-done((bf16[144,768]{1,0:T(8,128)(2,1)S(1)}, bf16[144,768]{1,0:T(8,128)(2,1)S(1)}, u32[]{:S(2)}, u32[]{:S(2)}) %collective-permute-start.8) | collective-permute-done | bytes 221216 | tf_op jit(solution)/shard_map/upper_lab_hop_2/ppermute | solution.py:172
  35.0 2.2 %collective-permute-start.11 = (bf16[192,768]{1,0:T(8,128)(2,1)S(1)}, bf16[192,768]{1,0:T(8,128)(2,1)S(1)}, u32[]{:S(2)}, u32[]{:S(2)}) collective-permute-start(bf16[192,768]{1,0:T(8,128)(2,1)S(1)} %constant_dynamic-update-slice_fusion.2.refs_0_), channel_id=1, source_target_pairs={{0,1},{1,3},{3,2},{2,0},{4,5},{5,7},{7,6},{6,4},{8,9},{9,11},{11,1... | collective-permute-start | bytes 884744 | tf_op jit(solution)/shard_map/part_1_lab_hop_1/ppermute | solution.py:172
  37.2 4.1 %collective-permute-done.6.refs_1_ = bf16[192,768]{1,0:T(8,128)(2,1)S(1)} collective-permute-done((bf16[192,768]{1,0:T(8,128)(2,1)S(1)}, bf16[192,768]{1,0:T(8,128)(2,1)S(1)}, u32[]{:S(2)}, u32[]{:S(2)}) %collective-permute-start.6) | collective-permute-done | bytes 294944 | tf_op jit(solution)/shard_map/part_0_lab_hop_1/ppermute | solution.py:172
  41.2 4.7 %collective-permute-done.9.refs_3_ = bf16[144,768]{1,0:T(8,128)(2,1)S(1)} collective-permute-done((bf16[144,768]{1,0:T(8,128)(2,1)S(1)}, bf16[144,768]{1,0:T(8,128)(2,1)S(1)}, u32[]{:S(2)}, u32[]{:S(2)}) %collective-permute-start.9) | collective-permute-done | bytes 221216 | tf_op jit(solution)/shard_map/upper_lab_hop_3/ppermute | solution.py:172
  46.7 1.6 %collective-permute-start.12 = (bf16[144,768]{1,0:T(8,128)(2,1)S(1)}, bf16[144,768]{1,0:T(8,128)(2,1)S(1)}, u32[]{:S(2)}, u32[]{:S(2)}) collective-permute-start(bf16[144,768]{1,0:T(8,128)(2,1)S(1)} %get-tuple-element.42), channel_id=1, source_target_pairs={{0,28},{4,0},{8,4},{12,8},{16,12},{20,16},{24,20},{28,24},{1,29},{... | collective-permute-start | bytes 663560 | tf_op jit(solution)/shard_map/upper_doc_shift_1/ppermute | solution.py:172
  49.2 2.4 %collective-permute-start.16 = (bf16[192,768]{1,0:T(8,128)(2,1)S(1)}, bf16[192,768]{1,0:T(8,128)(2,1)S(1)}, u32[]{:S(2)}, u32[]{:S(2)}) collective-permute-start(bf16[192,768]{1,0:T(8,128)(2,1)S(1)} %collective-permute-done.6.refs_1_), channel_id=1, source_target_pairs={{0,1},{1,3},{3,2},{2,0},{4,5},{5,7},{7,6},{6,4},{8,9},{9,11},{11,1... | collective-permute-start | bytes 884744 | tf_op jit(solution)/shard_map/part_0_lab_hop_2/ppermute | solution.py:172
  51.7 2.7 %collective-permute-start.13 = (bf16[192,768]{1,0:T(8,128)(2,1)S(1)}, bf16[192,768]{1,0:T(8,128)(2,1)S(1)}, u32[]{:S(2)}, u32[]{:S(2)}) collective-permute-start(bf16[192,768]{1,0:T(8,128)(2,1)S(1)} %collective-permute-done.11.refs_1_), channel_id=1, source_target_pairs={{0,1},{1,3},{3,2},{2,0},{4,5},{5,7},{7,6},{6,4},{8,9},{9,11},{11,1... | collective-permute-start | bytes 884744 | tf_op jit(solution)/shard_map/part_1_lab_hop_2/ppermute | solution.py:172
  54.7 1.5 %collective-permute-start.14 = (bf16[144,768]{1,0:T(8,128)(2,1)S(1)}, bf16[144,768]{1,0:T(8,128)(2,1)S(1)}, u32[]{:S(2)}, u32[]{:S(2)}) collective-permute-start(bf16[144,768]{1,0:T(8,128)(2,1)S(1)} %get-tuple-element.44), channel_id=1, source_target_pairs={{0,24},{4,28},{8,0},{12,4},{16,8},{20,12},{24,16},{28,20},{1,25},{... | collective-permute-start | bytes 663560 | tf_op jit(solution)/shard_map/upper_doc_shift_2/ppermute | solution.py:172
  56.2 3.8 %collective-permute-done.16.refs_2_ = bf16[192,768]{1,0:T(8,128)(2,1)S(1)} collective-permute-done((bf16[192,768]{1,0:T(8,128)(2,1)S(1)}, bf16[192,768]{1,0:T(8,128)(2,1)S(1)}, u32[]{:S(2)}, u32[]{:S(2)}) %collective-permute-start.16) | collective-permute-done | bytes 294944 | tf_op jit(solution)/shard_map/part_0_lab_hop_2/ppermute | solution.py:172
  61.9 4.5 %collective-permute-done.13.refs_2_ = bf16[192,768]{1,0:T(8,128)(2,1)S(1)} collective-permute-done((bf16[192,768]{1,0:T(8,128)(2,1)S(1)}, bf16[192,768]{1,0:T(8,128)(2,1)S(1)}, u32[]{:S(2)}, u32[]{:S(2)}) %collective-permute-start.13) | collective-permute-done | bytes 294944 | tf_op jit(solution)/shard_map/part_1_lab_hop_2/ppermute | solution.py:172
  67.3 5.3 %collective-permute-done.17.refs_3_ = bf16[192,768]{1,0:T(8,128)(2,1)S(1)} collective-permute-done((bf16[192,768]{1,0:T(8,128)(2,1)S(1)}, bf16[192,768]{1,0:T(8,128)(2,1)S(1)}, u32[]{:S(2)}, u32[]{:S(2)}) %collective-permute-start.17) | collective-permute-done | bytes 294944 | tf_op jit(solution)/shard_map/part_0_lab_hop_3/ppermute | solution.py:172
  72.7 2.2 %update_block.4 = (f32[256,768]{1,0:T(8,128)S(1)}, f32[256,768]{1,0:T(8,128)S(1)}) custom-call(s32[4]{0:T(128)S(1)} %gather_fusion, bf16[144,768]{1,0:T(8,128)(2,1)S(1)} %get-tuple-element.47.panel_ref, bf16[192,768]{1,0:T(8,128)(2,1)S(1)} %constant_dynamic-update-slice_fusion.refs_0_, bf16[192,768]{1,0:T(8,128)(2,1)S(1)} %collective-permute-done.6.refs_1_, ...), custom_call_target="tpu_custom_call" | custom-call | flops 805306368 | bytes 3932160 | tf_op jit(solution)/shard_map/update_block/pallas_call | solution.py:145
  74.9 2.2 %update_block.5 = (f32[256,768]{1,0:T(8,128)S(1)}, f32[256,768]{1,0:T(8,128)S(1)}) custom-call(s32[4]{0:T(128)S(1)} %gather_fusion, bf16[144,768]{1,0:T(8,128)(2,1)S(1)} %collective-permute-done.12.panel_ref, bf16[192,768]{1,0:T(8,128)(2,1)S(1)} %constant_dynamic-update-slice_fusion.refs_0_, bf16[192,768]{1,0:T(8,128)(2,1)S(1)} %collective-permute-done.6.refs_1_, ...), custom_call_target="tpu_custom_call" | custom-call | flops 805306368 | bytes 3932160 | tf_op jit(solution)/shard_map/update_block/pallas_call | solution.py:145
  77.2 2.2 %update_block.6 = (f32[256,768]{1,0:T(8,128)S(1)}, f32[256,768]{1,0:T(8,128)S(1)}) custom-call(s32[4]{0:T(128)S(1)} %gather_fusion, bf16[144,768]{1,0:T(8,128)(2,1)S(1)} %collective-permute-done.14.panel_ref, bf16[192,768]{1,0:T(8,128)(2,1)S(1)} %constant_dynamic-update-slice_fusion.2.refs_0_, bf16[192,768]{1,0:T(8,128)(2,1)S(1)} %collective-permute-done.11.refs_1_, ...), custom_call_target="tpu_custom_call" | custom-call | flops 805306368 | bytes 3932160 | tf_op jit(solution)/shard_map/update_block/pallas_call | solution.py:145
  79.4 3.4 %update_block.7 = (f32[256,768]{1,0:T(8,128)}, f32[256,768]{1,0:T(8,128)}) custom-call(s32[4]{0:T(128)S(1)} %gather_fusion, bf16[144,768]{1,0:T(8,128)(2,1)S(1)} %collective-permute-done.10.panel_ref, bf16[192,768]{1,0:T(8,128)(2,1)S(1)} %constant_dynamic-update-slice_fusion.2.refs_0_, bf16[192,768]{1,0:T(8,128)(2,1)S(1)} %collective-permute-done.11.refs_1_, ...), custom_call_target="tpu_custom_call" | custom-call | flops 805306368 | bytes 3932160 | tf_op jit(solution)/shard_map/update_block/pallas_call | solution.py:145
  (61 shorter events, 13.7 us)
Async XLA Ops:
  0.6 53.9 %copy-start = (s32[4,32,4]{1,2,0:T(4,128)S(1)}, s32[4,32,4]{1,2,0:T(4,128)}, u32[]{:S(2)}) copy-start(s32[4,32,4]{1,2,0:T(4,128)} %param.14) | copy-start | bytes 6148
  0.6 1.1 %copy-start.1 = (bf16[512,768]{1,0:T(8,128)(2,1)S(1)}, bf16[512,768]{1,0:T(8,128)(2,1)}, u32[]{:S(2)}) copy-start(bf16[512,768]{1,0:T(8,128)(2,1)} %source.1) | copy-start | bytes 2359300
  2.6 12.9 %collective-permute-start = (bf16[96,768]{1,0:T(8,128)(2,1)S(1)}, bf16[96,768]{1,0:T(8,128)(2,1)S(1)}, u32[]{:S(2)}, u32[]{:S(2)}) collective-permute-start(bf16[96,768]{1,0:T(8,128)(2,1)S(1)} %get-tuple-element.29), channel_id=1, source_target_pairs={{0,1},{1,2},{2,3},{3,0},{4,5},{5,6},{6,7},{7,4},{8,9},{9,10},{10,1... | collective-permute-start | bytes 442376 | tf_op jit(solution)/shard_map/lower_lab_shift_1/ppermute | solution.py:172
  5.6 12.3 %collective-permute-start.1 = (bf16[96,768]{1,0:T(8,128)(2,1)S(1)}, bf16[96,768]{1,0:T(8,128)(2,1)S(1)}, u32[]{:S(2)}, u32[]{:S(2)}) collective-permute-start(bf16[96,768]{1,0:T(8,128)(2,1)S(1)} %get-tuple-element.30), channel_id=1, source_target_pairs={{0,2},{1,3},{2,0},{3,1},{4,6},{5,7},{6,4},{7,5},{8,10},{9,11},{10,... | collective-permute-start | bytes 442376 | tf_op jit(solution)/shard_map/lower_lab_shift_2/ppermute | solution.py:172
  8.2 1.4 %copy-start.4 = (s32[512,16]{0,1:T(8,128)S(1)}, s32[512,16]{0,1:T(8,128)}, u32[]{:S(2)}) copy-start(s32[512,16]{0,1:T(8,128)} %param.10) | copy-start | bytes 98308
  8.2 1.4 %slice-start = ((bf16[512,768]{1,0:T(8,128)(2,1)}), bf16[128,768]{1,0:T(8,128)(2,1)S(1)}, s32[]{:S(2)}) async-start(bf16[512,768]{1,0:T(8,128)(2,1)} %source.1), calls=%async_computation | async-start | bytes 393216 | tf_op jit(solution)/shard_map/slice | solution.py:191
  8.2 9.7 %collective-permute-start.2 = (bf16[96,768]{1,0:T(8,128)(2,1)S(1)}, bf16[96,768]{1,0:T(8,128)(2,1)S(1)}, u32[]{:S(2)}, u32[]{:S(2)}) collective-permute-start(bf16[96,768]{1,0:T(8,128)(2,1)S(1)} %get-tuple-element.31), channel_id=1, source_target_pairs={{0,3},{1,0},{2,1},{3,2},{4,7},{5,4},{6,5},{7,6},{8,11},{9,8},{10,9... | collective-permute-start | bytes 442376 | tf_op jit(solution)/shard_map/lower_lab_shift_3/ppermute | solution.py:172
  9.7 16.1 %collective-permute-start.7 = (bf16[144,768]{1,0:T(8,128)(2,1)S(1)}, bf16[144,768]{1,0:T(8,128)(2,1)S(1)}, u32[]{:S(2)}, u32[]{:S(2)}) collective-permute-start(bf16[144,768]{1,0:T(8,128)(2,1)S(1)} %fusion.2.refs_0_), channel_id=1, source_target_pairs={{0,1},{1,3},{3,2},{2,0},{4,5},{5,7},{7,6},{6,4},{8,9},{9,11},{11,1... | collective-permute-start | bytes 663560 | tf_op jit(solution)/shard_map/upper_lab_hop_1/ppermute | solution.py:172
  10.4 0.7 copy-start.6
  18.6 7.2 %collective-permute-start.3 = (bf16[96,768]{1,0:T(8,128)(2,1)S(1)}, bf16[96,768]{1,0:T(8,128)(2,1)S(1)}, u32[]{:S(2)}, u32[]{:S(2)}) collective-permute-start(bf16[96,768]{1,0:T(8,128)(2,1)S(1)} %get-tuple-element.33), channel_id=1, source_target_pairs={{0,28},{4,0},{8,4},{12,8},{16,12},{20,16},{24,20},{28,24},{1,29},{... | collective-permute-start | bytes 442376 | tf_op jit(solution)/shard_map/lower_doc_shift_1/ppermute | solution.py:172
  21.3 6.8 %collective-permute-start.4 = (bf16[96,768]{1,0:T(8,128)(2,1)S(1)}, bf16[96,768]{1,0:T(8,128)(2,1)S(1)}, u32[]{:S(2)}, u32[]{:S(2)}) collective-permute-start(bf16[96,768]{1,0:T(8,128)(2,1)S(1)} %get-tuple-element.34), channel_id=1, source_target_pairs={{0,24},{4,28},{8,0},{12,4},{16,8},{20,12},{24,16},{28,20},{1,25},{... | collective-permute-start | bytes 442376 | tf_op jit(solution)/shard_map/lower_doc_shift_2/ppermute | solution.py:172
  21.8 6.3 %collective-permute-start.5 = (bf16[96,768]{1,0:T(8,128)(2,1)S(1)}, bf16[96,768]{1,0:T(8,128)(2,1)S(1)}, u32[]{:S(2)}, u32[]{:S(2)}) collective-permute-start(bf16[96,768]{1,0:T(8,128)(2,1)S(1)} %get-tuple-element.35), channel_id=1, source_target_pairs={{0,20},{4,24},{8,28},{12,0},{16,4},{20,8},{24,12},{28,16},{1,21},{... | collective-permute-start | bytes 442376 | tf_op jit(solution)/shard_map/lower_doc_shift_3/ppermute | solution.py:172
  25.7 9.2 %collective-permute-start.8 = (bf16[144,768]{1,0:T(8,128)(2,1)S(1)}, bf16[144,768]{1,0:T(8,128)(2,1)S(1)}, u32[]{:S(2)}, u32[]{:S(2)}) collective-permute-start(bf16[144,768]{1,0:T(8,128)(2,1)S(1)} %collective-permute-done.7.refs_1_), channel_id=1, source_target_pairs={{0,1},{1,3},{3,2},{2,0},{4,5},{5,7},{7,6},{6,4},{8,9},{9,11},{11,1... | collective-permute-start | bytes 663560 | tf_op jit(solution)/shard_map/upper_lab_hop_2/ppermute | solution.py:172
  25.9 46.8 %copy-start.2 = (f32[256,768]{1,0:T(8,128)S(1)}, f32[256,768]{1,0:T(8,128)}, u32[]{:S(2)}) copy-start(f32[256,768]{1,0:T(8,128)} %refs_6_.1) | copy-start | bytes 2359300
  28.1 13.1 %collective-permute-start.6 = (bf16[192,768]{1,0:T(8,128)(2,1)S(1)}, bf16[192,768]{1,0:T(8,128)(2,1)S(1)}, u32[]{:S(2)}, u32[]{:S(2)}) collective-permute-start(bf16[192,768]{1,0:T(8,128)(2,1)S(1)} %constant_dynamic-update-slice_fusion.refs_0_), channel_id=1, source_target_pairs={{0,1},{1,3},{3,2},{2,0},{4,5},{5,7},{7,6},{6,4},{8,9},{9,11},{11,1... | collective-permute-start | bytes 884744 | tf_op jit(solution)/shard_map/part_0_lab_hop_1/ppermute | solution.py:172
  34.9 11.1 %collective-permute-start.9 = (bf16[144,768]{1,0:T(8,128)(2,1)S(1)}, bf16[144,768]{1,0:T(8,128)(2,1)S(1)}, u32[]{:S(2)}, u32[]{:S(2)}) collective-permute-start(bf16[144,768]{1,0:T(8,128)(2,1)S(1)} %collective-permute-done.8.refs_2_), channel_id=1, source_target_pairs={{0,1},{1,3},{3,2},{2,0},{4,5},{5,7},{7,6},{6,4},{8,9},{9,11},{11,1... | collective-permute-start | bytes 663560 | tf_op jit(solution)/shard_map/upper_lab_hop_3/ppermute | solution.py:172
  35.0 16.7 %collective-permute-start.11 = (bf16[192,768]{1,0:T(8,128)(2,1)S(1)}, bf16[192,768]{1,0:T(8,128)(2,1)S(1)}, u32[]{:S(2)}, u32[]{:S(2)}) collective-permute-start(bf16[192,768]{1,0:T(8,128)(2,1)S(1)} %constant_dynamic-update-slice_fusion.2.refs_0_), channel_id=1, source_target_pairs={{0,1},{1,3},{3,2},{2,0},{4,5},{5,7},{7,6},{6,4},{8,9},{9,11},{11,1... | collective-permute-start | bytes 884744 | tf_op jit(solution)/shard_map/part_1_lab_hop_1/ppermute | solution.py:172
  46.7 5.1 %collective-permute-start.12 = (bf16[144,768]{1,0:T(8,128)(2,1)S(1)}, bf16[144,768]{1,0:T(8,128)(2,1)S(1)}, u32[]{:S(2)}, u32[]{:S(2)}) collective-permute-start(bf16[144,768]{1,0:T(8,128)(2,1)S(1)} %get-tuple-element.42), channel_id=1, source_target_pairs={{0,28},{4,0},{8,4},{12,8},{16,12},{20,16},{24,20},{28,24},{1,29},{... | collective-permute-start | bytes 663560 | tf_op jit(solution)/shard_map/upper_doc_shift_1/ppermute | solution.py:172
  49.2 10.9 %collective-permute-start.16 = (bf16[192,768]{1,0:T(8,128)(2,1)S(1)}, bf16[192,768]{1,0:T(8,128)(2,1)S(1)}, u32[]{:S(2)}, u32[]{:S(2)}) collective-permute-start(bf16[192,768]{1,0:T(8,128)(2,1)S(1)} %collective-permute-done.6.refs_1_), channel_id=1, source_target_pairs={{0,1},{1,3},{3,2},{2,0},{4,5},{5,7},{7,6},{6,4},{8,9},{9,11},{11,1... | collective-permute-start | bytes 884744 | tf_op jit(solution)/shard_map/part_0_lab_hop_2/ppermute | solution.py:172
  51.7 14.6 %collective-permute-start.13 = (bf16[192,768]{1,0:T(8,128)(2,1)S(1)}, bf16[192,768]{1,0:T(8,128)(2,1)S(1)}, u32[]{:S(2)}, u32[]{:S(2)}) collective-permute-start(bf16[192,768]{1,0:T(8,128)(2,1)S(1)} %collective-permute-done.11.refs_1_), channel_id=1, source_target_pairs={{0,1},{1,3},{3,2},{2,0},{4,5},{5,7},{7,6},{6,4},{8,9},{9,11},{11,1... | collective-permute-start | bytes 884744 | tf_op jit(solution)/shard_map/part_1_lab_hop_2/ppermute | solution.py:172
  54.7 7.1 %collective-permute-start.14 = (bf16[144,768]{1,0:T(8,128)(2,1)S(1)}, bf16[144,768]{1,0:T(8,128)(2,1)S(1)}, u32[]{:S(2)}, u32[]{:S(2)}) collective-permute-start(bf16[144,768]{1,0:T(8,128)(2,1)S(1)} %get-tuple-element.44), channel_id=1, source_target_pairs={{0,24},{4,28},{8,0},{12,4},{16,8},{20,12},{24,16},{28,20},{1,25},{... | collective-permute-start | bytes 663560 | tf_op jit(solution)/shard_map/upper_doc_shift_2/ppermute | solution.py:172
  60.1 12.6 %collective-permute-start.17 = (bf16[192,768]{1,0:T(8,128)(2,1)S(1)}, bf16[192,768]{1,0:T(8,128)(2,1)S(1)}, u32[]{:S(2)}, u32[]{:S(2)}) collective-permute-start(bf16[192,768]{1,0:T(8,128)(2,1)S(1)} %collective-permute-done.16.refs_2_), channel_id=1, source_target_pairs={{0,1},{1,3},{3,2},{2,0},{4,5},{5,7},{7,6},{6,4},{8,9},{9,11},{11,1... | collective-permute-start | bytes 884744 | tf_op jit(solution)/shard_map/part_0_lab_hop_3/ppermute | solution.py:172
  66.4 10.8 %collective-permute-start.15 = (bf16[192,768]{1,0:T(8,128)(2,1)S(1)}, bf16[192,768]{1,0:T(8,128)(2,1)S(1)}, u32[]{:S(2)}, u32[]{:S(2)}) collective-permute-start(bf16[192,768]{1,0:T(8,128)(2,1)S(1)} %collective-permute-done.13.refs_2_), channel_id=1, source_target_pairs={{0,1},{1,3},{3,2},{2,0},{4,5},{5,7},{7,6},{6,4},{8,9},{9,11},{11,1... | collective-permute-start | bytes 884744 | tf_op jit(solution)/shard_map/part_1_lab_hop_3/ppermute | solution.py:172
  67.3 12.1 %collective-permute-start.10 = (bf16[144,768]{1,0:T(8,128)(2,1)S(1)}, bf16[144,768]{1,0:T(8,128)(2,1)S(1)}, u32[]{:S(2)}, u32[]{:S(2)}) collective-permute-start(bf16[144,768]{1,0:T(8,128)(2,1)S(1)} %get-tuple-element.41), channel_id=1, source_target_pairs={{0,20},{4,24},{8,28},{12,0},{16,4},{20,8},{24,12},{28,16},{1,21},{... | collective-permute-start | bytes 663560 | tf_op jit(solution)/shard_map/upper_doc_shift_3/ppermute | solution.py:172
  (2 other events, 1.3 us)

commit v4 on v3

--- a/solution.py
+++ b/solution.py
@@ -13,50 +13,53 @@
 LOWER = 6
 GROUPS = ((0, 1), (2, 3))
 LANES = 128
+COLUMNS = 256
 UPDATE_MIB = 7
-PACK_MIB = 48
+PACK_MIB = 60
 
 learning_rate = 0.1
 beta_rate = 0.9
 pull_rate = 1.0
 
 VMEM = pl.BlockSpec(memory_space=pltpu.VMEM)
-SMEM = pl.BlockSpec(memory_space=pltpu.SMEM)
-ANY = pl.BlockSpec(memory_space=pl.ANY)
+HBM = pl.BlockSpec(memory_space=pltpu.HBM)
 MIB = 1024 * 1024
+
+
+def circle(n):
+    return [*range(0, 1), *range(1, n, 2), *reversed(range(2, n, 2))]
 
 
 def select_kernel(n, which_ref, *refs):
     sources, outs = refs[:n], refs[n:]
     for k, out in enumerate(outs):
-        for i, source in enumerate(sources):
-
-            @pl.when(which_ref[k] == i)
-            def _(source=source, out=out):
-                out[...] = source[...]
+        which = which_ref[k : k + 1, :]
+        value = sources[0][...]
+        for i in range(1, n):
+            value = jnp.where(which == jnp.bfloat16(i), sources[i][...], value)
+        out[...] = value
 
 
 def select(which, sources):
     size = sources[0].size * sources[0].dtype.itemsize
+    count = which.shape[0]
     return pl.pallas_call(
         functools.partial(select_kernel, len(sources)),
-        out_shape=[pltpu.VMEM(sources[0].shape, sources[0].dtype)] * which.shape[0],
-        in_specs=[SMEM] + [VMEM] * len(sources),
-        out_specs=[VMEM] * which.shape[0],
+        out_shape=[pltpu.VMEM(sources[0].shape, sources[0].dtype)] * count,
+        in_specs=[VMEM] * (1 + len(sources)),
+        out_specs=[VMEM] * count,
         compiler_params=pltpu.CompilerParams(vmem_limit_bytes=12 * MIB),
-        cost_estimate=pl.CostEstimate(
-            flops=0, bytes_accessed=2 * which.shape[0] * size, transcendentals=0
-        ),
+        cost_estimate=pl.CostEstimate(flops=0, bytes_accessed=2 * count * size, transcendentals=0),
         name="select_panels",
     )(which, *sources)
 
 
-def pack_kernel(start, size, lab_ref, source, *refs):
+def pack_kernel(start, size, source, *refs):
     outs, sem = refs[:-1], refs[-1]
     n = len(outs)
     copies = []
     for k, out in enumerate(outs):
-        piece = lax.rem(lab_ref[0] + k, n)
+        piece = lax.rem(lax.axis_index("lab") + k, n)
         row = pl.multiple_of(start + piece * size, 16)
         copies.append(pltpu.make_async_copy(source.at[pl.ds(row, size)], out, sem.at[k]))
     for copy in copies:
@@ -65,18 +68,18 @@
         copy.wait()
 
 
-def pack(source, start, n, lab):
+def pack(source, start, n):
     size = (source.shape[0] - start) // n
     shape = (size, source.shape[1])
     return pl.pallas_call(
         functools.partial(pack_kernel, start, size),
         out_shape=[pltpu.VMEM(shape, source.dtype)] * n,
-        in_specs=[SMEM, ANY],
+        in_specs=[HBM],
         out_specs=[VMEM] * n,
         scratch_shapes=[pltpu.SemaphoreType.DMA((n,))],
         compiler_params=pltpu.CompilerParams(vmem_limit_bytes=PACK_MIB * MIB),
         name="pack_pieces",
-    )(lab, source)
+    )(source)
 
 
 def coded(high, low):
@@ -98,22 +101,28 @@
     return dot(pair[1], other) + dot(pair[0], other)
 
 
-def update_kernel(first, top, size, offset, scale, places_ref, panel_ref, *refs):
-    n = places_ref.shape[0]
+def update_kernel(first, last, n, top, size, offset, scale, panel_ref, *refs):
+    order = circle(n)
+    lab = lax.axis_index("lab")
+    place = sum(jnp.where(lab == i, order.index(i), 0) for i in range(n))
     pieces, refs = refs[:n], refs[n:]
-    if first:
-        live_ref, pick_ref, weight_ref, weight_out, moment_out, rows_ref = refs
-    else:
-        live_ref, pick_ref, weight_ref, moment_ref, weight_out, moment_out, rows_ref = refs
+    live_ref, pick_ref, weight_ref, *refs = refs
+    moment_ref = None if first else refs.pop(0)
+    weight_out, moment_out, rows_ref, *refs = refs
     labels = weight_ref.shape[0]
     count = rows_ref.shape[0]
     rows_ref[:top, :] = panel_ref[:top, :]
     for k, piece in enumerate(pieces):
-        row = pl.multiple_of(top + places_ref[k] * size, 16)
+        at = lax.rem(place + n - k, n)
+        plane = sum(jnp.where(at == i, order[i], 0) for i in range(n))
+        row = pl.multiple_of(top + plane * size, 16)
         rows_ref[pl.ds(row, size), :] = piece[offset : offset + size, :]
     rows = rows_ref[...]
     weight = weight_ref[...]
     pair = split(weight)
+    dot = functools.partial(jnp.dot, preferred_element_type=jnp.float32)
+    parent = dot(pick_ref[...], pair[1]) + dot(pick_ref[...], pair[0])
+    pull = pull_rate * (weight - parent)
     label = lax.broadcasted_iota(jnp.int32, (labels, LANES), 0)
     label = ((label & 127) + 128) << (label >> 7)
     label = (label.astype(jnp.float32) * live_ref[:, count:]).astype(jnp.bfloat16)
@@ -124,16 +133,30 @@
         target = jnp.where(label == code, jnp.bfloat16(1.0), target)
     scores = product(pair, rows, ((1,), (1,))) * scale
     resid = (jax.nn.sigmoid(scores) - target.astype(jnp.float32)) * live_ref[:, :count]
-    grad = product(split(resid), rows, ((1,), (0,)))
-    dot = functools.partial(jnp.dot, preferred_element_type=jnp.float32)
-    parent = dot(pick_ref[...], pair[1]) + dot(pick_ref[...], pair[0])
-    grad = grad * scale + pull_rate * (weight - parent)
-    moment = grad if first else beta_rate * moment_ref[...] + grad
-    moment_out[...] = moment
-    weight_out[...] = weight - learning_rate * moment
-
-
-def update(places, panel, pieces, offset, live, pick, weight, moment, last):
+    resid = split(resid)
+    columns = COLUMNS if last else weight.shape[1]
+    copies = []
+    for c in range(0, weight.shape[1], columns):
+        part = slice(c, c + columns)
+        grad = product(resid, rows[:, part], ((1,), (0,))) * scale + pull[:, part]
+        moment = grad if first else beta_rate * moment_ref[:, part] + grad
+        value = weight[:, part] - learning_rate * moment
+        if not last:
+            moment_out[:, part] = moment
+            weight_out[:, part] = value
+            continue
+        weight_held, moment_held, sem = refs
+        weight_held[:, part] = value
+        moment_held[:, part] = moment
+        for held, out in ((weight_held, weight_out), (moment_held, moment_out)):
+            done = sem.at[len(copies)]
+            copies.append(pltpu.make_async_copy(held.at[:, part], out.at[:, part], done))
+            copies[-1].start()
+    for copy in copies:
+        copy.wait()
+
+
+def update(panel, pieces, offset, live, pick, weight, moment, last):
     labels, width = weight.shape
     count = live.shape[1] - LANES
     top = panel.shape[0] - POS
@@ -141,13 +164,17 @@
     first = moment is None
     state = [weight] if first else [weight, moment]
     shape = (jax.ShapeDtypeStruct if last else pltpu.VMEM)(weight.shape, jnp.float32)
+    scratch = [pltpu.VMEM((count, width), panel.dtype)]
+    if last:
+        scratch += [pltpu.VMEM(weight.shape, jnp.float32)] * 2
+        scratch += [pltpu.SemaphoreType.DMA((2 * width // COLUMNS,))]
     scale = 1.0 / float(width) ** 0.5
     return pl.pallas_call(
-        functools.partial(update_kernel, first, top, size, offset, scale),
+        functools.partial(update_kernel, first, last, len(pieces), top, size, offset, scale),
         out_shape=[shape, shape],
-        in_specs=[SMEM] + [VMEM] * (len(pieces) + 3 + len(state)),
-        out_specs=[VMEM, VMEM],
-        scratch_shapes=[pltpu.VMEM((count, width), panel.dtype)],
+        in_specs=[VMEM] * (len(pieces) + 3 + len(state)),
+        out_specs=[HBM if last else VMEM] * 2,
+        scratch_shapes=scratch,
         compiler_params=pltpu.CompilerParams(vmem_limit_bytes=UPDATE_MIB * MIB),
         cost_estimate=pl.CostEstimate(
             flops=8 * labels * width * count,
@@ -155,15 +182,11 @@
             transcendentals=labels * count,
         ),
         name="update_block",
-    )(places, panel, *pieces, live, pick, *state)
+    )(panel, *pieces, live, pick, *state)
 
 
 def after(value, *earlier):
     return lax.optimization_barrier((value, *earlier))[0]
-
-
-def circle(n):
-    return [*range(0, 1), *range(1, n, 2), *reversed(range(2, n, 2))]
 
 
 def send(what, value, axis, pairs, *earlier):
@@ -184,19 +207,21 @@
     size = max(1, rows * LOWER // grain // 8) * 16
     top = rows - size * lab_count
 
-    mine = pack(embeddings, top, lab_count, lab_index[None])
+    mine = pack(embeddings, top, lab_count)
 
     codes = coded(positives.T >> 7, positives.T & 127).astype(jnp.bfloat16)
     codes = jnp.pad(codes, ((0, 0), (0, width - rows)))
     upper = jnp.concatenate([embeddings[:top], codes], axis=0)
 
     order = circle(lab_count)
-    order_of = jnp.array(order, jnp.int32)
     place_of = jnp.array([order.index(i) for i in range(lab_count)], jnp.int32)
     owner = lax.dynamic_index_in_dim(owners, doc_index, 1, keepdims=False)
     which_upper = (place_of[lab_index] - place_of[owner]) % lab_count
     which_lower = (lab_index - owner) % lab_count
-    places = order_of[(place_of[lab_index] - jnp.arange(lab_count, dtype=jnp.int32)) % lab_count]
+    which_upper, which_lower = (
+        jnp.broadcast_to(which[:, None], (STEPS, width)).astype(jnp.bfloat16)
+        for which in (which_upper, which_lower)
+    )
     lists = lax.dynamic_index_in_dim(shortlist, home, 1, keepdims=False)
     used = lax.dynamic_index_in_dim(counts, home, 1, keepdims=True)
     listed = lists[:, :, None] == jnp.arange(rows, dtype=jnp.int32) // TILE
@@ -208,7 +233,7 @@
     parent_rows = lax.dynamic_slice_in_dim(parents, home * labels, labels, 0)
     pick = parent_rows[:, None] == jnp.arange(labels, dtype=jnp.int32)
     pick = pick.astype(jnp.bfloat16)
-    prepared = (which_upper, places, live, pick)
+    prepared = (which_upper, live, pick)
 
     around = [(order[i], order[(i + 1) % lab_count]) for i in range(lab_count)]
 
@@ -251,7 +276,6 @@
     weight, moment = weights, None
     for s in range(STEPS):
         weight, moment = update(
-            places,
             found[s],
             parts[s in GROUPS[1]],
             (s - GROUPS[s in GROUPS[1]][0]) * size,

time: 83 us -> 80.5 us (0.970)
  waiting for transfers between devices: 34.9 us -> 38.9 us
  Pallas kernels: 12.2 us -> 9.17 us
  local copies, waits for them, and re-layouts: 6.3 us -> 4.67 us
  starting transfers between devices: 26.5 us -> 25.3 us
    ppermute x18, waiting for transfers between devices: 34.9 us -> 38.9 us  [send(): return lax.ppermute(value, axis, pairs)]
    pallas_call x4, Pallas kernels: 10 us -> 7.57 us  [update(): pl.pallas_call(functools.partial(update_kernel, first, last, len(pieces),...]
    ppermute x18, starting transfers between devices: 26.5 us -> 25.3 us  [send(): return lax.ppermute(value, axis, pairs)]
    unnamed x16 -> x14, local copies, waits for them, and re-layouts: 3.18 us -> 2.05 us
    pallas_call x2, Pallas kernels: 1.4 us -> 0.43 us  [select(): pl.pallas_call(functools.partial(select_kernel, len(sources)), out_shape=...]
    convert_element_type x0 -> x2, other arithmetic: none -> 0.85 us  [local(): jnp.broadcast_to(which[:, None], (STEPS, width)).astype(jnp.bfloat16)]
  transfers between devices with their start and end apart: 18 -> 18, of which waited for: 11 -> 12; matrix products, arithmetic and copies ran while one was open for 6% -> 5% of each run, Pallas kernels for 10% -> 7%
where the time goes in v4:
time: 80.5 us; the launch traced here: 80.3 us
  waiting for transfers between devices  38.9 us (48%)
  starting transfers between devices  25.3 us (31%)
  Pallas kernels  9.17 us (11%)
  local copies, waits for them, and re-layouts  4.67 us (6%)
  other arithmetic  1.42 us (2%)
  between operations  0.82 us (1%)
    ppermute x18, waiting for transfers between devices, send(): return lax.ppermute(value, axis, pairs)  38.9 us
    ppermute x18, starting transfers between devices, send(): return lax.ppermute(value, axis, pairs)  25.3 us
    pallas_call x4, Pallas kernels, update(): pl.pallas_call(functools.partial(update_kernel, first, last, len(pieces),...  7.57 us
    unnamed x14, local copies, waits for them, and re-layouts  2.05 us
  transfers between devices with their start and end apart: 18, of which 12 were waited for; matrix products, arithmetic and copies ran while one was open for 5% of the time, Pallas kernels for 7%

profile of v4, /device:TPU:0, one launch (start us, length us, event | category | flops | bytes accessed | tf_op | source)
XLA Modules:
  0.0 80.3 jit_solution(4171010238982748006)
XLA Ops:
  1.8 3.1 %collective-permute-start = (bf16[96,768]{1,0:T(8,128)(2,1)S(1)}, bf16[96,768]{1,0:T(8,128)(2,1)S(1)}, u32[]{:S(2)}, u32[]{:S(2)}) collective-permute-start(bf16[96,768]{1,0:T(8,128)(2,1)S(1)} %get-tuple-element.29), channel_id=1, source_target_pairs={{0,1},{1,2},{2,3},{3,0},{4,5},{5,6},{6,7},{7,4},{8,9},{9,10},{10,1... | collective-permute-start | bytes 442376 | tf_op jit(solution)/shard_map/lower_lab_shift_1/ppermute | solution.py:195
  4.9 2.6 %collective-permute-start.1 = (bf16[96,768]{1,0:T(8,128)(2,1)S(1)}, bf16[96,768]{1,0:T(8,128)(2,1)S(1)}, u32[]{:S(2)}, u32[]{:S(2)}) collective-permute-start(bf16[96,768]{1,0:T(8,128)(2,1)S(1)} %get-tuple-element.30), channel_id=1, source_target_pairs={{0,2},{1,3},{2,0},{3,1},{4,6},{5,7},{6,4},{7,5},{8,10},{9,11},{10,... | collective-permute-start | bytes 442376 | tf_op jit(solution)/shard_map/lower_lab_shift_2/ppermute | solution.py:195
  7.5 1.3 %collective-permute-start.2 = (bf16[96,768]{1,0:T(8,128)(2,1)S(1)}, bf16[96,768]{1,0:T(8,128)(2,1)S(1)}, u32[]{:S(2)}, u32[]{:S(2)}) collective-permute-start(bf16[96,768]{1,0:T(8,128)(2,1)S(1)} %get-tuple-element.31), channel_id=1, source_target_pairs={{0,3},{1,0},{2,1},{3,2},{4,7},{5,4},{6,5},{7,6},{8,11},{9,8},{10,9... | collective-permute-start | bytes 442376 | tf_op jit(solution)/shard_map/lower_lab_shift_3/ppermute | solution.py:195
  13.5 3.7 %collective-permute-done.1.refs_2_ = bf16[96,768]{1,0:T(8,128)(2,1)S(1)} collective-permute-done((bf16[96,768]{1,0:T(8,128)(2,1)S(1)}, bf16[96,768]{1,0:T(8,128)(2,1)S(1)}, u32[]{:S(2)}, u32[]{:S(2)}) %collective-permute-start.1) | collective-permute-done | bytes 147488 | tf_op jit(solution)/shard_map/lower_lab_shift_2/ppermute | solution.py:195
  17.4 2.0 %collective-permute-start.3 = (bf16[96,768]{1,0:T(8,128)(2,1)S(1)}, bf16[96,768]{1,0:T(8,128)(2,1)S(1)}, u32[]{:S(2)}, u32[]{:S(2)}) collective-permute-start(bf16[96,768]{1,0:T(8,128)(2,1)S(1)} %get-tuple-element.33), channel_id=1, source_target_pairs={{0,28},{4,0},{8,4},{12,8},{16,12},{20,16},{24,20},{28,24},{1,29},{... | collective-permute-start | bytes 442376 | tf_op jit(solution)/shard_map/lower_doc_shift_1/ppermute | solution.py:195
  21.0 4.0 %collective-permute-done.7.refs_1_ = bf16[144,768]{1,0:T(8,128)(2,1)S(1)} collective-permute-done((bf16[144,768]{1,0:T(8,128)(2,1)S(1)}, bf16[144,768]{1,0:T(8,128)(2,1)S(1)}, u32[]{:S(2)}, u32[]{:S(2)}) %collective-permute-start.7) | collective-permute-done | bytes 221216 | tf_op jit(solution)/shard_map/upper_lab_hop_1/ppermute | solution.py:195
  25.1 1.8 %collective-permute-done.4 = bf16[96,768]{1,0:T(8,128)(2,1)S(1)} collective-permute-done((bf16[96,768]{1,0:T(8,128)(2,1)S(1)}, bf16[96,768]{1,0:T(8,128)(2,1)S(1)}, u32[]{:S(2)}, u32[]{:S(2)}) %collective-permute-start.4) | collective-permute-done | bytes 147488 | tf_op jit(solution)/shard_map/lower_doc_shift_2/ppermute | solution.py:195
  26.9 3.7 %collective-permute-start.6 = (bf16[192,768]{1,0:T(8,128)(2,1)S(1)}, bf16[192,768]{1,0:T(8,128)(2,1)S(1)}, u32[]{:S(2)}, u32[]{:S(2)}) collective-permute-start(bf16[192,768]{1,0:T(8,128)(2,1)S(1)} %constant_dynamic-update-slice_fusion.refs_0_), channel_id=1, source_target_pairs={{0,1},{1,3},{3,2},{2,0},{4,5},{5,7},{7,6},{6,4},{8,9},{9,11},{11,1... | collective-permute-start | bytes 884744 | tf_op jit(solution)/shard_map/part_0_lab_hop_1/ppermute | solution.py:195
  30.6 3.6 %collective-permute-done.8.refs_2_ = bf16[144,768]{1,0:T(8,128)(2,1)S(1)} collective-permute-done((bf16[144,768]{1,0:T(8,128)(2,1)S(1)}, bf16[144,768]{1,0:T(8,128)(2,1)S(1)}, u32[]{:S(2)}, u32[]{:S(2)}) %collective-permute-start.8) | collective-permute-done | bytes 221216 | tf_op jit(solution)/shard_map/upper_lab_hop_2/ppermute | solution.py:195
  34.3 1.8 %collective-permute-start.11 = (bf16[192,768]{1,0:T(8,128)(2,1)S(1)}, bf16[192,768]{1,0:T(8,128)(2,1)S(1)}, u32[]{:S(2)}, u32[]{:S(2)}) collective-permute-start(bf16[192,768]{1,0:T(8,128)(2,1)S(1)} %constant_dynamic-update-slice_fusion.2.refs_0_), channel_id=1, source_target_pairs={{0,1},{1,3},{3,2},{2,0},{4,5},{5,7},{7,6},{6,4},{8,9},{9,11},{11,1... | collective-permute-start | bytes 884744 | tf_op jit(solution)/shard_map/part_1_lab_hop_1/ppermute | solution.py:195
  36.1 4.5 %collective-permute-done.6.refs_1_ = bf16[192,768]{1,0:T(8,128)(2,1)S(1)} collective-permute-done((bf16[192,768]{1,0:T(8,128)(2,1)S(1)}, bf16[192,768]{1,0:T(8,128)(2,1)S(1)}, u32[]{:S(2)}, u32[]{:S(2)}) %collective-permute-start.6) | collective-permute-done | bytes 294944 | tf_op jit(solution)/shard_map/part_0_lab_hop_1/ppermute | solution.py:195
  40.6 4.7 %collective-permute-done.9.refs_3_ = bf16[144,768]{1,0:T(8,128)(2,1)S(1)} collective-permute-done((bf16[144,768]{1,0:T(8,128)(2,1)S(1)}, bf16[144,768]{1,0:T(8,128)(2,1)S(1)}, u32[]{:S(2)}, u32[]{:S(2)}) %collective-permute-start.9) | collective-permute-done | bytes 221216 | tf_op jit(solution)/shard_map/upper_lab_hop_3/ppermute | solution.py:195
  47.5 2.4 %collective-permute-start.16 = (bf16[192,768]{1,0:T(8,128)(2,1)S(1)}, bf16[192,768]{1,0:T(8,128)(2,1)S(1)}, u32[]{:S(2)}, u32[]{:S(2)}) collective-permute-start(bf16[192,768]{1,0:T(8,128)(2,1)S(1)} %collective-permute-done.6.refs_1_), channel_id=1, source_target_pairs={{0,1},{1,3},{3,2},{2,0},{4,5},{5,7},{7,6},{6,4},{8,9},{9,11},{11,1... | collective-permute-start | bytes 884744 | tf_op jit(solution)/shard_map/part_0_lab_hop_2/ppermute | solution.py:195
  50.8 2.1 %collective-permute-start.13 = (bf16[192,768]{1,0:T(8,128)(2,1)S(1)}, bf16[192,768]{1,0:T(8,128)(2,1)S(1)}, u32[]{:S(2)}, u32[]{:S(2)}) collective-permute-start(bf16[192,768]{1,0:T(8,128)(2,1)S(1)} %collective-permute-done.11.refs_1_), channel_id=1, source_target_pairs={{0,1},{1,3},{3,2},{2,0},{4,5},{5,7},{7,6},{6,4},{8,9},{9,11},{11,1... | collective-permute-start | bytes 884744 | tf_op jit(solution)/shard_map/part_1_lab_hop_2/ppermute | solution.py:195
  53.1 1.9 %collective-permute-start.14 = (bf16[144,768]{1,0:T(8,128)(2,1)S(1)}, bf16[144,768]{1,0:T(8,128)(2,1)S(1)}, u32[]{:S(2)}, u32[]{:S(2)}) collective-permute-start(bf16[144,768]{1,0:T(8,128)(2,1)S(1)} %get-tuple-element.44), channel_id=1, source_target_pairs={{0,24},{4,28},{8,0},{12,4},{16,8},{20,12},{24,16},{28,20},{1,25},{... | collective-permute-start | bytes 663560 | tf_op jit(solution)/shard_map/upper_doc_shift_2/ppermute | solution.py:195
  55.0 3.4 %collective-permute-done.16.refs_2_ = bf16[192,768]{1,0:T(8,128)(2,1)S(1)} collective-permute-done((bf16[192,768]{1,0:T(8,128)(2,1)S(1)}, bf16[192,768]{1,0:T(8,128)(2,1)S(1)}, u32[]{:S(2)}, u32[]{:S(2)}) %collective-permute-start.16) | collective-permute-done | bytes 294944 | tf_op jit(solution)/shard_map/part_0_lab_hop_2/ppermute | solution.py:195
  59.3 1.3 %collective-permute-done.14.panel_ref = bf16[144,768]{1,0:T(8,128)(2,1)S(1)} collective-permute-done((bf16[144,768]{1,0:T(8,128)(2,1)S(1)}, bf16[144,768]{1,0:T(8,128)(2,1)S(1)}, u32[]{:S(2)}, u32[]{:S(2)}) %collective-permute-start.14) | collective-permute-done | bytes 221216 | tf_op jit(solution)/shard_map/upper_doc_shift_2/ppermute | solution.py:195
  60.6 4.1 %collective-permute-done.13.refs_2_ = bf16[192,768]{1,0:T(8,128)(2,1)S(1)} collective-permute-done((bf16[192,768]{1,0:T(8,128)(2,1)S(1)}, bf16[192,768]{1,0:T(8,128)(2,1)S(1)}, u32[]{:S(2)}, u32[]{:S(2)}) %collective-permute-start.13) | collective-permute-done | bytes 294944 | tf_op jit(solution)/shard_map/part_1_lab_hop_2/ppermute | solution.py:195
  65.7 5.3 %collective-permute-done.17.refs_3_ = bf16[192,768]{1,0:T(8,128)(2,1)S(1)} collective-permute-done((bf16[192,768]{1,0:T(8,128)(2,1)S(1)}, bf16[192,768]{1,0:T(8,128)(2,1)S(1)}, u32[]{:S(2)}, u32[]{:S(2)}) %collective-permute-start.17) | collective-permute-done | bytes 294944 | tf_op jit(solution)/shard_map/part_0_lab_hop_3/ppermute | solution.py:195
  71.1 1.6 %update_block.4 = (f32[256,768]{1,0:T(8,128)S(1)}, f32[256,768]{1,0:T(8,128)S(1)}) custom-call(bf16[144,768]{1,0:T(8,128)(2,1)S(1)} %get-tuple-element.47.panel_ref, bf16[192,768]{1,0:T(8,128)(2,1)S(1)} %constant_dynamic-update-slice_fusion.refs_0_, bf16[192,768]{1,0:T(8,128)(2,1)S(1)} %collective-permute-done.6.refs_1_, ...), custom_call_target="tpu_custom_call" | custom-call | flops 805306368 | bytes 3932160 | tf_op jit(solution)/shard_map/update_block/pallas_call | solution.py:172
  72.7 1.7 %update_block.5 = (f32[256,768]{1,0:T(8,128)S(1)}, f32[256,768]{1,0:T(8,128)S(1)}) custom-call(bf16[144,768]{1,0:T(8,128)(2,1)S(1)} %collective-permute-done.12.panel_ref, bf16[192,768]{1,0:T(8,128)(2,1)S(1)} %constant_dynamic-update-slice_fusion.refs_0_, bf16[192,768]{1,0:T(8,128)(2,1)S(1)} %collective-permute-done.6.refs_1_, ...), custom_call_target="tpu_custom_call" | custom-call | flops 805306368 | bytes 3932160 | tf_op jit(solution)/shard_map/update_block/pallas_call | solution.py:172
  74.4 1.6 %collective-permute-done.15.refs_3_ = bf16[192,768]{1,0:T(8,128)(2,1)S(1)} collective-permute-done((bf16[192,768]{1,0:T(8,128)(2,1)S(1)}, bf16[192,768]{1,0:T(8,128)(2,1)S(1)}, u32[]{:S(2)}, u32[]{:S(2)}) %collective-permute-start.15) | collective-permute-done | bytes 294944 | tf_op jit(solution)/shard_map/part_1_lab_hop_3/ppermute | solution.py:195
  76.0 1.7 %update_block.6 = (f32[256,768]{1,0:T(8,128)S(1)}, f32[256,768]{1,0:T(8,128)S(1)}) custom-call(bf16[144,768]{1,0:T(8,128)(2,1)S(1)} %collective-permute-done.14.panel_ref, bf16[192,768]{1,0:T(8,128)(2,1)S(1)} %constant_dynamic-update-slice_fusion.2.refs_0_, bf16[192,768]{1,0:T(8,128)(2,1)S(1)} %collective-permute-done.11.refs_1_, ...), custom_call_target="tpu_custom_call" | custom-call | flops 805306368 | bytes 3932160 | tf_op jit(solution)/shard_map/update_block/pallas_call | solution.py:172
  77.7 2.6 %update_block.7 = (f32[256,768]{1,0:T(8,128)}, f32[256,768]{1,0:T(8,128)}) custom-call(bf16[144,768]{1,0:T(8,128)(2,1)S(1)} %collective-permute-done.10.panel_ref, bf16[192,768]{1,0:T(8,128)(2,1)S(1)} %constant_dynamic-update-slice_fusion.2.refs_0_, bf16[192,768]{1,0:T(8,128)(2,1)S(1)} %collective-permute-done.11.refs_1_, ...), custom_call_target="tpu_custom_call" | custom-call | flops 805306368 | bytes 3932160 | tf_op jit(solution)/shard_map/update_block/pallas_call | solution.py:172
  (58 shorter events, 12.9 us)
Async XLA Ops:
  0.6 52.3 %copy-start = (s32[4,32,4]{1,2,0:T(4,128)S(1)}, s32[4,32,4]{1,2,0:T(4,128)}, u32[]{:S(2)}) copy-start(s32[4,32,4]{1,2,0:T(4,128)} %param.13) | copy-start | bytes 6148
  1.8 11.7 %collective-permute-start = (bf16[96,768]{1,0:T(8,128)(2,1)S(1)}, bf16[96,768]{1,0:T(8,128)(2,1)S(1)}, u32[]{:S(2)}, u32[]{:S(2)}) collective-permute-start(bf16[96,768]{1,0:T(8,128)(2,1)S(1)} %get-tuple-element.29), channel_id=1, source_target_pairs={{0,1},{1,2},{2,3},{3,0},{4,5},{5,6},{6,7},{7,4},{8,9},{9,10},{10,1... | collective-permute-start | bytes 442376 | tf_op jit(solution)/shard_map/lower_lab_shift_1/ppermute | solution.py:195
  4.9 12.3 %collective-permute-start.1 = (bf16[96,768]{1,0:T(8,128)(2,1)S(1)}, bf16[96,768]{1,0:T(8,128)(2,1)S(1)}, u32[]{:S(2)}, u32[]{:S(2)}) collective-permute-start(bf16[96,768]{1,0:T(8,128)(2,1)S(1)} %get-tuple-element.30), channel_id=1, source_target_pairs={{0,2},{1,3},{2,0},{3,1},{4,6},{5,7},{6,4},{7,5},{8,10},{9,11},{10,... | collective-permute-start | bytes 442376 | tf_op jit(solution)/shard_map/lower_lab_shift_2/ppermute | solution.py:195
  7.5 1.4 %copy-start.3 = (s32[512,16]{0,1:T(8,128)S(1)}, s32[512,16]{0,1:T(8,128)}, u32[]{:S(2)}) copy-start(s32[512,16]{0,1:T(8,128)} %param.9) | copy-start | bytes 98308
  7.5 1.4 %slice-start = ((bf16[512,768]{1,0:T(8,128)(2,1)}), bf16[128,768]{1,0:T(8,128)(2,1)S(1)}, s32[]{:S(2)}) async-start(bf16[512,768]{1,0:T(8,128)(2,1)} %source.1), calls=%async_computation | async-start | bytes 393216 | tf_op jit(solution)/shard_map/slice | solution.py:214
  7.5 9.7 %collective-permute-start.2 = (bf16[96,768]{1,0:T(8,128)(2,1)S(1)}, bf16[96,768]{1,0:T(8,128)(2,1)S(1)}, u32[]{:S(2)}, u32[]{:S(2)}) collective-permute-start(bf16[96,768]{1,0:T(8,128)(2,1)S(1)} %get-tuple-element.31), channel_id=1, source_target_pairs={{0,3},{1,0},{2,1},{3,2},{4,7},{5,4},{6,5},{7,6},{8,11},{9,8},{10,9... | collective-permute-start | bytes 442376 | tf_op jit(solution)/shard_map/lower_lab_shift_3/ppermute | solution.py:195
  8.9 16.1 %collective-permute-start.7 = (bf16[144,768]{1,0:T(8,128)(2,1)S(1)}, bf16[144,768]{1,0:T(8,128)(2,1)S(1)}, u32[]{:S(2)}, u32[]{:S(2)}) collective-permute-start(bf16[144,768]{1,0:T(8,128)(2,1)S(1)} %fusion.2.refs_0_), channel_id=1, source_target_pairs={{0,1},{1,3},{3,2},{2,0},{4,5},{5,7},{7,6},{6,4},{8,9},{9,11},{11,1... | collective-permute-start | bytes 663560 | tf_op jit(solution)/shard_map/upper_lab_hop_1/ppermute | solution.py:195
  9.7 0.7 copy-start.4
  17.4 7.7 %collective-permute-start.3 = (bf16[96,768]{1,0:T(8,128)(2,1)S(1)}, bf16[96,768]{1,0:T(8,128)(2,1)S(1)}, u32[]{:S(2)}, u32[]{:S(2)}) collective-permute-start(bf16[96,768]{1,0:T(8,128)(2,1)S(1)} %get-tuple-element.33), channel_id=1, source_target_pairs={{0,28},{4,0},{8,4},{12,8},{16,12},{20,16},{24,20},{28,24},{1,29},{... | collective-permute-start | bytes 442376 | tf_op jit(solution)/shard_map/lower_doc_shift_1/ppermute | solution.py:195
  20.1 6.8 %collective-permute-start.4 = (bf16[96,768]{1,0:T(8,128)(2,1)S(1)}, bf16[96,768]{1,0:T(8,128)(2,1)S(1)}, u32[]{:S(2)}, u32[]{:S(2)}) collective-permute-start(bf16[96,768]{1,0:T(8,128)(2,1)S(1)} %get-tuple-element.34), channel_id=1, source_target_pairs={{0,24},{4,28},{8,0},{12,4},{16,8},{20,12},{24,16},{28,20},{1,25},{... | collective-permute-start | bytes 442376 | tf_op jit(solution)/shard_map/lower_doc_shift_2/ppermute | solution.py:195
  20.7 6.2 %collective-permute-start.5 = (bf16[96,768]{1,0:T(8,128)(2,1)S(1)}, bf16[96,768]{1,0:T(8,128)(2,1)S(1)}, u32[]{:S(2)}, u32[]{:S(2)}) collective-permute-start(bf16[96,768]{1,0:T(8,128)(2,1)S(1)} %get-tuple-element.35), channel_id=1, source_target_pairs={{0,20},{4,24},{8,28},{12,0},{16,4},{20,8},{24,12},{28,16},{1,21},{... | collective-permute-start | bytes 442376 | tf_op jit(solution)/shard_map/lower_doc_shift_3/ppermute | solution.py:195
  25.1 9.2 %collective-permute-start.8 = (bf16[144,768]{1,0:T(8,128)(2,1)S(1)}, bf16[144,768]{1,0:T(8,128)(2,1)S(1)}, u32[]{:S(2)}, u32[]{:S(2)}) collective-permute-start(bf16[144,768]{1,0:T(8,128)(2,1)S(1)} %collective-permute-done.7.refs_1_), channel_id=1, source_target_pairs={{0,1},{1,3},{3,2},{2,0},{4,5},{5,7},{7,6},{6,4},{8,9},{9,11},{11,1... | collective-permute-start | bytes 663560 | tf_op jit(solution)/shard_map/upper_lab_hop_2/ppermute | solution.py:195
  25.1 45.9 %copy-start.1 = (f32[256,768]{1,0:T(8,128)S(1)}, f32[256,768]{1,0:T(8,128)}, u32[]{:S(2)}) copy-start(f32[256,768]{1,0:T(8,128)} %refs_6_.1) | copy-start | bytes 2359300
  26.9 13.7 %collective-permute-start.6 = (bf16[192,768]{1,0:T(8,128)(2,1)S(1)}, bf16[192,768]{1,0:T(8,128)(2,1)S(1)}, u32[]{:S(2)}, u32[]{:S(2)}) collective-permute-start(bf16[192,768]{1,0:T(8,128)(2,1)S(1)} %constant_dynamic-update-slice_fusion.refs_0_), channel_id=1, source_target_pairs={{0,1},{1,3},{3,2},{2,0},{4,5},{5,7},{7,6},{6,4},{8,9},{9,11},{11,1... | collective-permute-start | bytes 884744 | tf_op jit(solution)/shard_map/part_0_lab_hop_1/ppermute | solution.py:195
  34.3 11.1 %collective-permute-start.9 = (bf16[144,768]{1,0:T(8,128)(2,1)S(1)}, bf16[144,768]{1,0:T(8,128)(2,1)S(1)}, u32[]{:S(2)}, u32[]{:S(2)}) collective-permute-start(bf16[144,768]{1,0:T(8,128)(2,1)S(1)} %collective-permute-done.8.refs_2_), channel_id=1, source_target_pairs={{0,1},{1,3},{3,2},{2,0},{4,5},{5,7},{7,6},{6,4},{8,9},{9,11},{11,1... | collective-permute-start | bytes 663560 | tf_op jit(solution)/shard_map/upper_lab_hop_3/ppermute | solution.py:195
  34.3 16.5 %collective-permute-start.11 = (bf16[192,768]{1,0:T(8,128)(2,1)S(1)}, bf16[192,768]{1,0:T(8,128)(2,1)S(1)}, u32[]{:S(2)}, u32[]{:S(2)}) collective-permute-start(bf16[192,768]{1,0:T(8,128)(2,1)S(1)} %constant_dynamic-update-slice_fusion.2.refs_0_), channel_id=1, source_target_pairs={{0,1},{1,3},{3,2},{2,0},{4,5},{5,7},{7,6},{6,4},{8,9},{9,11},{11,1... | collective-permute-start | bytes 884744 | tf_op jit(solution)/shard_map/part_1_lab_hop_1/ppermute | solution.py:195
  45.6 5.2 %collective-permute-start.12 = (bf16[144,768]{1,0:T(8,128)(2,1)S(1)}, bf16[144,768]{1,0:T(8,128)(2,1)S(1)}, u32[]{:S(2)}, u32[]{:S(2)}) collective-permute-start(bf16[144,768]{1,0:T(8,128)(2,1)S(1)} %get-tuple-element.42), channel_id=1, source_target_pairs={{0,28},{4,0},{8,4},{12,8},{16,12},{20,16},{24,20},{28,24},{1,29},{... | collective-permute-start | bytes 663560 | tf_op jit(solution)/shard_map/upper_doc_shift_1/ppermute | solution.py:195
  46.7 0.7 copy-start.5
  47.5 10.9 %collective-permute-start.16 = (bf16[192,768]{1,0:T(8,128)(2,1)S(1)}, bf16[192,768]{1,0:T(8,128)(2,1)S(1)}, u32[]{:S(2)}, u32[]{:S(2)}) collective-permute-start(bf16[192,768]{1,0:T(8,128)(2,1)S(1)} %collective-permute-done.6.refs_1_), channel_id=1, source_target_pairs={{0,1},{1,3},{3,2},{2,0},{4,5},{5,7},{7,6},{6,4},{8,9},{9,11},{11,1... | collective-permute-start | bytes 884744 | tf_op jit(solution)/shard_map/part_0_lab_hop_2/ppermute | solution.py:195
  50.8 13.9 %collective-permute-start.13 = (bf16[192,768]{1,0:T(8,128)(2,1)S(1)}, bf16[192,768]{1,0:T(8,128)(2,1)S(1)}, u32[]{:S(2)}, u32[]{:S(2)}) collective-permute-start(bf16[192,768]{1,0:T(8,128)(2,1)S(1)} %collective-permute-done.11.refs_1_), channel_id=1, source_target_pairs={{0,1},{1,3},{3,2},{2,0},{4,5},{5,7},{7,6},{6,4},{8,9},{9,11},{11,1... | collective-permute-start | bytes 884744 | tf_op jit(solution)/shard_map/part_1_lab_hop_2/ppermute | solution.py:195
  53.1 7.5 %collective-permute-start.14 = (bf16[144,768]{1,0:T(8,128)(2,1)S(1)}, bf16[144,768]{1,0:T(8,128)(2,1)S(1)}, u32[]{:S(2)}, u32[]{:S(2)}) collective-permute-start(bf16[144,768]{1,0:T(8,128)(2,1)S(1)} %get-tuple-element.44), channel_id=1, source_target_pairs={{0,24},{4,28},{8,0},{12,4},{16,8},{20,12},{24,16},{28,20},{1,25},{... | collective-permute-start | bytes 663560 | tf_op jit(solution)/shard_map/upper_doc_shift_2/ppermute | solution.py:195
  58.4 12.6 %collective-permute-start.17 = (bf16[192,768]{1,0:T(8,128)(2,1)S(1)}, bf16[192,768]{1,0:T(8,128)(2,1)S(1)}, u32[]{:S(2)}, u32[]{:S(2)}) collective-permute-start(bf16[192,768]{1,0:T(8,128)(2,1)S(1)} %collective-permute-done.16.refs_2_), channel_id=1, source_target_pairs={{0,1},{1,3},{3,2},{2,0},{4,5},{5,7},{7,6},{6,4},{8,9},{9,11},{11,1... | collective-permute-start | bytes 884744 | tf_op jit(solution)/shard_map/part_0_lab_hop_3/ppermute | solution.py:195
  64.7 11.2 %collective-permute-start.15 = (bf16[192,768]{1,0:T(8,128)(2,1)S(1)}, bf16[192,768]{1,0:T(8,128)(2,1)S(1)}, u32[]{:S(2)}, u32[]{:S(2)}) collective-permute-start(bf16[192,768]{1,0:T(8,128)(2,1)S(1)} %collective-permute-done.13.refs_2_), channel_id=1, source_target_pairs={{0,1},{1,3},{3,2},{2,0},{4,5},{5,7},{7,6},{6,4},{8,9},{9,11},{11,1... | collective-permute-start | bytes 884744 | tf_op jit(solution)/shard_map/part_1_lab_hop_3/ppermute | solution.py:195
  65.7 12.0 %collective-permute-start.10 = (bf16[144,768]{1,0:T(8,128)(2,1)S(1)}, bf16[144,768]{1,0:T(8,128)(2,1)S(1)}, u32[]{:S(2)}, u32[]{:S(2)}) collective-permute-start(bf16[144,768]{1,0:T(8,128)(2,1)S(1)} %get-tuple-element.41), channel_id=1, source_target_pairs={{0,20},{4,24},{8,28},{12,0},{16,4},{20,8},{24,12},{28,16},{1,21},{... | collective-permute-start | bytes 663560 | tf_op jit(solution)/shard_map/upper_doc_shift_3/ppermute | solution.py:195
  (1 other events, 0.7 us)

commit v5 on v4

--- a/solution.py
+++ b/solution.py
@@ -10,7 +10,7 @@
 TILE = 128
 STEPS = 4
 POS = 16
-LOWER = 6
+LOWER = 5
 GROUPS = ((0, 1), (2, 3))
 LANES = 128
 COLUMNS = 256
@@ -262,16 +262,13 @@
         part = parts[g]
         part.append(send(f"part_{g}_lab_hop_{len(part)}", part[-1], "lab", around, *earlier))
 
-    spread(0, *lower)
+    spread(0, *lower[1:])
     found = select(which_upper, [after(held[0], parts[0][1]), *held[1:]])
     found = [found[0]] + [shift("upper", s, found[s]) for s in range(1, STEPS)]
     spread(1)
     for r in range(2, lab_count):
-        if r == 2:
-            spread(0)
-        else:
-            spread(0, found[min(r - 2, STEPS - 1)])
-        spread(1, found[min(r - 1, STEPS - 1)])
+        spread(0)
+        spread(1, found[0 if r == 2 else 2])
 
     weight, moment = weights, None
     for s in range(STEPS):

time: 80.5 us -> 78.3 us (0.973)
  starting transfers between devices: 25.3 us -> 19.9 us
  waiting for transfers between devices: 38.9 us -> 43.5 us
  local copies, waits for them, and re-layouts: 4.67 us -> 3.3 us
    ppermute x18, starting transfers between devices: 25.3 us -> 19.9 us  [send(): return lax.ppermute(value, axis, pairs)]
    ppermute x18, waiting for transfers between devices: 38.9 us -> 43.5 us  [send(): return lax.ppermute(value, axis, pairs)]
    unnamed x14, local copies, waits for them, and re-layouts: 2.05 us -> 0.69 us
  transfers between devices with their start and end apart: 18 -> 18, of which waited for: 12 -> 10; matrix products, arithmetic and copies ran while one was open for 5% -> 5% of each run, Pallas kernels for 7% -> 7%
where the time goes in v5:
time: 78.3 us; the launch traced here: 78.1 us
  waiting for transfers between devices  43.5 us (56%)
  starting transfers between devices  19.9 us (25%)
  Pallas kernels  9.21 us (12%)
  local copies, waits for them, and re-layouts  3.3 us (4%)
  other arithmetic  1.43 us (2%)
  between operations  0.83 us (1%)
    ppermute x18, waiting for transfers between devices, send(): return lax.ppermute(value, axis, pairs)  43.5 us
    ppermute x18, starting transfers between devices, send(): return lax.ppermute(value, axis, pairs)  19.9 us
    pallas_call x4, Pallas kernels, update(): pl.pallas_call(functools.partial(update_kernel, first, last, len(pieces),...  7.57 us
  transfers between devices with their start and end apart: 18, of which 10 were waited for; matrix products, arithmetic and copies ran while one was open for 5% of the time, Pallas kernels for 7%

profile of v5, /device:TPU:0, one launch (start us, length us, event | category | flops | bytes accessed | tf_op | source)
XLA Modules:
  0.0 78.1 jit_solution(3303996950450303917)
XLA Ops:
  0.6 1.1 %pack_pieces.1 = (bf16[80,768]{1,0:T(8,128)(2,1)S(1)}, bf16[80,768]{1,0:T(8,128)(2,1)S(1)}, bf16[80,768]{1,0:T(8,128)(2,1)S(1)}, bf16[80,768]{1,0:T(8,128)(2,1)S(1)}) custom-call(bf16[512,768]{1,0:T(8,128)(2,1)} %source.1), custom_call_target="tpu_custom_call" | custom-call | tf_op jit(solution)/shard_map/pack_pieces/pallas_call | solution.py:74
  1.8 3.1 %collective-permute-start = (bf16[80,768]{1,0:T(8,128)(2,1)S(1)}, bf16[80,768]{1,0:T(8,128)(2,1)S(1)}, u32[]{:S(2)}, u32[]{:S(2)}) collective-permute-start(bf16[80,768]{1,0:T(8,128)(2,1)S(1)} %get-tuple-element.28), channel_id=1, source_target_pairs={{0,1},{1,2},{2,3},{3,0},{4,5},{5,6},{6,7},{7,4},{8,9},{9,10},{10,1... | collective-permute-start | bytes 368648 | tf_op jit(solution)/shard_map/lower_lab_shift_1/ppermute | solution.py:195
  4.9 2.6 %collective-permute-start.1 = (bf16[80,768]{1,0:T(8,128)(2,1)S(1)}, bf16[80,768]{1,0:T(8,128)(2,1)S(1)}, u32[]{:S(2)}, u32[]{:S(2)}) collective-permute-start(bf16[80,768]{1,0:T(8,128)(2,1)S(1)} %get-tuple-element.29), channel_id=1, source_target_pairs={{0,2},{1,3},{2,0},{3,1},{4,6},{5,7},{6,4},{7,5},{8,10},{9,11},{10,... | collective-permute-start | bytes 368648 | tf_op jit(solution)/shard_map/lower_lab_shift_2/ppermute | solution.py:195
  7.5 1.3 %collective-permute-start.2 = (bf16[80,768]{1,0:T(8,128)(2,1)S(1)}, bf16[80,768]{1,0:T(8,128)(2,1)S(1)}, u32[]{:S(2)}, u32[]{:S(2)}) collective-permute-start(bf16[80,768]{1,0:T(8,128)(2,1)S(1)} %get-tuple-element.30), channel_id=1, source_target_pairs={{0,3},{1,0},{2,1},{3,2},{4,7},{5,4},{6,5},{7,6},{8,11},{9,8},{10,9... | collective-permute-start | bytes 368648 | tf_op jit(solution)/shard_map/lower_lab_shift_3/ppermute | solution.py:195
  9.6 0.8 dynamic_slice.25
  12.8 2.8 %collective-permute-done.1.refs_2_ = bf16[80,768]{1,0:T(8,128)(2,1)S(1)} collective-permute-done((bf16[80,768]{1,0:T(8,128)(2,1)S(1)}, bf16[80,768]{1,0:T(8,128)(2,1)S(1)}, u32[]{:S(2)}, u32[]{:S(2)}) %collective-permute-start.1) | collective-permute-done | bytes 122912 | tf_op jit(solution)/shard_map/lower_lab_shift_2/ppermute | solution.py:195
  15.8 2.0 %collective-permute-start.3 = (bf16[80,768]{1,0:T(8,128)(2,1)S(1)}, bf16[80,768]{1,0:T(8,128)(2,1)S(1)}, u32[]{:S(2)}, u32[]{:S(2)}) collective-permute-start(bf16[80,768]{1,0:T(8,128)(2,1)S(1)} %get-tuple-element.32), channel_id=1, source_target_pairs={{0,28},{4,0},{8,4},{12,8},{16,12},{20,16},{24,20},{28,24},{1,29},{... | collective-permute-start | bytes 368648 | tf_op jit(solution)/shard_map/lower_doc_shift_1/ppermute | solution.py:195
  19.3 5.6 %collective-permute-done.7.refs_1_ = bf16[208,768]{1,0:T(8,128)(2,1)S(1)} collective-permute-done((bf16[208,768]{1,0:T(8,128)(2,1)S(1)}, bf16[208,768]{1,0:T(8,128)(2,1)S(1)}, u32[]{:S(2)}, u32[]{:S(2)}) %collective-permute-start.7) | collective-permute-done | bytes 319520 | tf_op jit(solution)/shard_map/upper_lab_hop_1/ppermute | solution.py:195
  25.1 2.8 %collective-permute-start.6 = (bf16[160,768]{1,0:T(8,128)(2,1)S(1)}, bf16[160,768]{1,0:T(8,128)(2,1)S(1)}, u32[]{:S(2)}, u32[]{:S(2)}) collective-permute-start(bf16[160,768]{1,0:T(8,128)(2,1)S(1)} %constant_dynamic-update-slice_fusion.refs_0_), channel_id=1, source_target_pairs={{0,1},{1,3},{3,2},{2,0},{4,5},{5,7},{7,6},{6,4},{8,9},{9,11},{11,1... | collective-permute-start | bytes 737288 | tf_op jit(solution)/shard_map/part_0_lab_hop_1/ppermute | solution.py:195
  27.9 8.4 %collective-permute-done.8.refs_2_ = bf16[208,768]{1,0:T(8,128)(2,1)S(1)} collective-permute-done((bf16[208,768]{1,0:T(8,128)(2,1)S(1)}, bf16[208,768]{1,0:T(8,128)(2,1)S(1)}, u32[]{:S(2)}, u32[]{:S(2)}) %collective-permute-start.8) | collective-permute-done | bytes 319520 | tf_op jit(solution)/shard_map/upper_lab_hop_2/ppermute | solution.py:195
  36.3 2.3 %collective-permute-start.11 = (bf16[160,768]{1,0:T(8,128)(2,1)S(1)}, bf16[160,768]{1,0:T(8,128)(2,1)S(1)}, u32[]{:S(2)}, u32[]{:S(2)}) collective-permute-start(bf16[160,768]{1,0:T(8,128)(2,1)S(1)} %constant_dynamic-update-slice_fusion.2.refs_0_), channel_id=1, source_target_pairs={{0,1},{1,3},{3,2},{2,0},{4,5},{5,7},{7,6},{6,4},{8,9},{9,11},{11,1... | collective-permute-start | bytes 737288 | tf_op jit(solution)/shard_map/part_1_lab_hop_1/ppermute | solution.py:195
  38.8 2.7 %collective-permute-done.6.refs_1_ = bf16[160,768]{1,0:T(8,128)(2,1)S(1)} collective-permute-done((bf16[160,768]{1,0:T(8,128)(2,1)S(1)}, bf16[160,768]{1,0:T(8,128)(2,1)S(1)}, u32[]{:S(2)}, u32[]{:S(2)}) %collective-permute-start.6) | collective-permute-done | bytes 245792 | tf_op jit(solution)/shard_map/part_0_lab_hop_1/ppermute | solution.py:195
  41.7 6.8 %collective-permute-done.9.refs_3_ = bf16[208,768]{1,0:T(8,128)(2,1)S(1)} collective-permute-done((bf16[208,768]{1,0:T(8,128)(2,1)S(1)}, bf16[208,768]{1,0:T(8,128)(2,1)S(1)}, u32[]{:S(2)}, u32[]{:S(2)}) %collective-permute-start.9) | collective-permute-done | bytes 319520 | tf_op jit(solution)/shard_map/upper_lab_hop_3/ppermute | solution.py:195
  48.8 4.9 %collective-permute-done.11.refs_1_ = bf16[160,768]{1,0:T(8,128)(2,1)S(1)} collective-permute-done((bf16[160,768]{1,0:T(8,128)(2,1)S(1)}, bf16[160,768]{1,0:T(8,128)(2,1)S(1)}, u32[]{:S(2)}, u32[]{:S(2)}) %collective-permute-start.11) | collective-permute-done | bytes 245792 | tf_op jit(solution)/shard_map/part_1_lab_hop_1/ppermute | solution.py:195
  53.7 2.4 %collective-permute-start.13 = (bf16[208,768]{1,0:T(8,128)(2,1)S(1)}, bf16[208,768]{1,0:T(8,128)(2,1)S(1)}, u32[]{:S(2)}, u32[]{:S(2)}) collective-permute-start(bf16[208,768]{1,0:T(8,128)(2,1)S(1)} %get-tuple-element.43), channel_id=1, source_target_pairs={{0,24},{4,28},{8,0},{12,4},{16,8},{20,12},{24,16},{28,20},{1,25},{... | collective-permute-start | bytes 958472 | tf_op jit(solution)/shard_map/upper_doc_shift_2/ppermute | solution.py:195
  56.4 2.6 %collective-permute-done.16.refs_2_ = bf16[160,768]{1,0:T(8,128)(2,1)S(1)} collective-permute-done((bf16[160,768]{1,0:T(8,128)(2,1)S(1)}, bf16[160,768]{1,0:T(8,128)(2,1)S(1)}, u32[]{:S(2)}, u32[]{:S(2)}) %collective-permute-start.16) | collective-permute-done | bytes 245792 | tf_op jit(solution)/shard_map/part_0_lab_hop_2/ppermute | solution.py:195
  59.4 1.4 %collective-permute-start.10 = (bf16[208,768]{1,0:T(8,128)(2,1)S(1)}, bf16[208,768]{1,0:T(8,128)(2,1)S(1)}, u32[]{:S(2)}, u32[]{:S(2)}) collective-permute-start(bf16[208,768]{1,0:T(8,128)(2,1)S(1)} %get-tuple-element.40), channel_id=1, source_target_pairs={{0,20},{4,24},{8,28},{12,0},{16,4},{20,8},{24,12},{28,16},{1,21},{... | collective-permute-start | bytes 958472 | tf_op jit(solution)/shard_map/upper_doc_shift_3/ppermute | solution.py:195
  60.8 3.4 %collective-permute-done.12.refs_2_ = bf16[160,768]{1,0:T(8,128)(2,1)S(1)} collective-permute-done((bf16[160,768]{1,0:T(8,128)(2,1)S(1)}, bf16[160,768]{1,0:T(8,128)(2,1)S(1)}, u32[]{:S(2)}, u32[]{:S(2)}) %collective-permute-start.12) | collective-permute-done | bytes 245792 | tf_op jit(solution)/shard_map/part_1_lab_hop_2/ppermute | solution.py:195
  64.3 5.2 %collective-permute-done.17.refs_3_ = bf16[160,768]{1,0:T(8,128)(2,1)S(1)} collective-permute-done((bf16[160,768]{1,0:T(8,128)(2,1)S(1)}, bf16[160,768]{1,0:T(8,128)(2,1)S(1)}, u32[]{:S(2)}, u32[]{:S(2)}) %collective-permute-start.17) | collective-permute-done | bytes 245792 | tf_op jit(solution)/shard_map/part_0_lab_hop_3/ppermute | solution.py:195
  69.5 1.6 %update_block.4 = (f32[256,768]{1,0:T(8,128)S(1)}, f32[256,768]{1,0:T(8,128)S(1)}) custom-call(bf16[208,768]{1,0:T(8,128)(2,1)S(1)} %get-tuple-element.41.panel_ref, bf16[160,768]{1,0:T(8,128)(2,1)S(1)} %constant_dynamic-update-slice_fusion.refs_0_, bf16[160,768]{1,0:T(8,128)(2,1)S(1)} %collective-permute-done.6.refs_1_, ...), custom_call_target="tpu_custom_call" | custom-call | flops 805306368 | bytes 3932160 | tf_op jit(solution)/shard_map/update_block/pallas_call | solution.py:172
  71.1 1.7 %update_block.5 = (f32[256,768]{1,0:T(8,128)S(1)}, f32[256,768]{1,0:T(8,128)S(1)}) custom-call(bf16[208,768]{1,0:T(8,128)(2,1)S(1)} %collective-permute-done.15.panel_ref, bf16[160,768]{1,0:T(8,128)(2,1)S(1)} %constant_dynamic-update-slice_fusion.refs_0_, bf16[160,768]{1,0:T(8,128)(2,1)S(1)} %collective-permute-done.6.refs_1_, ...), custom_call_target="tpu_custom_call" | custom-call | flops 805306368 | bytes 3932160 | tf_op jit(solution)/shard_map/update_block/pallas_call | solution.py:172
  72.8 1.0 %collective-permute-done.14.refs_3_ = bf16[160,768]{1,0:T(8,128)(2,1)S(1)} collective-permute-done((bf16[160,768]{1,0:T(8,128)(2,1)S(1)}, bf16[160,768]{1,0:T(8,128)(2,1)S(1)}, u32[]{:S(2)}, u32[]{:S(2)}) %collective-permute-start.14) | collective-permute-done | bytes 245792 | tf_op jit(solution)/shard_map/part_1_lab_hop_3/ppermute | solution.py:195
  73.8 1.7 %update_block.6 = (f32[256,768]{1,0:T(8,128)S(1)}, f32[256,768]{1,0:T(8,128)S(1)}) custom-call(bf16[208,768]{1,0:T(8,128)(2,1)S(1)} %collective-permute-done.13.panel_ref, bf16[160,768]{1,0:T(8,128)(2,1)S(1)} %constant_dynamic-update-slice_fusion.2.refs_0_, bf16[160,768]{1,0:T(8,128)(2,1)S(1)} %collective-permute-done.11.refs_1_, ...), custom_call_target="tpu_custom_call" | custom-call | flops 805306368 | bytes 3932160 | tf_op jit(solution)/shard_map/update_block/pallas_call | solution.py:172
  75.5 2.6 %update_block.7 = (f32[256,768]{1,0:T(8,128)}, f32[256,768]{1,0:T(8,128)}) custom-call(bf16[208,768]{1,0:T(8,128)(2,1)S(1)} %collective-permute-done.10.panel_ref, bf16[160,768]{1,0:T(8,128)(2,1)S(1)} %constant_dynamic-update-slice_fusion.2.refs_0_, bf16[160,768]{1,0:T(8,128)(2,1)S(1)} %collective-permute-done.11.refs_1_, ...), custom_call_target="tpu_custom_call" | custom-call | flops 805306368 | bytes 3932160 | tf_op jit(solution)/shard_map/update_block/pallas_call | solution.py:172
  (58 shorter events, 6.4 us)
Async XLA Ops:
  0.6 55.5 %copy-start = (s32[4,32,4]{1,2,0:T(4,128)S(1)}, s32[4,32,4]{1,2,0:T(4,128)}, u32[]{:S(2)}) copy-start(s32[4,32,4]{1,2,0:T(4,128)} %param.13) | copy-start | bytes 6148
  1.8 11.0 %collective-permute-start = (bf16[80,768]{1,0:T(8,128)(2,1)S(1)}, bf16[80,768]{1,0:T(8,128)(2,1)S(1)}, u32[]{:S(2)}, u32[]{:S(2)}) collective-permute-start(bf16[80,768]{1,0:T(8,128)(2,1)S(1)} %get-tuple-element.28), channel_id=1, source_target_pairs={{0,1},{1,2},{2,3},{3,0},{4,5},{5,6},{6,7},{7,4},{8,9},{9,10},{10,1... | collective-permute-start | bytes 368648 | tf_op jit(solution)/shard_map/lower_lab_shift_1/ppermute | solution.py:195
  4.9 10.7 %collective-permute-start.1 = (bf16[80,768]{1,0:T(8,128)(2,1)S(1)}, bf16[80,768]{1,0:T(8,128)(2,1)S(1)}, u32[]{:S(2)}, u32[]{:S(2)}) collective-permute-start(bf16[80,768]{1,0:T(8,128)(2,1)S(1)} %get-tuple-element.29), channel_id=1, source_target_pairs={{0,2},{1,3},{2,0},{3,1},{4,6},{5,7},{6,4},{7,5},{8,10},{9,11},{10,... | collective-permute-start | bytes 368648 | tf_op jit(solution)/shard_map/lower_lab_shift_2/ppermute | solution.py:195
  7.4 1.4 %copy-start.3 = (s32[512,16]{0,1:T(8,128)S(1)}, s32[512,16]{0,1:T(8,128)}, u32[]{:S(2)}) copy-start(s32[512,16]{0,1:T(8,128)} %param.9) | copy-start | bytes 98308
  7.4 1.4 %slice-start = ((bf16[512,768]{1,0:T(8,128)(2,1)}), bf16[192,768]{1,0:T(8,128)(2,1)S(1)}, s32[]{:S(2)}) async-start(bf16[512,768]{1,0:T(8,128)(2,1)} %source.1), calls=%async_computation | async-start | bytes 589824 | tf_op jit(solution)/shard_map/slice | solution.py:214
  7.5 8.1 %collective-permute-start.2 = (bf16[80,768]{1,0:T(8,128)(2,1)S(1)}, bf16[80,768]{1,0:T(8,128)(2,1)S(1)}, u32[]{:S(2)}, u32[]{:S(2)}) collective-permute-start(bf16[80,768]{1,0:T(8,128)(2,1)S(1)} %get-tuple-element.30), channel_id=1, source_target_pairs={{0,3},{1,0},{2,1},{3,2},{4,7},{5,4},{6,5},{7,6},{8,11},{9,8},{10,9... | collective-permute-start | bytes 368648 | tf_op jit(solution)/shard_map/lower_lab_shift_3/ppermute | solution.py:195
  8.9 16.1 %collective-permute-start.7 = (bf16[208,768]{1,0:T(8,128)(2,1)S(1)}, bf16[208,768]{1,0:T(8,128)(2,1)S(1)}, u32[]{:S(2)}, u32[]{:S(2)}) collective-permute-start(bf16[208,768]{1,0:T(8,128)(2,1)S(1)} %fusion.1.refs_0_), channel_id=1, source_target_pairs={{0,1},{1,3},{3,2},{2,0},{4,5},{5,7},{7,6},{6,4},{8,9},{9,11},{11,1... | collective-permute-start | bytes 958472 | tf_op jit(solution)/shard_map/upper_lab_hop_1/ppermute | solution.py:195
  10.5 1.2 %copy-start.4 = (s32[4,8]{1,0:T(4,128)S(1)}, s32[4,8]{1,0:T(4,128)}, u32[]{:S(2)}) copy-start(s32[4,8]{1,0:T(4,128)} %param.12) | copy-start | bytes 388
  15.8 9.2 %collective-permute-start.3 = (bf16[80,768]{1,0:T(8,128)(2,1)S(1)}, bf16[80,768]{1,0:T(8,128)(2,1)S(1)}, u32[]{:S(2)}, u32[]{:S(2)}) collective-permute-start(bf16[80,768]{1,0:T(8,128)(2,1)S(1)} %get-tuple-element.32), channel_id=1, source_target_pairs={{0,28},{4,0},{8,4},{12,8},{16,12},{20,16},{24,20},{28,24},{1,29},{... | collective-permute-start | bytes 368648 | tf_op jit(solution)/shard_map/lower_doc_shift_1/ppermute | solution.py:195
  18.5 6.6 %collective-permute-start.4 = (bf16[80,768]{1,0:T(8,128)(2,1)S(1)}, bf16[80,768]{1,0:T(8,128)(2,1)S(1)}, u32[]{:S(2)}, u32[]{:S(2)}) collective-permute-start(bf16[80,768]{1,0:T(8,128)(2,1)S(1)} %get-tuple-element.33), channel_id=1, source_target_pairs={{0,24},{4,28},{8,0},{12,4},{16,8},{20,12},{24,16},{28,20},{1,25},{... | collective-permute-start | bytes 368648 | tf_op jit(solution)/shard_map/lower_doc_shift_2/ppermute | solution.py:195
  19.1 6.0 %collective-permute-start.5 = (bf16[80,768]{1,0:T(8,128)(2,1)S(1)}, bf16[80,768]{1,0:T(8,128)(2,1)S(1)}, u32[]{:S(2)}, u32[]{:S(2)}) collective-permute-start(bf16[80,768]{1,0:T(8,128)(2,1)S(1)} %get-tuple-element.34), channel_id=1, source_target_pairs={{0,20},{4,24},{8,28},{12,0},{16,4},{20,8},{24,12},{28,16},{1,21},{... | collective-permute-start | bytes 368648 | tf_op jit(solution)/shard_map/lower_doc_shift_3/ppermute | solution.py:195
  25.0 11.3 %collective-permute-start.8 = (bf16[208,768]{1,0:T(8,128)(2,1)S(1)}, bf16[208,768]{1,0:T(8,128)(2,1)S(1)}, u32[]{:S(2)}, u32[]{:S(2)}) collective-permute-start(bf16[208,768]{1,0:T(8,128)(2,1)S(1)} %collective-permute-done.7.refs_1_), channel_id=1, source_target_pairs={{0,1},{1,3},{3,2},{2,0},{4,5},{5,7},{7,6},{6,4},{8,9},{9,11},{11,1... | collective-permute-start | bytes 958472 | tf_op jit(solution)/shard_map/upper_lab_hop_2/ppermute | solution.py:195
  25.1 16.5 %collective-permute-start.6 = (bf16[160,768]{1,0:T(8,128)(2,1)S(1)}, bf16[160,768]{1,0:T(8,128)(2,1)S(1)}, u32[]{:S(2)}, u32[]{:S(2)}) collective-permute-start(bf16[160,768]{1,0:T(8,128)(2,1)S(1)} %constant_dynamic-update-slice_fusion.refs_0_), channel_id=1, source_target_pairs={{0,1},{1,3},{3,2},{2,0},{4,5},{5,7},{7,6},{6,4},{8,9},{9,11},{11,1... | collective-permute-start | bytes 737288 | tf_op jit(solution)/shard_map/part_0_lab_hop_1/ppermute | solution.py:195
  27.9 10.8 %copy-start.5 = (s32[4,32]{1,0:T(4,128)S(1)}, s32[4,32]{1,0:T(4,128)}, u32[]{:S(2)}) copy-start(s32[4,32]{1,0:T(4,128)} %param.14) | copy-start | bytes 1540
  27.9 41.6 %copy-start.1 = (f32[256,768]{1,0:T(8,128)S(1)}, f32[256,768]{1,0:T(8,128)}, u32[]{:S(2)}) copy-start(f32[256,768]{1,0:T(8,128)} %refs_6_.1) | copy-start | bytes 2359300
  36.3 12.1 %collective-permute-start.9 = (bf16[208,768]{1,0:T(8,128)(2,1)S(1)}, bf16[208,768]{1,0:T(8,128)(2,1)S(1)}, u32[]{:S(2)}, u32[]{:S(2)}) collective-permute-start(bf16[208,768]{1,0:T(8,128)(2,1)S(1)} %collective-permute-done.8.refs_2_), channel_id=1, source_target_pairs={{0,1},{1,3},{3,2},{2,0},{4,5},{5,7},{7,6},{6,4},{8,9},{9,11},{11,1... | collective-permute-start | bytes 958472 | tf_op jit(solution)/shard_map/upper_lab_hop_3/ppermute | solution.py:195
  36.3 17.4 %collective-permute-start.11 = (bf16[160,768]{1,0:T(8,128)(2,1)S(1)}, bf16[160,768]{1,0:T(8,128)(2,1)S(1)}, u32[]{:S(2)}, u32[]{:S(2)}) collective-permute-start(bf16[160,768]{1,0:T(8,128)(2,1)S(1)} %constant_dynamic-update-slice_fusion.2.refs_0_), channel_id=1, source_target_pairs={{0,1},{1,3},{3,2},{2,0},{4,5},{5,7},{7,6},{6,4},{8,9},{9,11},{11,1... | collective-permute-start | bytes 737288 | tf_op jit(solution)/shard_map/part_1_lab_hop_1/ppermute | solution.py:195
  41.6 17.4 %collective-permute-start.16 = (bf16[160,768]{1,0:T(8,128)(2,1)S(1)}, bf16[160,768]{1,0:T(8,128)(2,1)S(1)}, u32[]{:S(2)}, u32[]{:S(2)}) collective-permute-start(bf16[160,768]{1,0:T(8,128)(2,1)S(1)} %collective-permute-done.6.refs_1_), channel_id=1, source_target_pairs={{0,1},{1,3},{3,2},{2,0},{4,5},{5,7},{7,6},{6,4},{8,9},{9,11},{11,1... | collective-permute-start | bytes 737288 | tf_op jit(solution)/shard_map/part_0_lab_hop_2/ppermute | solution.py:195
  53.7 10.5 %collective-permute-start.12 = (bf16[160,768]{1,0:T(8,128)(2,1)S(1)}, bf16[160,768]{1,0:T(8,128)(2,1)S(1)}, u32[]{:S(2)}, u32[]{:S(2)}) collective-permute-start(bf16[160,768]{1,0:T(8,128)(2,1)S(1)} %collective-permute-done.11.refs_1_), channel_id=1, source_target_pairs={{0,1},{1,3},{3,2},{2,0},{4,5},{5,7},{7,6},{6,4},{8,9},{9,11},{11,1... | collective-permute-start | bytes 737288 | tf_op jit(solution)/shard_map/part_1_lab_hop_2/ppermute | solution.py:195
  53.7 10.5 %collective-permute-start.13 = (bf16[208,768]{1,0:T(8,128)(2,1)S(1)}, bf16[208,768]{1,0:T(8,128)(2,1)S(1)}, u32[]{:S(2)}, u32[]{:S(2)}) collective-permute-start(bf16[208,768]{1,0:T(8,128)(2,1)S(1)} %get-tuple-element.43), channel_id=1, source_target_pairs={{0,24},{4,28},{8,0},{12,4},{16,8},{20,12},{24,16},{28,20},{1,25},{... | collective-permute-start | bytes 958472 | tf_op jit(solution)/shard_map/upper_doc_shift_2/ppermute | solution.py:195
  59.0 10.5 %collective-permute-start.17 = (bf16[160,768]{1,0:T(8,128)(2,1)S(1)}, bf16[160,768]{1,0:T(8,128)(2,1)S(1)}, u32[]{:S(2)}, u32[]{:S(2)}) collective-permute-start(bf16[160,768]{1,0:T(8,128)(2,1)S(1)} %collective-permute-done.16.refs_2_), channel_id=1, source_target_pairs={{0,1},{1,3},{3,2},{2,0},{4,5},{5,7},{7,6},{6,4},{8,9},{9,11},{11,1... | collective-permute-start | bytes 737288 | tf_op jit(solution)/shard_map/part_0_lab_hop_3/ppermute | solution.py:195
  59.0 12.2 %collective-permute-start.15 = (bf16[208,768]{1,0:T(8,128)(2,1)S(1)}, bf16[208,768]{1,0:T(8,128)(2,1)S(1)}, u32[]{:S(2)}, u32[]{:S(2)}) collective-permute-start(bf16[208,768]{1,0:T(8,128)(2,1)S(1)} %get-tuple-element.45), channel_id=1, source_target_pairs={{0,28},{4,0},{8,4},{12,8},{16,12},{20,16},{24,20},{28,24},{1,29},{... | collective-permute-start | bytes 958472 | tf_op jit(solution)/shard_map/upper_doc_shift_1/ppermute | solution.py:195
  59.4 16.1 %collective-permute-start.10 = (bf16[208,768]{1,0:T(8,128)(2,1)S(1)}, bf16[208,768]{1,0:T(8,128)(2,1)S(1)}, u32[]{:S(2)}, u32[]{:S(2)}) collective-permute-start(bf16[208,768]{1,0:T(8,128)(2,1)S(1)} %get-tuple-element.40), channel_id=1, source_target_pairs={{0,20},{4,24},{8,28},{12,0},{16,4},{20,8},{24,12},{28,16},{1,21},{... | collective-permute-start | bytes 958472 | tf_op jit(solution)/shard_map/upper_doc_shift_3/ppermute | solution.py:195
  64.2 9.6 %collective-permute-start.14 = (bf16[160,768]{1,0:T(8,128)(2,1)S(1)}, bf16[160,768]{1,0:T(8,128)(2,1)S(1)}, u32[]{:S(2)}, u32[]{:S(2)}) collective-permute-start(bf16[160,768]{1,0:T(8,128)(2,1)S(1)} %collective-permute-done.12.refs_2_), channel_id=1, source_target_pairs={{0,1},{1,3},{3,2},{2,0},{4,5},{5,7},{7,6},{6,4},{8,9},{9,11},{11,1... | collective-permute-start | bytes 737288 | tf_op jit(solution)/shard_map/part_1_lab_hop_3/ppermute | solution.py:195
  (1 other events, 0.7 us)

commit v6 on v5

--- a/solution.py
+++ b/solution.py
@@ -10,7 +10,7 @@
 TILE = 128
 STEPS = 4
 POS = 16
-LOWER = 5
+LOWER = 4
 GROUPS = ((0, 1), (2, 3))
 LANES = 128
 COLUMNS = 256
@@ -101,17 +101,21 @@
     return dot(pair[1], other) + dot(pair[0], other)
 
 
-def update_kernel(first, last, n, top, size, offset, scale, panel_ref, *refs):
+def update_kernel(first, last, n, tops, size, offset, scale, *refs):
     order = circle(n)
     lab = lax.axis_index("lab")
     place = sum(jnp.where(lab == i, order.index(i), 0) for i in range(n))
+    panels, refs = refs[: len(tops)], refs[len(tops) :]
     pieces, refs = refs[:n], refs[n:]
     live_ref, pick_ref, weight_ref, *refs = refs
     moment_ref = None if first else refs.pop(0)
     weight_out, moment_out, rows_ref, *refs = refs
     labels = weight_ref.shape[0]
     count = rows_ref.shape[0]
-    rows_ref[:top, :] = panel_ref[:top, :]
+    top = 0
+    for panel_ref, rows in zip(panels, tops):
+        rows_ref[top : top + rows, :] = panel_ref[:rows, :]
+        top += rows
     for k, piece in enumerate(pieces):
         at = lax.rem(place + n - k, n)
         plane = sum(jnp.where(at == i, order[i], 0) for i in range(n))
@@ -129,7 +133,7 @@
     label = jnp.concatenate([label] * (count // LANES), axis=1)
     target = jnp.zeros(label.shape, jnp.bfloat16)
     for k in range(POS):
-        code = panel_ref[top + k : top + k + 1, :count]
+        code = panels[0][tops[0] + k : tops[0] + k + 1, :count]
         target = jnp.where(label == code, jnp.bfloat16(1.0), target)
     scores = product(pair, rows, ((1,), (1,))) * scale
     resid = (jax.nn.sigmoid(scores) - target.astype(jnp.float32)) * live_ref[:, :count]
@@ -156,23 +160,24 @@
         copy.wait()
 
 
-def update(panel, pieces, offset, live, pick, weight, moment, last):
+def update(panels, pieces, offset, live, pick, weight, moment, last):
     labels, width = weight.shape
     count = live.shape[1] - LANES
-    top = panel.shape[0] - POS
-    size = (count - top) // len(pieces)
+    tops = [panel.shape[0] for panel in panels]
+    tops[0] -= POS
+    size = (count - sum(tops)) // len(pieces)
     first = moment is None
     state = [weight] if first else [weight, moment]
     shape = (jax.ShapeDtypeStruct if last else pltpu.VMEM)(weight.shape, jnp.float32)
-    scratch = [pltpu.VMEM((count, width), panel.dtype)]
+    scratch = [pltpu.VMEM((count, width), panels[0].dtype)]
     if last:
         scratch += [pltpu.VMEM(weight.shape, jnp.float32)] * 2
         scratch += [pltpu.SemaphoreType.DMA((2 * width // COLUMNS,))]
     scale = 1.0 / float(width) ** 0.5
     return pl.pallas_call(
-        functools.partial(update_kernel, first, last, len(pieces), top, size, offset, scale),
+        functools.partial(update_kernel, first, last, len(pieces), tops, size, offset, scale),
         out_shape=[shape, shape],
-        in_specs=[VMEM] * (len(pieces) + 3 + len(state)),
+        in_specs=[VMEM] * (len(panels) + len(pieces) + 2 + len(state)),
         out_specs=[HBM if last else VMEM] * 2,
         scratch_shapes=scratch,
         compiler_params=pltpu.CompilerParams(vmem_limit_bytes=UPDATE_MIB * MIB),
@@ -182,7 +187,7 @@
             transcendentals=labels * count,
         ),
         name="update_block",
-    )(panel, *pieces, live, pick, *state)
+    )(*panels, *pieces, live, pick, *state)
 
 
 def after(value, *earlier):
@@ -211,7 +216,8 @@
 
     codes = coded(positives.T >> 7, positives.T & 127).astype(jnp.bfloat16)
     codes = jnp.pad(codes, ((0, 0), (0, width - rows)))
-    upper = jnp.concatenate([embeddings[:top], codes], axis=0)
+    first = top // 32 * 16
+    upper = [jnp.concatenate([embeddings[:first], codes], axis=0), embeddings[first:top]]
 
     order = circle(lab_count)
     place_of = jnp.array([order.index(i) for i in range(lab_count)], jnp.int32)
@@ -245,35 +251,38 @@
     for k in range(1, lab_count):
         pairs = [(i, (i + k) % lab_count) for i in range(lab_count)]
         met.append(send(f"lower_lab_shift_{k}", mine[k], "lab", pairs))
-    held = [upper]
-
-    def hop(*earlier):
-        held.append(send(f"upper_lab_hop_{len(held)}", held[-1], "lab", around, *earlier))
-
-    hop(mine[0])
+    held = [[chunk] for chunk in upper]
+
+    def hop(what, line, *earlier):
+        line.append(send(f"{what}_lab_hop_{len(line)}", line[-1], "lab", around, *earlier))
+
+    hop("upper_0", held[0], mine[0])
+    hop("upper_1", held[1], mine[0])
     lower = select(which_lower, met)
-    hop(*prepared, lower[0])
+    hop("upper_0", held[0], *prepared, lower[0])
     lower = [lower[0]] + [shift("lower", s, lower[s]) for s in range(1, STEPS)]
+    parts = [[jnp.concatenate([lower[s] for s in steps], axis=0)] for steps in GROUPS]
+    hop("upper_1", held[1], held[0][2])
     for r in range(3, lab_count):
-        hop(*lower[1:])
-    parts = [[jnp.concatenate([lower[s] for s in steps], axis=0)] for steps in GROUPS]
-
-    def spread(g, *earlier):
-        part = parts[g]
-        part.append(send(f"part_{g}_lab_hop_{len(part)}", part[-1], "lab", around, *earlier))
-
-    spread(0, *lower[1:])
-    found = select(which_upper, [after(held[0], parts[0][1]), *held[1:]])
-    found = [found[0]] + [shift("upper", s, found[s]) for s in range(1, STEPS)]
-    spread(1)
+        hop("upper_0", held[0], *lower[1:])
+    hop("part_0", parts[0], *lower[1:])
+    ahead = select(which_upper, held[0])
+    panels = [[ahead[0]]] + [[shift("upper_0", s, ahead[s])] for s in range(1, STEPS)]
+    for r in range(3, lab_count):
+        hop("upper_1", held[1], ahead[0])
+    hop("part_1", parts[1])
+    found = select(which_upper, held[1])
+    panels[0].append(found[0])
+    for s in range(1, STEPS):
+        panels[s].append(shift("upper_1", s, found[s], panels[s][0]))
     for r in range(2, lab_count):
-        spread(0)
-        spread(1, found[0 if r == 2 else 2])
+        hop("part_0", parts[0], *(panels[2][:1] if r > 2 else ()))
+        hop("part_1", parts[1], panels[1 if r == 2 else 2][0])
 
     weight, moment = weights, None
     for s in range(STEPS):
         weight, moment = update(
-            found[s],
+            panels[s],
             parts[s in GROUPS[1]],
             (s - GROUPS[s in GROUPS[1]][0]) * size,
             live[s : s + 1],

time: 78.3 us -> 73.5 us (0.939); the launches traced: 78.1 us -> 72.4 us
  waiting for transfers between devices: 43.5 us -> 30.8 us
  starting transfers between devices: 19.9 us -> 25.4 us
  local copies, waits for them, and re-layouts: 3.3 us -> 4.68 us
    ppermute x18 -> x24, waiting for transfers between devices: 43.5 us -> 30.8 us  [send(): return lax.ppermute(value, axis, pairs)]
    ppermute x18 -> x24, starting transfers between devices: 19.9 us -> 25.4 us  [send(): return lax.ppermute(value, axis, pairs)]
    unnamed x14 -> x16, local copies, waits for them, and re-layouts: 0.69 us -> 2.04 us
  transfers between devices with their start and end apart: 18 -> 24, of which waited for: 10 -> 11; matrix products, arithmetic and copies ran while one was open for 5% -> 6% of each run, Pallas kernels for 7% -> 8%
where the time goes in v6:
time: 73.5 us; the launch traced here: 72.4 us
  waiting for transfers between devices  30.8 us (42%)
  starting transfers between devices  25.4 us (35%)
  Pallas kernels  9.19 us (13%)
  local copies, waits for them, and re-layouts  4.68 us (6%)
  other arithmetic  1.42 us (2%)
  between operations  0.93 us (1%)
    ppermute x24, waiting for transfers between devices, send(): return lax.ppermute(value, axis, pairs)  30.8 us
    ppermute x24, starting transfers between devices, send(): return lax.ppermute(value, axis, pairs)  25.4 us
    pallas_call x4, Pallas kernels, update(): pl.pallas_call(functools.partial(update_kernel, first, last, len(pieces),...  7.39 us
    unnamed x16, local copies, waits for them, and re-layouts  2.04 us
  transfers between devices with their start and end apart: 24, of which 11 were waited for; matrix products, arithmetic and copies ran while one was open for 6% of the time, Pallas kernels for 8%

profile of v6, /device:TPU:0, one launch (start us, length us, event | category | flops | bytes accessed | tf_op | source)
XLA Modules:
  0.0 72.4 jit_solution(10316176103053199964)
XLA Ops:
  0.7 1.2 %pack_pieces.1 = (bf16[64,768]{1,0:T(8,128)(2,1)S(1)}, bf16[64,768]{1,0:T(8,128)(2,1)S(1)}, bf16[64,768]{1,0:T(8,128)(2,1)S(1)}, bf16[64,768]{1,0:T(8,128)(2,1)S(1)}) custom-call(bf16[512,768]{1,0:T(8,128)(2,1)} %source.1), custom_call_target="tpu_custom_call" | custom-call | tf_op jit(solution)/shard_map/pack_pieces/pallas_call | solution.py:74
  1.8 3.1 %collective-permute-start.1 = (bf16[64,768]{1,0:T(8,128)(2,1)S(1)}, bf16[64,768]{1,0:T(8,128)(2,1)S(1)}, u32[]{:S(2)}, u32[]{:S(2)}) collective-permute-start(bf16[64,768]{1,0:T(8,128)(2,1)S(1)} %get-tuple-element.39), channel_id=1, source_target_pairs={{0,1},{1,2},{2,3},{3,0},{4,5},{5,6},{6,7},{7,4},{8,9},{9,10},{10,1... | collective-permute-start | bytes 294920 | tf_op jit(solution)/shard_map/lower_lab_shift_1/ppermute | solution.py:200
  4.9 2.6 %collective-permute-start.2 = (bf16[64,768]{1,0:T(8,128)(2,1)S(1)}, bf16[64,768]{1,0:T(8,128)(2,1)S(1)}, u32[]{:S(2)}, u32[]{:S(2)}) collective-permute-start(bf16[64,768]{1,0:T(8,128)(2,1)S(1)} %get-tuple-element.40), channel_id=1, source_target_pairs={{0,2},{1,3},{2,0},{3,1},{4,6},{5,7},{6,4},{7,5},{8,10},{9,11},{10,... | collective-permute-start | bytes 294920 | tf_op jit(solution)/shard_map/lower_lab_shift_2/ppermute | solution.py:200
  7.5 1.3 %collective-permute-start.3 = (bf16[64,768]{1,0:T(8,128)(2,1)S(1)}, bf16[64,768]{1,0:T(8,128)(2,1)S(1)}, u32[]{:S(2)}, u32[]{:S(2)}) collective-permute-start(bf16[64,768]{1,0:T(8,128)(2,1)S(1)} %get-tuple-element.41), channel_id=1, source_target_pairs={{0,3},{1,0},{2,1},{3,2},{4,7},{5,4},{6,5},{7,6},{8,11},{9,8},{10,9... | collective-permute-start | bytes 294920 | tf_op jit(solution)/shard_map/lower_lab_shift_3/ppermute | solution.py:200
  15.9 0.8 %collective-permute-start.5 = (bf16[64,768]{1,0:T(8,128)(2,1)S(1)}, bf16[64,768]{1,0:T(8,128)(2,1)S(1)}, u32[]{:S(2)}, u32[]{:S(2)}) collective-permute-start(bf16[64,768]{1,0:T(8,128)(2,1)S(1)} %get-tuple-element.44), channel_id=1, source_target_pairs={{0,28},{4,0},{8,4},{12,8},{16,12},{20,16},{24,20},{28,24},{1,29},{... | collective-permute-start | bytes 294920 | tf_op jit(solution)/shard_map/lower_doc_shift_1/ppermute | solution.py:200
  16.7 1.7 %collective-permute-start.6 = (bf16[64,768]{1,0:T(8,128)(2,1)S(1)}, bf16[64,768]{1,0:T(8,128)(2,1)S(1)}, u32[]{:S(2)}, u32[]{:S(2)}) collective-permute-start(bf16[64,768]{1,0:T(8,128)(2,1)S(1)} %get-tuple-element.45), channel_id=1, source_target_pairs={{0,24},{4,28},{8,0},{12,4},{16,8},{20,12},{24,16},{28,20},{1,25},{... | collective-permute-start | bytes 294920 | tf_op jit(solution)/shard_map/lower_doc_shift_2/ppermute | solution.py:200
  18.7 2.2 %collective-permute-done.refs_1_ = bf16[144,768]{1,0:T(8,128)(2,1)S(1)} collective-permute-done((bf16[144,768]{1,0:T(8,128)(2,1)S(1)}, bf16[144,768]{1,0:T(8,128)(2,1)S(1)}, u32[]{:S(2)}, u32[]{:S(2)}) %collective-permute-start) | collective-permute-done | bytes 221216 | tf_op jit(solution)/shard_map/upper_0_lab_hop_1/ppermute | solution.py:200
  21.0 1.7 %collective-permute-done.6 = bf16[64,768]{1,0:T(8,128)(2,1)S(1)} collective-permute-done((bf16[64,768]{1,0:T(8,128)(2,1)S(1)}, bf16[64,768]{1,0:T(8,128)(2,1)S(1)}, u32[]{:S(2)}, u32[]{:S(2)}) %collective-permute-start.6) | collective-permute-done | bytes 98336 | tf_op jit(solution)/shard_map/lower_doc_shift_2/ppermute | solution.py:200
  23.2 1.5 %collective-permute-start.21 = (bf16[128,768]{1,0:T(8,128)(2,1)S(1)}, bf16[128,768]{1,0:T(8,128)(2,1)S(1)}, u32[]{:S(2)}, u32[]{:S(2)}) collective-permute-start(bf16[128,768]{1,0:T(8,128)(2,1)S(1)} %constant_dynamic-update-slice_fusion.2.refs_2_), channel_id=1, source_target_pairs={{0,1},{1,3},{3,2},{2,0},{4,5},{5,7},{7,6},{6,4},{8,9},{9,11},{11,1... | collective-permute-start | bytes 589832 | tf_op jit(solution)/shard_map/part_0_lab_hop_1/ppermute | solution.py:200
  24.6 5.6 %collective-permute-done.4.refs_2_ = bf16[144,768]{1,0:T(8,128)(2,1)S(1)} collective-permute-done((bf16[144,768]{1,0:T(8,128)(2,1)S(1)}, bf16[144,768]{1,0:T(8,128)(2,1)S(1)}, u32[]{:S(2)}, u32[]{:S(2)}) %collective-permute-start.4) | collective-permute-done | bytes 221216 | tf_op jit(solution)/shard_map/upper_0_lab_hop_2/ppermute | solution.py:200
  30.3 3.2 %collective-permute-start.14 = (bf16[128,768]{1,0:T(8,128)(2,1)S(1)}, bf16[128,768]{1,0:T(8,128)(2,1)S(1)}, u32[]{:S(2)}, u32[]{:S(2)}) collective-permute-start(bf16[128,768]{1,0:T(8,128)(2,1)S(1)} %constant_dynamic-update-slice_fusion.refs_2_), channel_id=1, source_target_pairs={{0,1},{1,3},{3,2},{2,0},{4,5},{5,7},{7,6},{6,4},{8,9},{9,11},{11,1... | collective-permute-start | bytes 589832 | tf_op jit(solution)/shard_map/part_1_lab_hop_1/ppermute | solution.py:200
  33.6 5.9 %collective-permute-done.8.refs_3_ = bf16[144,768]{1,0:T(8,128)(2,1)S(1)} collective-permute-done((bf16[144,768]{1,0:T(8,128)(2,1)S(1)}, bf16[144,768]{1,0:T(8,128)(2,1)S(1)}, u32[]{:S(2)}, u32[]{:S(2)}) %collective-permute-start.8) | collective-permute-done | bytes 221216 | tf_op jit(solution)/shard_map/upper_0_lab_hop_3/ppermute | solution.py:200
  40.8 1.9 %collective-permute-start.17 = (bf16[144,768]{1,0:T(8,128)(2,1)S(1)}, bf16[144,768]{1,0:T(8,128)(2,1)S(1)}, u32[]{:S(2)}, u32[]{:S(2)}) collective-permute-start(bf16[144,768]{1,0:T(8,128)(2,1)S(1)} %get-tuple-element.57), channel_id=1, source_target_pairs={{0,24},{4,28},{8,0},{12,4},{16,8},{20,12},{24,16},{28,20},{1,25},{... | collective-permute-start | bytes 663560 | tf_op jit(solution)/shard_map/upper_0_doc_shift_2/ppermute | solution.py:200
  42.7 5.2 %collective-permute-done.11.refs_2_ = bf16[128,768]{1,0:T(8,128)(2,1)S(1)} collective-permute-done((bf16[128,768]{1,0:T(8,128)(2,1)S(1)}, bf16[128,768]{1,0:T(8,128)(2,1)S(1)}, u32[]{:S(2)}, u32[]{:S(2)}) %collective-permute-start.11) | collective-permute-done | bytes 196640 | tf_op jit(solution)/shard_map/upper_1_lab_hop_2/ppermute | solution.py:200
  48.0 3.2 %collective-permute-start.16 = (bf16[128,768]{1,0:T(8,128)(2,1)S(1)}, bf16[128,768]{1,0:T(8,128)(2,1)S(1)}, u32[]{:S(2)}, u32[]{:S(2)}) collective-permute-start(bf16[128,768]{1,0:T(8,128)(2,1)S(1)} %collective-permute-done.14.refs_3_), channel_id=1, source_target_pairs={{0,1},{1,3},{3,2},{2,0},{4,5},{5,7},{7,6},{6,4},{8,9},{9,11},{11,1... | collective-permute-start | bytes 589832 | tf_op jit(solution)/shard_map/part_1_lab_hop_2/ppermute | solution.py:200
  51.4 5.3 %collective-permute-done.12.refs_3_ = bf16[128,768]{1,0:T(8,128)(2,1)S(1)} collective-permute-done((bf16[128,768]{1,0:T(8,128)(2,1)S(1)}, bf16[128,768]{1,0:T(8,128)(2,1)S(1)}, u32[]{:S(2)}, u32[]{:S(2)}) %collective-permute-start.12) | collective-permute-done | bytes 196640 | tf_op jit(solution)/shard_map/upper_1_lab_hop_3/ppermute | solution.py:200
  57.1 2.5 %collective-permute-start.19 = (bf16[128,768]{1,0:T(8,128)(2,1)S(1)}, bf16[128,768]{1,0:T(8,128)(2,1)S(1)}, u32[]{:S(2)}, u32[]{:S(2)}) collective-permute-start(bf16[128,768]{1,0:T(8,128)(2,1)S(1)} %get-tuple-element.60), channel_id=1, source_target_pairs={{0,24},{4,28},{8,0},{12,4},{16,8},{20,12},{24,16},{28,20},{1,25},{... | collective-permute-start | bytes 589832 | tf_op jit(solution)/shard_map/upper_1_doc_shift_2/ppermute | solution.py:200
  59.6 1.3 %collective-permute-done.16.refs_4_ = bf16[128,768]{1,0:T(8,128)(2,1)S(1)} collective-permute-done((bf16[128,768]{1,0:T(8,128)(2,1)S(1)}, bf16[128,768]{1,0:T(8,128)(2,1)S(1)}, u32[]{:S(2)}, u32[]{:S(2)}) %collective-permute-start.16) | collective-permute-done | bytes 196640 | tf_op jit(solution)/shard_map/part_1_lab_hop_2/ppermute | solution.py:200
  60.9 0.9 %collective-permute-start.18 = (bf16[128,768]{1,0:T(8,128)(2,1)S(1)}, bf16[128,768]{1,0:T(8,128)(2,1)S(1)}, u32[]{:S(2)}, u32[]{:S(2)}) collective-permute-start(bf16[128,768]{1,0:T(8,128)(2,1)S(1)} %collective-permute-done.16.refs_4_), channel_id=1, source_target_pairs={{0,1},{1,3},{3,2},{2,0},{4,5},{5,7},{7,6},{6,4},{8,9},{9,11},{11,1... | collective-permute-start | bytes 589832 | tf_op jit(solution)/shard_map/part_1_lab_hop_3/ppermute | solution.py:200
  61.9 2.4 %collective-permute-done.23.refs_5_ = bf16[128,768]{1,0:T(8,128)(2,1)S(1)} collective-permute-done((bf16[128,768]{1,0:T(8,128)(2,1)S(1)}, bf16[128,768]{1,0:T(8,128)(2,1)S(1)}, u32[]{:S(2)}, u32[]{:S(2)}) %collective-permute-start.23) | collective-permute-done | bytes 196640 | tf_op jit(solution)/shard_map/part_0_lab_hop_3/ppermute | solution.py:200
  64.4 1.6 %update_block.4 = (f32[256,768]{1,0:T(8,128)S(1)}, f32[256,768]{1,0:T(8,128)S(1)}) custom-call(bf16[144,768]{1,0:T(8,128)(2,1)S(1)} %get-tuple-element.51.refs_0_, bf16[128,768]{1,0:T(8,128)(2,1)S(1)} %get-tuple-element.65.refs_1_, bf16[128,768]{1,0:T(8,128)(2,1)S(1)} %constant_dynamic-update-slice_fusion.2.refs_2_, ...), custom_call_target="tpu_custom_call" | custom-call | flops 805306368 | bytes 3932160 | tf_op jit(solution)/shard_map/update_block/pallas_call | solution.py:177
  66.0 1.6 %update_block.5 = (f32[256,768]{1,0:T(8,128)S(1)}, f32[256,768]{1,0:T(8,128)S(1)}) custom-call(bf16[144,768]{1,0:T(8,128)(2,1)S(1)} %collective-permute-done.15.refs_0_, bf16[128,768]{1,0:T(8,128)(2,1)S(1)} %collective-permute-done.20.refs_1_, bf16[128,768]{1,0:T(8,128)(2,1)S(1)} %constant_dynamic-update-slice_fusion.2.refs_2_, ...), custom_call_target="tpu_custom_call" | custom-call | flops 805306368 | bytes 3932160 | tf_op jit(solution)/shard_map/update_block/pallas_call | solution.py:177
  68.2 1.6 %update_block.6 = (f32[256,768]{1,0:T(8,128)S(1)}, f32[256,768]{1,0:T(8,128)S(1)}) custom-call(bf16[144,768]{1,0:T(8,128)(2,1)S(1)} %collective-permute-done.17.refs_0_, bf16[128,768]{1,0:T(8,128)(2,1)S(1)} %collective-permute-done.19.refs_1_, bf16[128,768]{1,0:T(8,128)(2,1)S(1)} %constant_dynamic-update-slice_fusion.refs_2_, ...), custom_call_target="tpu_custom_call" | custom-call | flops 805306368 | bytes 3932160 | tf_op jit(solution)/shard_map/update_block/pallas_call | solution.py:177
  69.8 2.6 %update_block.7 = (f32[256,768]{1,0:T(8,128)}, f32[256,768]{1,0:T(8,128)}) custom-call(bf16[144,768]{1,0:T(8,128)(2,1)S(1)} %collective-permute-done.9.refs_0_, bf16[128,768]{1,0:T(8,128)(2,1)S(1)} %collective-permute-done.13.refs_1_, bf16[128,768]{1,0:T(8,128)(2,1)S(1)} %constant_dynamic-update-slice_fusion.refs_2_, ...), custom_call_target="tpu_custom_call" | custom-call | flops 805306368 | bytes 3932160 | tf_op jit(solution)/shard_map/update_block/pallas_call | solution.py:177
  (72 shorter events, 10.4 us)
Async XLA Ops:
  1.8 13.8 %collective-permute-start.1 = (bf16[64,768]{1,0:T(8,128)(2,1)S(1)}, bf16[64,768]{1,0:T(8,128)(2,1)S(1)}, u32[]{:S(2)}, u32[]{:S(2)}) collective-permute-start(bf16[64,768]{1,0:T(8,128)(2,1)S(1)} %get-tuple-element.39), channel_id=1, source_target_pairs={{0,1},{1,2},{2,3},{3,0},{4,5},{5,6},{6,7},{7,4},{8,9},{9,10},{10,1... | collective-permute-start | bytes 294920 | tf_op jit(solution)/shard_map/lower_lab_shift_1/ppermute | solution.py:200
  4.9 10.7 %collective-permute-start.2 = (bf16[64,768]{1,0:T(8,128)(2,1)S(1)}, bf16[64,768]{1,0:T(8,128)(2,1)S(1)}, u32[]{:S(2)}, u32[]{:S(2)}) collective-permute-start(bf16[64,768]{1,0:T(8,128)(2,1)S(1)} %get-tuple-element.40), channel_id=1, source_target_pairs={{0,2},{1,3},{2,0},{3,1},{4,6},{5,7},{6,4},{7,5},{8,10},{9,11},{10,... | collective-permute-start | bytes 294920 | tf_op jit(solution)/shard_map/lower_lab_shift_2/ppermute | solution.py:200
  7.5 8.2 %collective-permute-start.3 = (bf16[64,768]{1,0:T(8,128)(2,1)S(1)}, bf16[64,768]{1,0:T(8,128)(2,1)S(1)}, u32[]{:S(2)}, u32[]{:S(2)}) collective-permute-start(bf16[64,768]{1,0:T(8,128)(2,1)S(1)} %get-tuple-element.41), channel_id=1, source_target_pairs={{0,3},{1,0},{2,1},{3,2},{4,7},{5,4},{6,5},{7,6},{8,11},{9,8},{10,9... | collective-permute-start | bytes 294920 | tf_op jit(solution)/shard_map/lower_lab_shift_3/ppermute | solution.py:200
  9.0 12.0 %collective-permute-start = (bf16[144,768]{1,0:T(8,128)(2,1)S(1)}, bf16[144,768]{1,0:T(8,128)(2,1)S(1)}, u32[]{:S(2)}, u32[]{:S(2)}) collective-permute-start(bf16[144,768]{1,0:T(8,128)(2,1)S(1)} %fusion.2.refs_0_), channel_id=1, source_target_pairs={{0,1},{1,3},{3,2},{2,0},{4,5},{5,7},{7,6},{6,4},{8,9},{9,11},{11,1... | collective-permute-start | bytes 663560 | tf_op jit(solution)/shard_map/upper_0_lab_hop_1/ppermute | solution.py:200
  9.7 23.8 %collective-permute-start.10 = (bf16[128,768]{1,0:T(8,128)(2,1)S(1)}, bf16[128,768]{1,0:T(8,128)(2,1)S(1)}, u32[]{:S(2)}, u32[]{:S(2)}) collective-permute-start(bf16[128,768]{1,0:T(8,128)(2,1)S(1)} %get-tuple-element.49.refs_0_), channel_id=1, source_target_pairs={{0,1},{1,3},{3,2},{2,0},{4,5},{5,7},{7,6},{6,4},{8,9},{9,11},{11,1... | collective-permute-start | bytes 589832 | tf_op jit(solution)/shard_map/upper_1_lab_hop_1/ppermute | solution.py:200
  15.9 5.1 %collective-permute-start.5 = (bf16[64,768]{1,0:T(8,128)(2,1)S(1)}, bf16[64,768]{1,0:T(8,128)(2,1)S(1)}, u32[]{:S(2)}, u32[]{:S(2)}) collective-permute-start(bf16[64,768]{1,0:T(8,128)(2,1)S(1)} %get-tuple-element.44), channel_id=1, source_target_pairs={{0,28},{4,0},{8,4},{12,8},{16,12},{20,16},{24,20},{28,24},{1,29},{... | collective-permute-start | bytes 294920 | tf_op jit(solution)/shard_map/lower_doc_shift_1/ppermute | solution.py:200
  16.7 6.1 %collective-permute-start.6 = (bf16[64,768]{1,0:T(8,128)(2,1)S(1)}, bf16[64,768]{1,0:T(8,128)(2,1)S(1)}, u32[]{:S(2)}, u32[]{:S(2)}) collective-permute-start(bf16[64,768]{1,0:T(8,128)(2,1)S(1)} %get-tuple-element.45), channel_id=1, source_target_pairs={{0,24},{4,28},{8,0},{12,4},{16,8},{20,12},{24,16},{28,20},{1,25},{... | collective-permute-start | bytes 294920 | tf_op jit(solution)/shard_map/lower_doc_shift_2/ppermute | solution.py:200
  18.4 4.7 %collective-permute-start.7 = (bf16[64,768]{1,0:T(8,128)(2,1)S(1)}, bf16[64,768]{1,0:T(8,128)(2,1)S(1)}, u32[]{:S(2)}, u32[]{:S(2)}) collective-permute-start(bf16[64,768]{1,0:T(8,128)(2,1)S(1)} %get-tuple-element.46), channel_id=1, source_target_pairs={{0,20},{4,24},{8,28},{12,0},{16,4},{20,8},{24,12},{28,16},{1,21},{... | collective-permute-start | bytes 294920 | tf_op jit(solution)/shard_map/lower_doc_shift_3/ppermute | solution.py:200
  21.0 9.3 %collective-permute-start.4 = (bf16[144,768]{1,0:T(8,128)(2,1)S(1)}, bf16[144,768]{1,0:T(8,128)(2,1)S(1)}, u32[]{:S(2)}, u32[]{:S(2)}) collective-permute-start(bf16[144,768]{1,0:T(8,128)(2,1)S(1)} %collective-permute-done.refs_1_), channel_id=1, source_target_pairs={{0,1},{1,3},{3,2},{2,0},{4,5},{5,7},{7,6},{6,4},{8,9},{9,11},{11,1... | collective-permute-start | bytes 663560 | tf_op jit(solution)/shard_map/upper_0_lab_hop_2/ppermute | solution.py:200
  23.2 17.5 %collective-permute-start.21 = (bf16[128,768]{1,0:T(8,128)(2,1)S(1)}, bf16[128,768]{1,0:T(8,128)(2,1)S(1)}, u32[]{:S(2)}, u32[]{:S(2)}) collective-permute-start(bf16[128,768]{1,0:T(8,128)(2,1)S(1)} %constant_dynamic-update-slice_fusion.2.refs_2_), channel_id=1, source_target_pairs={{0,1},{1,3},{3,2},{2,0},{4,5},{5,7},{7,6},{6,4},{8,9},{9,11},{11,1... | collective-permute-start | bytes 589832 | tf_op jit(solution)/shard_map/part_0_lab_hop_1/ppermute | solution.py:200
  30.2 9.3 %collective-permute-start.8 = (bf16[144,768]{1,0:T(8,128)(2,1)S(1)}, bf16[144,768]{1,0:T(8,128)(2,1)S(1)}, u32[]{:S(2)}, u32[]{:S(2)}) collective-permute-start(bf16[144,768]{1,0:T(8,128)(2,1)S(1)} %collective-permute-done.4.refs_2_), channel_id=1, source_target_pairs={{0,1},{1,3},{3,2},{2,0},{4,5},{5,7},{7,6},{6,4},{8,9},{9,11},{11,1... | collective-permute-start | bytes 663560 | tf_op jit(solution)/shard_map/upper_0_lab_hop_3/ppermute | solution.py:200
  30.3 17.7 %collective-permute-start.14 = (bf16[128,768]{1,0:T(8,128)(2,1)S(1)}, bf16[128,768]{1,0:T(8,128)(2,1)S(1)}, u32[]{:S(2)}, u32[]{:S(2)}) collective-permute-start(bf16[128,768]{1,0:T(8,128)(2,1)S(1)} %constant_dynamic-update-slice_fusion.refs_2_), channel_id=1, source_target_pairs={{0,1},{1,3},{3,2},{2,0},{4,5},{5,7},{7,6},{6,4},{8,9},{9,11},{11,1... | collective-permute-start | bytes 589832 | tf_op jit(solution)/shard_map/part_1_lab_hop_1/ppermute | solution.py:200
  33.5 14.4 %collective-permute-start.11 = (bf16[128,768]{1,0:T(8,128)(2,1)S(1)}, bf16[128,768]{1,0:T(8,128)(2,1)S(1)}, u32[]{:S(2)}, u32[]{:S(2)}) collective-permute-start(bf16[128,768]{1,0:T(8,128)(2,1)S(1)} %collective-permute-done.10.refs_1_), channel_id=1, source_target_pairs={{0,1},{1,3},{3,2},{2,0},{4,5},{5,7},{7,6},{6,4},{8,9},{9,11},{11,1... | collective-permute-start | bytes 589832 | tf_op jit(solution)/shard_map/upper_1_lab_hop_2/ppermute | solution.py:200
  39.8 8.2 %collective-permute-start.15 = (bf16[144,768]{1,0:T(8,128)(2,1)S(1)}, bf16[144,768]{1,0:T(8,128)(2,1)S(1)}, u32[]{:S(2)}, u32[]{:S(2)}) collective-permute-start(bf16[144,768]{1,0:T(8,128)(2,1)S(1)} %get-tuple-element.55), channel_id=1, source_target_pairs={{0,28},{4,0},{8,4},{12,8},{16,12},{20,16},{24,20},{28,24},{1,29},{... | collective-permute-start | bytes 663560 | tf_op jit(solution)/shard_map/upper_0_doc_shift_1/ppermute | solution.py:200
  40.7 16.2 %collective-permute-start.22 = (bf16[128,768]{1,0:T(8,128)(2,1)S(1)}, bf16[128,768]{1,0:T(8,128)(2,1)S(1)}, u32[]{:S(2)}, u32[]{:S(2)}) collective-permute-start(bf16[128,768]{1,0:T(8,128)(2,1)S(1)} %collective-permute-done.21.refs_3_), channel_id=1, source_target_pairs={{0,1},{1,3},{3,2},{2,0},{4,5},{5,7},{7,6},{6,4},{8,9},{9,11},{11,1... | collective-permute-start | bytes 589832 | tf_op jit(solution)/shard_map/part_0_lab_hop_2/ppermute | solution.py:200
  40.8 16.2 %collective-permute-start.17 = (bf16[144,768]{1,0:T(8,128)(2,1)S(1)}, bf16[144,768]{1,0:T(8,128)(2,1)S(1)}, u32[]{:S(2)}, u32[]{:S(2)}) collective-permute-start(bf16[144,768]{1,0:T(8,128)(2,1)S(1)} %get-tuple-element.57), channel_id=1, source_target_pairs={{0,24},{4,28},{8,0},{12,4},{16,8},{20,12},{24,16},{28,20},{1,25},{... | collective-permute-start | bytes 663560 | tf_op jit(solution)/shard_map/upper_0_doc_shift_2/ppermute | solution.py:200
  47.9 8.7 %collective-permute-start.12 = (bf16[128,768]{1,0:T(8,128)(2,1)S(1)}, bf16[128,768]{1,0:T(8,128)(2,1)S(1)}, u32[]{:S(2)}, u32[]{:S(2)}) collective-permute-start(bf16[128,768]{1,0:T(8,128)(2,1)S(1)} %collective-permute-done.11.refs_2_), channel_id=1, source_target_pairs={{0,1},{1,3},{3,2},{2,0},{4,5},{5,7},{7,6},{6,4},{8,9},{9,11},{11,1... | collective-permute-start | bytes 589832 | tf_op jit(solution)/shard_map/upper_1_lab_hop_3/ppermute | solution.py:200
  48.0 12.9 %collective-permute-start.16 = (bf16[128,768]{1,0:T(8,128)(2,1)S(1)}, bf16[128,768]{1,0:T(8,128)(2,1)S(1)}, u32[]{:S(2)}, u32[]{:S(2)}) collective-permute-start(bf16[128,768]{1,0:T(8,128)(2,1)S(1)} %collective-permute-done.14.refs_3_), channel_id=1, source_target_pairs={{0,1},{1,3},{3,2},{2,0},{4,5},{5,7},{7,6},{6,4},{8,9},{9,11},{11,1... | collective-permute-start | bytes 589832 | tf_op jit(solution)/shard_map/part_1_lab_hop_2/ppermute | solution.py:200
  51.3 10.6 %collective-permute-start.9 = (bf16[144,768]{1,0:T(8,128)(2,1)S(1)}, bf16[144,768]{1,0:T(8,128)(2,1)S(1)}, u32[]{:S(2)}, u32[]{:S(2)}) collective-permute-start(bf16[144,768]{1,0:T(8,128)(2,1)S(1)} %get-tuple-element.48), channel_id=1, source_target_pairs={{0,20},{4,24},{8,28},{12,0},{16,4},{20,8},{24,12},{28,16},{1,21},{... | collective-permute-start | bytes 663560 | tf_op jit(solution)/shard_map/upper_0_doc_shift_3/ppermute | solution.py:200
  57.0 7.4 %collective-permute-start.23 = (bf16[128,768]{1,0:T(8,128)(2,1)S(1)}, bf16[128,768]{1,0:T(8,128)(2,1)S(1)}, u32[]{:S(2)}, u32[]{:S(2)}) collective-permute-start(bf16[128,768]{1,0:T(8,128)(2,1)S(1)} %collective-permute-done.22.refs_4_), channel_id=1, source_target_pairs={{0,1},{1,3},{3,2},{2,0},{4,5},{5,7},{7,6},{6,4},{8,9},{9,11},{11,1... | collective-permute-start | bytes 589832 | tf_op jit(solution)/shard_map/part_0_lab_hop_3/ppermute | solution.py:200
  57.0 9.0 %collective-permute-start.20 = (bf16[128,768]{1,0:T(8,128)(2,1)S(1)}, bf16[128,768]{1,0:T(8,128)(2,1)S(1)}, u32[]{:S(2)}, u32[]{:S(2)}) collective-permute-start(bf16[128,768]{1,0:T(8,128)(2,1)S(1)} %get-tuple-element.62), channel_id=1, source_target_pairs={{0,28},{4,0},{8,4},{12,8},{16,12},{20,16},{24,20},{28,24},{1,29},{... | collective-permute-start | bytes 589832 | tf_op jit(solution)/shard_map/upper_1_doc_shift_1/ppermute | solution.py:200
  57.1 10.8 %collective-permute-start.19 = (bf16[128,768]{1,0:T(8,128)(2,1)S(1)}, bf16[128,768]{1,0:T(8,128)(2,1)S(1)}, u32[]{:S(2)}, u32[]{:S(2)}) collective-permute-start(bf16[128,768]{1,0:T(8,128)(2,1)S(1)} %get-tuple-element.60), channel_id=1, source_target_pairs={{0,24},{4,28},{8,0},{12,4},{16,8},{20,12},{24,16},{28,20},{1,25},{... | collective-permute-start | bytes 589832 | tf_op jit(solution)/shard_map/upper_1_doc_shift_2/ppermute | solution.py:200
  60.9 7.3 %collective-permute-start.18 = (bf16[128,768]{1,0:T(8,128)(2,1)S(1)}, bf16[128,768]{1,0:T(8,128)(2,1)S(1)}, u32[]{:S(2)}, u32[]{:S(2)}) collective-permute-start(bf16[128,768]{1,0:T(8,128)(2,1)S(1)} %collective-permute-done.16.refs_4_), channel_id=1, source_target_pairs={{0,1},{1,3},{3,2},{2,0},{4,5},{5,7},{7,6},{6,4},{8,9},{9,11},{11,1... | collective-permute-start | bytes 589832 | tf_op jit(solution)/shard_map/part_1_lab_hop_3/ppermute | solution.py:200
  61.9 8.0 %collective-permute-start.13 = (bf16[128,768]{1,0:T(8,128)(2,1)S(1)}, bf16[128,768]{1,0:T(8,128)(2,1)S(1)}, u32[]{:S(2)}, u32[]{:S(2)}) collective-permute-start(bf16[128,768]{1,0:T(8,128)(2,1)S(1)} %get-tuple-element.54), channel_id=1, source_target_pairs={{0,20},{4,24},{8,28},{12,0},{16,4},{20,8},{24,12},{28,16},{1,21},{... | collective-permute-start | bytes 589832 | tf_op jit(solution)/shard_map/upper_1_doc_shift_3/ppermute | solution.py:200
  (7 other events, 85.6 us)

commit v7 on v6

--- a/solution.py
+++ b/solution.py
@@ -271,7 +271,7 @@
     for r in range(3, lab_count):
         hop("upper_1", held[1], ahead[0])
     hop("part_1", parts[1])
-    found = select(which_upper, held[1])
+    found = select(which_upper, [after(held[1][0], panels[2][0]), *held[1][1:]])
     panels[0].append(found[0])
     for s in range(1, STEPS):
         panels[s].append(shift("upper_1", s, found[s], panels[s][0]))

time: 73.5 us -> 72.8 us (level); the launches traced: 72.4 us -> 72.5 us
  waiting for transfers between devices: 30.8 us -> 31.9 us
  starting transfers between devices: 25.4 us -> 24.5 us
    ppermute x24, waiting for transfers between devices: 30.8 us -> 31.9 us  [send(): return lax.ppermute(value, axis, pairs)]
    ppermute x24, starting transfers between devices: 25.4 us -> 24.5 us  [send(): return lax.ppermute(value, axis, pairs)]
where the time goes in v7:
time: 72.8 us; the launch traced here: 72.5 us
  waiting for transfers between devices  31.9 us (44%)
  starting transfers between devices  24.5 us (34%)
  Pallas kernels  9.19 us (13%)
  local copies, waits for them, and re-layouts  4.68 us (6%)
  other arithmetic  1.42 us (2%)
  between operations  0.91 us (1%)
    ppermute x24, waiting for transfers between devices, send(): return lax.ppermute(value, axis, pairs)  31.9 us
    ppermute x24, starting transfers between devices, send(): return lax.ppermute(value, axis, pairs)  24.5 us
    pallas_call x4, Pallas kernels, update(): pl.pallas_call(functools.partial(update_kernel, first, last, len(pieces),...  7.39 us
    unnamed x16, local copies, waits for them, and re-layouts  2.04 us
  transfers between devices with their start and end apart: 24, of which 11 were waited for; matrix products, arithmetic and copies ran while one was open for 6% of the time, Pallas kernels for 8%

profile of v7, /device:TPU:0, one launch (start us, length us, event | category | flops | bytes accessed | tf_op | source)
XLA Modules:
  0.0 72.5 jit_solution(2053429169830583144)
XLA Ops:
  0.7 1.2 %pack_pieces.1 = (bf16[64,768]{1,0:T(8,128)(2,1)S(1)}, bf16[64,768]{1,0:T(8,128)(2,1)S(1)}, bf16[64,768]{1,0:T(8,128)(2,1)S(1)}, bf16[64,768]{1,0:T(8,128)(2,1)S(1)}) custom-call(bf16[512,768]{1,0:T(8,128)(2,1)} %source.1), custom_call_target="tpu_custom_call" | custom-call | tf_op jit(solution)/shard_map/pack_pieces/pallas_call | solution.py:74
  1.8 3.1 %collective-permute-start.1 = (bf16[64,768]{1,0:T(8,128)(2,1)S(1)}, bf16[64,768]{1,0:T(8,128)(2,1)S(1)}, u32[]{:S(2)}, u32[]{:S(2)}) collective-permute-start(bf16[64,768]{1,0:T(8,128)(2,1)S(1)} %get-tuple-element.40), channel_id=1, source_target_pairs={{0,1},{1,2},{2,3},{3,0},{4,5},{5,6},{6,7},{7,4},{8,9},{9,10},{10,1... | collective-permute-start | bytes 294920 | tf_op jit(solution)/shard_map/lower_lab_shift_1/ppermute | solution.py:200
  4.9 2.6 %collective-permute-start.2 = (bf16[64,768]{1,0:T(8,128)(2,1)S(1)}, bf16[64,768]{1,0:T(8,128)(2,1)S(1)}, u32[]{:S(2)}, u32[]{:S(2)}) collective-permute-start(bf16[64,768]{1,0:T(8,128)(2,1)S(1)} %get-tuple-element.41), channel_id=1, source_target_pairs={{0,2},{1,3},{2,0},{3,1},{4,6},{5,7},{6,4},{7,5},{8,10},{9,11},{10,... | collective-permute-start | bytes 294920 | tf_op jit(solution)/shard_map/lower_lab_shift_2/ppermute | solution.py:200
  7.5 1.3 %collective-permute-start.3 = (bf16[64,768]{1,0:T(8,128)(2,1)S(1)}, bf16[64,768]{1,0:T(8,128)(2,1)S(1)}, u32[]{:S(2)}, u32[]{:S(2)}) collective-permute-start(bf16[64,768]{1,0:T(8,128)(2,1)S(1)} %get-tuple-element.42), channel_id=1, source_target_pairs={{0,3},{1,0},{2,1},{3,2},{4,7},{5,4},{6,5},{7,6},{8,11},{9,8},{10,9... | collective-permute-start | bytes 294920 | tf_op jit(solution)/shard_map/lower_lab_shift_3/ppermute | solution.py:200
  15.9 0.8 %collective-permute-start.5 = (bf16[64,768]{1,0:T(8,128)(2,1)S(1)}, bf16[64,768]{1,0:T(8,128)(2,1)S(1)}, u32[]{:S(2)}, u32[]{:S(2)}) collective-permute-start(bf16[64,768]{1,0:T(8,128)(2,1)S(1)} %get-tuple-element.45), channel_id=1, source_target_pairs={{0,28},{4,0},{8,4},{12,8},{16,12},{20,16},{24,20},{28,24},{1,29},{... | collective-permute-start | bytes 294920 | tf_op jit(solution)/shard_map/lower_doc_shift_1/ppermute | solution.py:200
  16.7 1.7 %collective-permute-start.6 = (bf16[64,768]{1,0:T(8,128)(2,1)S(1)}, bf16[64,768]{1,0:T(8,128)(2,1)S(1)}, u32[]{:S(2)}, u32[]{:S(2)}) collective-permute-start(bf16[64,768]{1,0:T(8,128)(2,1)S(1)} %get-tuple-element.46), channel_id=1, source_target_pairs={{0,24},{4,28},{8,0},{12,4},{16,8},{20,12},{24,16},{28,20},{1,25},{... | collective-permute-start | bytes 294920 | tf_op jit(solution)/shard_map/lower_doc_shift_2/ppermute | solution.py:200
  18.7 2.2 %collective-permute-done.refs_1_ = bf16[144,768]{1,0:T(8,128)(2,1)S(1)} collective-permute-done((bf16[144,768]{1,0:T(8,128)(2,1)S(1)}, bf16[144,768]{1,0:T(8,128)(2,1)S(1)}, u32[]{:S(2)}, u32[]{:S(2)}) %collective-permute-start) | collective-permute-done | bytes 221216 | tf_op jit(solution)/shard_map/upper_0_lab_hop_1/ppermute | solution.py:200
  21.0 1.7 %collective-permute-done.6 = bf16[64,768]{1,0:T(8,128)(2,1)S(1)} collective-permute-done((bf16[64,768]{1,0:T(8,128)(2,1)S(1)}, bf16[64,768]{1,0:T(8,128)(2,1)S(1)}, u32[]{:S(2)}, u32[]{:S(2)}) %collective-permute-start.6) | collective-permute-done | bytes 98336 | tf_op jit(solution)/shard_map/lower_doc_shift_2/ppermute | solution.py:200
  23.2 1.5 %collective-permute-start.21 = (bf16[128,768]{1,0:T(8,128)(2,1)S(1)}, bf16[128,768]{1,0:T(8,128)(2,1)S(1)}, u32[]{:S(2)}, u32[]{:S(2)}) collective-permute-start(bf16[128,768]{1,0:T(8,128)(2,1)S(1)} %constant_dynamic-update-slice_fusion.2.refs_2_), channel_id=1, source_target_pairs={{0,1},{1,3},{3,2},{2,0},{4,5},{5,7},{7,6},{6,4},{8,9},{9,11},{11,1... | collective-permute-start | bytes 589832 | tf_op jit(solution)/shard_map/part_0_lab_hop_1/ppermute | solution.py:200
  24.6 5.6 %collective-permute-done.4.refs_2_ = bf16[144,768]{1,0:T(8,128)(2,1)S(1)} collective-permute-done((bf16[144,768]{1,0:T(8,128)(2,1)S(1)}, bf16[144,768]{1,0:T(8,128)(2,1)S(1)}, u32[]{:S(2)}, u32[]{:S(2)}) %collective-permute-start.4) | collective-permute-done | bytes 221216 | tf_op jit(solution)/shard_map/upper_0_lab_hop_2/ppermute | solution.py:200
  30.3 3.2 %collective-permute-start.15 = (bf16[128,768]{1,0:T(8,128)(2,1)S(1)}, bf16[128,768]{1,0:T(8,128)(2,1)S(1)}, u32[]{:S(2)}, u32[]{:S(2)}) collective-permute-start(bf16[128,768]{1,0:T(8,128)(2,1)S(1)} %constant_dynamic-update-slice_fusion.refs_2_), channel_id=1, source_target_pairs={{0,1},{1,3},{3,2},{2,0},{4,5},{5,7},{7,6},{6,4},{8,9},{9,11},{11,1... | collective-permute-start | bytes 589832 | tf_op jit(solution)/shard_map/part_1_lab_hop_1/ppermute | solution.py:200
  33.6 5.9 %collective-permute-done.8.refs_3_ = bf16[144,768]{1,0:T(8,128)(2,1)S(1)} collective-permute-done((bf16[144,768]{1,0:T(8,128)(2,1)S(1)}, bf16[144,768]{1,0:T(8,128)(2,1)S(1)}, u32[]{:S(2)}, u32[]{:S(2)}) %collective-permute-start.8) | collective-permute-done | bytes 221216 | tf_op jit(solution)/shard_map/upper_0_lab_hop_3/ppermute | solution.py:200
  40.8 1.9 %collective-permute-start.10 = (bf16[144,768]{1,0:T(8,128)(2,1)S(1)}, bf16[144,768]{1,0:T(8,128)(2,1)S(1)}, u32[]{:S(2)}, u32[]{:S(2)}) collective-permute-start(bf16[144,768]{1,0:T(8,128)(2,1)S(1)} %get-tuple-element.50), channel_id=1, source_target_pairs={{0,24},{4,28},{8,0},{12,4},{16,8},{20,12},{24,16},{28,20},{1,25},{... | collective-permute-start | bytes 663560 | tf_op jit(solution)/shard_map/upper_0_doc_shift_2/ppermute | solution.py:200
  42.7 5.2 %collective-permute-done.12.refs_2_ = bf16[128,768]{1,0:T(8,128)(2,1)S(1)} collective-permute-done((bf16[128,768]{1,0:T(8,128)(2,1)S(1)}, bf16[128,768]{1,0:T(8,128)(2,1)S(1)}, u32[]{:S(2)}, u32[]{:S(2)}) %collective-permute-start.12) | collective-permute-done | bytes 196640 | tf_op jit(solution)/shard_map/upper_1_lab_hop_2/ppermute | solution.py:200
  48.0 3.2 %collective-permute-start.17 = (bf16[128,768]{1,0:T(8,128)(2,1)S(1)}, bf16[128,768]{1,0:T(8,128)(2,1)S(1)}, u32[]{:S(2)}, u32[]{:S(2)}) collective-permute-start(bf16[128,768]{1,0:T(8,128)(2,1)S(1)} %collective-permute-done.15.refs_3_), channel_id=1, source_target_pairs={{0,1},{1,3},{3,2},{2,0},{4,5},{5,7},{7,6},{6,4},{8,9},{9,11},{11,1... | collective-permute-start | bytes 589832 | tf_op jit(solution)/shard_map/part_1_lab_hop_2/ppermute | solution.py:200
  51.4 0.8 %collective-permute-done.22.refs_4_ = bf16[128,768]{1,0:T(8,128)(2,1)S(1)} collective-permute-done((bf16[128,768]{1,0:T(8,128)(2,1)S(1)}, bf16[128,768]{1,0:T(8,128)(2,1)S(1)}, u32[]{:S(2)}, u32[]{:S(2)}) %collective-permute-start.22) | collective-permute-done | bytes 196640 | tf_op jit(solution)/shard_map/part_0_lab_hop_2/ppermute | solution.py:200
  52.2 4.5 %collective-permute-done.13.refs_3_ = bf16[128,768]{1,0:T(8,128)(2,1)S(1)} collective-permute-done((bf16[128,768]{1,0:T(8,128)(2,1)S(1)}, bf16[128,768]{1,0:T(8,128)(2,1)S(1)}, u32[]{:S(2)}, u32[]{:S(2)}) %collective-permute-start.13) | collective-permute-done | bytes 196640 | tf_op jit(solution)/shard_map/upper_1_lab_hop_3/ppermute | solution.py:200
  57.0 2.5 %collective-permute-start.19 = (bf16[128,768]{1,0:T(8,128)(2,1)S(1)}, bf16[128,768]{1,0:T(8,128)(2,1)S(1)}, u32[]{:S(2)}, u32[]{:S(2)}) collective-permute-start(bf16[128,768]{1,0:T(8,128)(2,1)S(1)} %get-tuple-element.62), channel_id=1, source_target_pairs={{0,24},{4,28},{8,0},{12,4},{16,8},{20,12},{24,16},{28,20},{1,25},{... | collective-permute-start | bytes 589832 | tf_op jit(solution)/shard_map/upper_1_doc_shift_2/ppermute | solution.py:200
  59.5 1.4 %collective-permute-done.17.refs_4_ = bf16[128,768]{1,0:T(8,128)(2,1)S(1)} collective-permute-done((bf16[128,768]{1,0:T(8,128)(2,1)S(1)}, bf16[128,768]{1,0:T(8,128)(2,1)S(1)}, u32[]{:S(2)}, u32[]{:S(2)}) %collective-permute-start.17) | collective-permute-done | bytes 196640 | tf_op jit(solution)/shard_map/part_1_lab_hop_2/ppermute | solution.py:200
  61.1 3.6 %collective-permute-done.23.refs_5_ = bf16[128,768]{1,0:T(8,128)(2,1)S(1)} collective-permute-done((bf16[128,768]{1,0:T(8,128)(2,1)S(1)}, bf16[128,768]{1,0:T(8,128)(2,1)S(1)}, u32[]{:S(2)}, u32[]{:S(2)}) %collective-permute-start.23) | collective-permute-done | bytes 196640 | tf_op jit(solution)/shard_map/part_0_lab_hop_3/ppermute | solution.py:200
  64.7 1.6 %update_block.4 = (f32[256,768]{1,0:T(8,128)S(1)}, f32[256,768]{1,0:T(8,128)S(1)}) custom-call(bf16[144,768]{1,0:T(8,128)(2,1)S(1)} %get-tuple-element.54.refs_0_, bf16[128,768]{1,0:T(8,128)(2,1)S(1)} %get-tuple-element.67.refs_1_, bf16[128,768]{1,0:T(8,128)(2,1)S(1)} %constant_dynamic-update-slice_fusion.2.refs_2_, ...), custom_call_target="tpu_custom_call" | custom-call | flops 805306368 | bytes 3932160 | tf_op jit(solution)/shard_map/update_block/pallas_call | solution.py:177
  66.3 1.6 %update_block.5 = (f32[256,768]{1,0:T(8,128)S(1)}, f32[256,768]{1,0:T(8,128)S(1)}) custom-call(bf16[144,768]{1,0:T(8,128)(2,1)S(1)} %collective-permute-done.16.refs_0_, bf16[128,768]{1,0:T(8,128)(2,1)S(1)} %collective-permute-done.20.refs_1_, bf16[128,768]{1,0:T(8,128)(2,1)S(1)} %constant_dynamic-update-slice_fusion.2.refs_2_, ...), custom_call_target="tpu_custom_call" | custom-call | flops 805306368 | bytes 3932160 | tf_op jit(solution)/shard_map/update_block/pallas_call | solution.py:177
  68.3 1.6 %update_block.6 = (f32[256,768]{1,0:T(8,128)S(1)}, f32[256,768]{1,0:T(8,128)S(1)}) custom-call(bf16[144,768]{1,0:T(8,128)(2,1)S(1)} %collective-permute-done.10.refs_0_, bf16[128,768]{1,0:T(8,128)(2,1)S(1)} %collective-permute-done.19.refs_1_, bf16[128,768]{1,0:T(8,128)(2,1)S(1)} %constant_dynamic-update-slice_fusion.refs_2_, ...), custom_call_target="tpu_custom_call" | custom-call | flops 805306368 | bytes 3932160 | tf_op jit(solution)/shard_map/update_block/pallas_call | solution.py:177
  69.9 2.6 %update_block.7 = (f32[256,768]{1,0:T(8,128)}, f32[256,768]{1,0:T(8,128)}) custom-call(bf16[144,768]{1,0:T(8,128)(2,1)S(1)} %collective-permute-done.9.refs_0_, bf16[128,768]{1,0:T(8,128)(2,1)S(1)} %collective-permute-done.14.refs_1_, bf16[128,768]{1,0:T(8,128)(2,1)S(1)} %constant_dynamic-update-slice_fusion.refs_2_, ...), custom_call_target="tpu_custom_call" | custom-call | flops 805306368 | bytes 3932160 | tf_op jit(solution)/shard_map/update_block/pallas_call | solution.py:177
  (72 shorter events, 10.1 us)
Async XLA Ops:
  1.8 13.8 %collective-permute-start.1 = (bf16[64,768]{1,0:T(8,128)(2,1)S(1)}, bf16[64,768]{1,0:T(8,128)(2,1)S(1)}, u32[]{:S(2)}, u32[]{:S(2)}) collective-permute-start(bf16[64,768]{1,0:T(8,128)(2,1)S(1)} %get-tuple-element.40), channel_id=1, source_target_pairs={{0,1},{1,2},{2,3},{3,0},{4,5},{5,6},{6,7},{7,4},{8,9},{9,10},{10,1... | collective-permute-start | bytes 294920 | tf_op jit(solution)/shard_map/lower_lab_shift_1/ppermute | solution.py:200
  4.9 10.7 %collective-permute-start.2 = (bf16[64,768]{1,0:T(8,128)(2,1)S(1)}, bf16[64,768]{1,0:T(8,128)(2,1)S(1)}, u32[]{:S(2)}, u32[]{:S(2)}) collective-permute-start(bf16[64,768]{1,0:T(8,128)(2,1)S(1)} %get-tuple-element.41), channel_id=1, source_target_pairs={{0,2},{1,3},{2,0},{3,1},{4,6},{5,7},{6,4},{7,5},{8,10},{9,11},{10,... | collective-permute-start | bytes 294920 | tf_op jit(solution)/shard_map/lower_lab_shift_2/ppermute | solution.py:200
  7.5 8.2 %collective-permute-start.3 = (bf16[64,768]{1,0:T(8,128)(2,1)S(1)}, bf16[64,768]{1,0:T(8,128)(2,1)S(1)}, u32[]{:S(2)}, u32[]{:S(2)}) collective-permute-start(bf16[64,768]{1,0:T(8,128)(2,1)S(1)} %get-tuple-element.42), channel_id=1, source_target_pairs={{0,3},{1,0},{2,1},{3,2},{4,7},{5,4},{6,5},{7,6},{8,11},{9,8},{10,9... | collective-permute-start | bytes 294920 | tf_op jit(solution)/shard_map/lower_lab_shift_3/ppermute | solution.py:200
  9.0 12.0 %collective-permute-start = (bf16[144,768]{1,0:T(8,128)(2,1)S(1)}, bf16[144,768]{1,0:T(8,128)(2,1)S(1)}, u32[]{:S(2)}, u32[]{:S(2)}) collective-permute-start(bf16[144,768]{1,0:T(8,128)(2,1)S(1)} %fusion.2.refs_0_), channel_id=1, source_target_pairs={{0,1},{1,3},{3,2},{2,0},{4,5},{5,7},{7,6},{6,4},{8,9},{9,11},{11,1... | collective-permute-start | bytes 663560 | tf_op jit(solution)/shard_map/upper_0_lab_hop_1/ppermute | solution.py:200
  9.7 23.8 %collective-permute-start.11 = (bf16[128,768]{1,0:T(8,128)(2,1)S(1)}, bf16[128,768]{1,0:T(8,128)(2,1)S(1)}, u32[]{:S(2)}, u32[]{:S(2)}) collective-permute-start(bf16[128,768]{1,0:T(8,128)(2,1)S(1)} %get-tuple-element.52.refs_0_), channel_id=1, source_target_pairs={{0,1},{1,3},{3,2},{2,0},{4,5},{5,7},{7,6},{6,4},{8,9},{9,11},{11,1... | collective-permute-start | bytes 589832 | tf_op jit(solution)/shard_map/upper_1_lab_hop_1/ppermute | solution.py:200
  15.9 5.1 %collective-permute-start.5 = (bf16[64,768]{1,0:T(8,128)(2,1)S(1)}, bf16[64,768]{1,0:T(8,128)(2,1)S(1)}, u32[]{:S(2)}, u32[]{:S(2)}) collective-permute-start(bf16[64,768]{1,0:T(8,128)(2,1)S(1)} %get-tuple-element.45), channel_id=1, source_target_pairs={{0,28},{4,0},{8,4},{12,8},{16,12},{20,16},{24,20},{28,24},{1,29},{... | collective-permute-start | bytes 294920 | tf_op jit(solution)/shard_map/lower_doc_shift_1/ppermute | solution.py:200
  16.7 6.1 %collective-permute-start.6 = (bf16[64,768]{1,0:T(8,128)(2,1)S(1)}, bf16[64,768]{1,0:T(8,128)(2,1)S(1)}, u32[]{:S(2)}, u32[]{:S(2)}) collective-permute-start(bf16[64,768]{1,0:T(8,128)(2,1)S(1)} %get-tuple-element.46), channel_id=1, source_target_pairs={{0,24},{4,28},{8,0},{12,4},{16,8},{20,12},{24,16},{28,20},{1,25},{... | collective-permute-start | bytes 294920 | tf_op jit(solution)/shard_map/lower_doc_shift_2/ppermute | solution.py:200
  18.4 4.7 %collective-permute-start.7 = (bf16[64,768]{1,0:T(8,128)(2,1)S(1)}, bf16[64,768]{1,0:T(8,128)(2,1)S(1)}, u32[]{:S(2)}, u32[]{:S(2)}) collective-permute-start(bf16[64,768]{1,0:T(8,128)(2,1)S(1)} %get-tuple-element.47), channel_id=1, source_target_pairs={{0,20},{4,24},{8,28},{12,0},{16,4},{20,8},{24,12},{28,16},{1,21},{... | collective-permute-start | bytes 294920 | tf_op jit(solution)/shard_map/lower_doc_shift_3/ppermute | solution.py:200
  21.0 9.3 %collective-permute-start.4 = (bf16[144,768]{1,0:T(8,128)(2,1)S(1)}, bf16[144,768]{1,0:T(8,128)(2,1)S(1)}, u32[]{:S(2)}, u32[]{:S(2)}) collective-permute-start(bf16[144,768]{1,0:T(8,128)(2,1)S(1)} %collective-permute-done.refs_1_), channel_id=1, source_target_pairs={{0,1},{1,3},{3,2},{2,0},{4,5},{5,7},{7,6},{6,4},{8,9},{9,11},{11,1... | collective-permute-start | bytes 663560 | tf_op jit(solution)/shard_map/upper_0_lab_hop_2/ppermute | solution.py:200
  23.2 17.5 %collective-permute-start.21 = (bf16[128,768]{1,0:T(8,128)(2,1)S(1)}, bf16[128,768]{1,0:T(8,128)(2,1)S(1)}, u32[]{:S(2)}, u32[]{:S(2)}) collective-permute-start(bf16[128,768]{1,0:T(8,128)(2,1)S(1)} %constant_dynamic-update-slice_fusion.2.refs_2_), channel_id=1, source_target_pairs={{0,1},{1,3},{3,2},{2,0},{4,5},{5,7},{7,6},{6,4},{8,9},{9,11},{11,1... | collective-permute-start | bytes 589832 | tf_op jit(solution)/shard_map/part_0_lab_hop_1/ppermute | solution.py:200
  30.2 9.3 %collective-permute-start.8 = (bf16[144,768]{1,0:T(8,128)(2,1)S(1)}, bf16[144,768]{1,0:T(8,128)(2,1)S(1)}, u32[]{:S(2)}, u32[]{:S(2)}) collective-permute-start(bf16[144,768]{1,0:T(8,128)(2,1)S(1)} %collective-permute-done.4.refs_2_), channel_id=1, source_target_pairs={{0,1},{1,3},{3,2},{2,0},{4,5},{5,7},{7,6},{6,4},{8,9},{9,11},{11,1... | collective-permute-start | bytes 663560 | tf_op jit(solution)/shard_map/upper_0_lab_hop_3/ppermute | solution.py:200
  30.3 17.7 %collective-permute-start.15 = (bf16[128,768]{1,0:T(8,128)(2,1)S(1)}, bf16[128,768]{1,0:T(8,128)(2,1)S(1)}, u32[]{:S(2)}, u32[]{:S(2)}) collective-permute-start(bf16[128,768]{1,0:T(8,128)(2,1)S(1)} %constant_dynamic-update-slice_fusion.refs_2_), channel_id=1, source_target_pairs={{0,1},{1,3},{3,2},{2,0},{4,5},{5,7},{7,6},{6,4},{8,9},{9,11},{11,1... | collective-permute-start | bytes 589832 | tf_op jit(solution)/shard_map/part_1_lab_hop_1/ppermute | solution.py:200
  33.5 14.4 %collective-permute-start.12 = (bf16[128,768]{1,0:T(8,128)(2,1)S(1)}, bf16[128,768]{1,0:T(8,128)(2,1)S(1)}, u32[]{:S(2)}, u32[]{:S(2)}) collective-permute-start(bf16[128,768]{1,0:T(8,128)(2,1)S(1)} %collective-permute-done.11.refs_1_), channel_id=1, source_target_pairs={{0,1},{1,3},{3,2},{2,0},{4,5},{5,7},{7,6},{6,4},{8,9},{9,11},{11,1... | collective-permute-start | bytes 589832 | tf_op jit(solution)/shard_map/upper_1_lab_hop_2/ppermute | solution.py:200
  39.8 8.2 %collective-permute-start.16 = (bf16[144,768]{1,0:T(8,128)(2,1)S(1)}, bf16[144,768]{1,0:T(8,128)(2,1)S(1)}, u32[]{:S(2)}, u32[]{:S(2)}) collective-permute-start(bf16[144,768]{1,0:T(8,128)(2,1)S(1)} %get-tuple-element.58), channel_id=1, source_target_pairs={{0,28},{4,0},{8,4},{12,8},{16,12},{20,16},{24,20},{28,24},{1,29},{... | collective-permute-start | bytes 663560 | tf_op jit(solution)/shard_map/upper_0_doc_shift_1/ppermute | solution.py:200
  40.7 11.4 %collective-permute-start.22 = (bf16[128,768]{1,0:T(8,128)(2,1)S(1)}, bf16[128,768]{1,0:T(8,128)(2,1)S(1)}, u32[]{:S(2)}, u32[]{:S(2)}) collective-permute-start(bf16[128,768]{1,0:T(8,128)(2,1)S(1)} %collective-permute-done.21.refs_3_), channel_id=1, source_target_pairs={{0,1},{1,3},{3,2},{2,0},{4,5},{5,7},{7,6},{6,4},{8,9},{9,11},{11,1... | collective-permute-start | bytes 589832 | tf_op jit(solution)/shard_map/part_0_lab_hop_2/ppermute | solution.py:200
  40.8 11.4 %collective-permute-start.10 = (bf16[144,768]{1,0:T(8,128)(2,1)S(1)}, bf16[144,768]{1,0:T(8,128)(2,1)S(1)}, u32[]{:S(2)}, u32[]{:S(2)}) collective-permute-start(bf16[144,768]{1,0:T(8,128)(2,1)S(1)} %get-tuple-element.50), channel_id=1, source_target_pairs={{0,24},{4,28},{8,0},{12,4},{16,8},{20,12},{24,16},{28,20},{1,25},{... | collective-permute-start | bytes 663560 | tf_op jit(solution)/shard_map/upper_0_doc_shift_2/ppermute | solution.py:200
  47.9 8.7 %collective-permute-start.13 = (bf16[128,768]{1,0:T(8,128)(2,1)S(1)}, bf16[128,768]{1,0:T(8,128)(2,1)S(1)}, u32[]{:S(2)}, u32[]{:S(2)}) collective-permute-start(bf16[128,768]{1,0:T(8,128)(2,1)S(1)} %collective-permute-done.12.refs_2_), channel_id=1, source_target_pairs={{0,1},{1,3},{3,2},{2,0},{4,5},{5,7},{7,6},{6,4},{8,9},{9,11},{11,1... | collective-permute-start | bytes 589832 | tf_op jit(solution)/shard_map/upper_1_lab_hop_3/ppermute | solution.py:200
  48.0 12.9 %collective-permute-start.17 = (bf16[128,768]{1,0:T(8,128)(2,1)S(1)}, bf16[128,768]{1,0:T(8,128)(2,1)S(1)}, u32[]{:S(2)}, u32[]{:S(2)}) collective-permute-start(bf16[128,768]{1,0:T(8,128)(2,1)S(1)} %collective-permute-done.15.refs_3_), channel_id=1, source_target_pairs={{0,1},{1,3},{3,2},{2,0},{4,5},{5,7},{7,6},{6,4},{8,9},{9,11},{11,1... | collective-permute-start | bytes 589832 | tf_op jit(solution)/shard_map/part_1_lab_hop_2/ppermute | solution.py:200
  51.3 9.7 %collective-permute-start.9 = (bf16[144,768]{1,0:T(8,128)(2,1)S(1)}, bf16[144,768]{1,0:T(8,128)(2,1)S(1)}, u32[]{:S(2)}, u32[]{:S(2)}) collective-permute-start(bf16[144,768]{1,0:T(8,128)(2,1)S(1)} %get-tuple-element.49), channel_id=1, source_target_pairs={{0,20},{4,24},{8,28},{12,0},{16,4},{20,8},{24,12},{28,16},{1,21},{... | collective-permute-start | bytes 663560 | tf_op jit(solution)/shard_map/upper_0_doc_shift_3/ppermute | solution.py:200
  52.2 12.5 %collective-permute-start.23 = (bf16[128,768]{1,0:T(8,128)(2,1)S(1)}, bf16[128,768]{1,0:T(8,128)(2,1)S(1)}, u32[]{:S(2)}, u32[]{:S(2)}) collective-permute-start(bf16[128,768]{1,0:T(8,128)(2,1)S(1)} %collective-permute-done.22.refs_4_), channel_id=1, source_target_pairs={{0,1},{1,3},{3,2},{2,0},{4,5},{5,7},{7,6},{6,4},{8,9},{9,11},{11,1... | collective-permute-start | bytes 589832 | tf_op jit(solution)/shard_map/part_0_lab_hop_3/ppermute | solution.py:200
  56.9 9.4 %collective-permute-start.20 = (bf16[128,768]{1,0:T(8,128)(2,1)S(1)}, bf16[128,768]{1,0:T(8,128)(2,1)S(1)}, u32[]{:S(2)}, u32[]{:S(2)}) collective-permute-start(bf16[128,768]{1,0:T(8,128)(2,1)S(1)} %get-tuple-element.64), channel_id=1, source_target_pairs={{0,28},{4,0},{8,4},{12,8},{16,12},{20,16},{24,20},{28,24},{1,29},{... | collective-permute-start | bytes 589832 | tf_op jit(solution)/shard_map/upper_1_doc_shift_1/ppermute | solution.py:200
  57.0 11.3 %collective-permute-start.19 = (bf16[128,768]{1,0:T(8,128)(2,1)S(1)}, bf16[128,768]{1,0:T(8,128)(2,1)S(1)}, u32[]{:S(2)}, u32[]{:S(2)}) collective-permute-start(bf16[128,768]{1,0:T(8,128)(2,1)S(1)} %get-tuple-element.62), channel_id=1, source_target_pairs={{0,24},{4,28},{8,0},{12,4},{16,8},{20,12},{24,16},{28,20},{1,25},{... | collective-permute-start | bytes 589832 | tf_op jit(solution)/shard_map/upper_1_doc_shift_2/ppermute | solution.py:200
  60.9 7.4 %collective-permute-start.18 = (bf16[128,768]{1,0:T(8,128)(2,1)S(1)}, bf16[128,768]{1,0:T(8,128)(2,1)S(1)}, u32[]{:S(2)}, u32[]{:S(2)}) collective-permute-start(bf16[128,768]{1,0:T(8,128)(2,1)S(1)} %collective-permute-done.17.refs_4_), channel_id=1, source_target_pairs={{0,1},{1,3},{3,2},{2,0},{4,5},{5,7},{7,6},{6,4},{8,9},{9,11},{11,1... | collective-permute-start | bytes 589832 | tf_op jit(solution)/shard_map/part_1_lab_hop_3/ppermute | solution.py:200
  61.0 8.9 %collective-permute-start.14 = (bf16[128,768]{1,0:T(8,128)(2,1)S(1)}, bf16[128,768]{1,0:T(8,128)(2,1)S(1)}, u32[]{:S(2)}, u32[]{:S(2)}) collective-permute-start(bf16[128,768]{1,0:T(8,128)(2,1)S(1)} %get-tuple-element.57), channel_id=1, source_target_pairs={{0,20},{4,24},{8,28},{12,0},{16,4},{20,8},{24,12},{28,16},{1,21},{... | collective-permute-start | bytes 589832 | tf_op jit(solution)/shard_map/upper_1_doc_shift_3/ppermute | solution.py:200
  (7 other events, 85.9 us)

commit v8 on v7

--- a/solution.py
+++ b/solution.py
@@ -132,9 +132,9 @@
     label = (label.astype(jnp.float32) * live_ref[:, count:]).astype(jnp.bfloat16)
     label = jnp.concatenate([label] * (count // LANES), axis=1)
     target = jnp.zeros(label.shape, jnp.bfloat16)
+    codes = panels[0][tops[0] : tops[0] + POS, :count]
     for k in range(POS):
-        code = panels[0][tops[0] + k : tops[0] + k + 1, :count]
-        target = jnp.where(label == code, jnp.bfloat16(1.0), target)
+        target = jnp.where(label == codes[k : k + 1, :], jnp.bfloat16(1.0), target)
     scores = product(pair, rows, ((1,), (1,))) * scale
     resid = (jax.nn.sigmoid(scores) - target.astype(jnp.float32)) * live_ref[:, :count]
     resid = split(resid)

time: 72.8 us -> 72.8 us (level)
  no operation moved by 1% of the time
where the time goes in v8:
time: 72.8 us; the launch traced here: 72.5 us
  waiting for transfers between devices  31.9 us (44%)
  starting transfers between devices  24.5 us (34%)
  Pallas kernels  9.18 us (13%)
  local copies, waits for them, and re-layouts  4.68 us (6%)
  other arithmetic  1.42 us (2%)
  between operations  0.91 us (1%)
    ppermute x24, waiting for transfers between devices, send(): return lax.ppermute(value, axis, pairs)  31.9 us
    ppermute x24, starting transfers between devices, send(): return lax.ppermute(value, axis, pairs)  24.5 us
    pallas_call x4, Pallas kernels, update(): pl.pallas_call(functools.partial(update_kernel, first, last, len(pieces),...  7.39 us
    unnamed x16, local copies, waits for them, and re-layouts  2.04 us
  transfers between devices with their start and end apart: 24, of which 11 were waited for; matrix products, arithmetic and copies ran while one was open for 6% of the time, Pallas kernels for 8%

profile of v8, /device:TPU:0, one launch (start us, length us, event | category | flops | bytes accessed | tf_op | source)
XLA Modules:
  0.0 72.5 jit_solution(17629277776505570183)
XLA Ops:
  0.7 1.2 %pack_pieces.1 = (bf16[64,768]{1,0:T(8,128)(2,1)S(1)}, bf16[64,768]{1,0:T(8,128)(2,1)S(1)}, bf16[64,768]{1,0:T(8,128)(2,1)S(1)}, bf16[64,768]{1,0:T(8,128)(2,1)S(1)}) custom-call(bf16[512,768]{1,0:T(8,128)(2,1)} %source.1), custom_call_target="tpu_custom_call" | custom-call | tf_op jit(solution)/shard_map/pack_pieces/pallas_call | solution.py:74
  1.8 3.1 %collective-permute-start.1 = (bf16[64,768]{1,0:T(8,128)(2,1)S(1)}, bf16[64,768]{1,0:T(8,128)(2,1)S(1)}, u32[]{:S(2)}, u32[]{:S(2)}) collective-permute-start(bf16[64,768]{1,0:T(8,128)(2,1)S(1)} %get-tuple-element.40), channel_id=1, source_target_pairs={{0,1},{1,2},{2,3},{3,0},{4,5},{5,6},{6,7},{7,4},{8,9},{9,10},{10,1... | collective-permute-start | bytes 294920 | tf_op jit(solution)/shard_map/lower_lab_shift_1/ppermute | solution.py:200
  4.9 2.6 %collective-permute-start.2 = (bf16[64,768]{1,0:T(8,128)(2,1)S(1)}, bf16[64,768]{1,0:T(8,128)(2,1)S(1)}, u32[]{:S(2)}, u32[]{:S(2)}) collective-permute-start(bf16[64,768]{1,0:T(8,128)(2,1)S(1)} %get-tuple-element.41), channel_id=1, source_target_pairs={{0,2},{1,3},{2,0},{3,1},{4,6},{5,7},{6,4},{7,5},{8,10},{9,11},{10,... | collective-permute-start | bytes 294920 | tf_op jit(solution)/shard_map/lower_lab_shift_2/ppermute | solution.py:200
  7.5 1.3 %collective-permute-start.3 = (bf16[64,768]{1,0:T(8,128)(2,1)S(1)}, bf16[64,768]{1,0:T(8,128)(2,1)S(1)}, u32[]{:S(2)}, u32[]{:S(2)}) collective-permute-start(bf16[64,768]{1,0:T(8,128)(2,1)S(1)} %get-tuple-element.42), channel_id=1, source_target_pairs={{0,3},{1,0},{2,1},{3,2},{4,7},{5,4},{6,5},{7,6},{8,11},{9,8},{10,9... | collective-permute-start | bytes 294920 | tf_op jit(solution)/shard_map/lower_lab_shift_3/ppermute | solution.py:200
  15.9 0.8 %collective-permute-start.5 = (bf16[64,768]{1,0:T(8,128)(2,1)S(1)}, bf16[64,768]{1,0:T(8,128)(2,1)S(1)}, u32[]{:S(2)}, u32[]{:S(2)}) collective-permute-start(bf16[64,768]{1,0:T(8,128)(2,1)S(1)} %get-tuple-element.45), channel_id=1, source_target_pairs={{0,28},{4,0},{8,4},{12,8},{16,12},{20,16},{24,20},{28,24},{1,29},{... | collective-permute-start | bytes 294920 | tf_op jit(solution)/shard_map/lower_doc_shift_1/ppermute | solution.py:200
  16.7 1.7 %collective-permute-start.6 = (bf16[64,768]{1,0:T(8,128)(2,1)S(1)}, bf16[64,768]{1,0:T(8,128)(2,1)S(1)}, u32[]{:S(2)}, u32[]{:S(2)}) collective-permute-start(bf16[64,768]{1,0:T(8,128)(2,1)S(1)} %get-tuple-element.46), channel_id=1, source_target_pairs={{0,24},{4,28},{8,0},{12,4},{16,8},{20,12},{24,16},{28,20},{1,25},{... | collective-permute-start | bytes 294920 | tf_op jit(solution)/shard_map/lower_doc_shift_2/ppermute | solution.py:200
  18.7 2.2 %collective-permute-done.refs_1_ = bf16[144,768]{1,0:T(8,128)(2,1)S(1)} collective-permute-done((bf16[144,768]{1,0:T(8,128)(2,1)S(1)}, bf16[144,768]{1,0:T(8,128)(2,1)S(1)}, u32[]{:S(2)}, u32[]{:S(2)}) %collective-permute-start) | collective-permute-done | bytes 221216 | tf_op jit(solution)/shard_map/upper_0_lab_hop_1/ppermute | solution.py:200
  21.0 1.7 %collective-permute-done.6 = bf16[64,768]{1,0:T(8,128)(2,1)S(1)} collective-permute-done((bf16[64,768]{1,0:T(8,128)(2,1)S(1)}, bf16[64,768]{1,0:T(8,128)(2,1)S(1)}, u32[]{:S(2)}, u32[]{:S(2)}) %collective-permute-start.6) | collective-permute-done | bytes 98336 | tf_op jit(solution)/shard_map/lower_doc_shift_2/ppermute | solution.py:200
  23.2 1.5 %collective-permute-start.21 = (bf16[128,768]{1,0:T(8,128)(2,1)S(1)}, bf16[128,768]{1,0:T(8,128)(2,1)S(1)}, u32[]{:S(2)}, u32[]{:S(2)}) collective-permute-start(bf16[128,768]{1,0:T(8,128)(2,1)S(1)} %constant_dynamic-update-slice_fusion.2.refs_2_), channel_id=1, source_target_pairs={{0,1},{1,3},{3,2},{2,0},{4,5},{5,7},{7,6},{6,4},{8,9},{9,11},{11,1... | collective-permute-start | bytes 589832 | tf_op jit(solution)/shard_map/part_0_lab_hop_1/ppermute | solution.py:200
  24.6 5.6 %collective-permute-done.4.refs_2_ = bf16[144,768]{1,0:T(8,128)(2,1)S(1)} collective-permute-done((bf16[144,768]{1,0:T(8,128)(2,1)S(1)}, bf16[144,768]{1,0:T(8,128)(2,1)S(1)}, u32[]{:S(2)}, u32[]{:S(2)}) %collective-permute-start.4) | collective-permute-done | bytes 221216 | tf_op jit(solution)/shard_map/upper_0_lab_hop_2/ppermute | solution.py:200
  30.3 3.2 %collective-permute-start.15 = (bf16[128,768]{1,0:T(8,128)(2,1)S(1)}, bf16[128,768]{1,0:T(8,128)(2,1)S(1)}, u32[]{:S(2)}, u32[]{:S(2)}) collective-permute-start(bf16[128,768]{1,0:T(8,128)(2,1)S(1)} %constant_dynamic-update-slice_fusion.refs_2_), channel_id=1, source_target_pairs={{0,1},{1,3},{3,2},{2,0},{4,5},{5,7},{7,6},{6,4},{8,9},{9,11},{11,1... | collective-permute-start | bytes 589832 | tf_op jit(solution)/shard_map/part_1_lab_hop_1/ppermute | solution.py:200
  33.6 5.9 %collective-permute-done.8.refs_3_ = bf16[144,768]{1,0:T(8,128)(2,1)S(1)} collective-permute-done((bf16[144,768]{1,0:T(8,128)(2,1)S(1)}, bf16[144,768]{1,0:T(8,128)(2,1)S(1)}, u32[]{:S(2)}, u32[]{:S(2)}) %collective-permute-start.8) | collective-permute-done | bytes 221216 | tf_op jit(solution)/shard_map/upper_0_lab_hop_3/ppermute | solution.py:200
  40.8 1.9 %collective-permute-start.10 = (bf16[144,768]{1,0:T(8,128)(2,1)S(1)}, bf16[144,768]{1,0:T(8,128)(2,1)S(1)}, u32[]{:S(2)}, u32[]{:S(2)}) collective-permute-start(bf16[144,768]{1,0:T(8,128)(2,1)S(1)} %get-tuple-element.50), channel_id=1, source_target_pairs={{0,24},{4,28},{8,0},{12,4},{16,8},{20,12},{24,16},{28,20},{1,25},{... | collective-permute-start | bytes 663560 | tf_op jit(solution)/shard_map/upper_0_doc_shift_2/ppermute | solution.py:200
  42.7 5.2 %collective-permute-done.12.refs_2_ = bf16[128,768]{1,0:T(8,128)(2,1)S(1)} collective-permute-done((bf16[128,768]{1,0:T(8,128)(2,1)S(1)}, bf16[128,768]{1,0:T(8,128)(2,1)S(1)}, u32[]{:S(2)}, u32[]{:S(2)}) %collective-permute-start.12) | collective-permute-done | bytes 196640 | tf_op jit(solution)/shard_map/upper_1_lab_hop_2/ppermute | solution.py:200
  48.0 3.2 %collective-permute-start.17 = (bf16[128,768]{1,0:T(8,128)(2,1)S(1)}, bf16[128,768]{1,0:T(8,128)(2,1)S(1)}, u32[]{:S(2)}, u32[]{:S(2)}) collective-permute-start(bf16[128,768]{1,0:T(8,128)(2,1)S(1)} %collective-permute-done.15.refs_3_), channel_id=1, source_target_pairs={{0,1},{1,3},{3,2},{2,0},{4,5},{5,7},{7,6},{6,4},{8,9},{9,11},{11,1... | collective-permute-start | bytes 589832 | tf_op jit(solution)/shard_map/part_1_lab_hop_2/ppermute | solution.py:200
  51.4 0.8 %collective-permute-done.22.refs_4_ = bf16[128,768]{1,0:T(8,128)(2,1)S(1)} collective-permute-done((bf16[128,768]{1,0:T(8,128)(2,1)S(1)}, bf16[128,768]{1,0:T(8,128)(2,1)S(1)}, u32[]{:S(2)}, u32[]{:S(2)}) %collective-permute-start.22) | collective-permute-done | bytes 196640 | tf_op jit(solution)/shard_map/part_0_lab_hop_2/ppermute | solution.py:200
  52.2 4.5 %collective-permute-done.13.refs_3_ = bf16[128,768]{1,0:T(8,128)(2,1)S(1)} collective-permute-done((bf16[128,768]{1,0:T(8,128)(2,1)S(1)}, bf16[128,768]{1,0:T(8,128)(2,1)S(1)}, u32[]{:S(2)}, u32[]{:S(2)}) %collective-permute-start.13) | collective-permute-done | bytes 196640 | tf_op jit(solution)/shard_map/upper_1_lab_hop_3/ppermute | solution.py:200
  57.0 2.5 %collective-permute-start.19 = (bf16[128,768]{1,0:T(8,128)(2,1)S(1)}, bf16[128,768]{1,0:T(8,128)(2,1)S(1)}, u32[]{:S(2)}, u32[]{:S(2)}) collective-permute-start(bf16[128,768]{1,0:T(8,128)(2,1)S(1)} %get-tuple-element.62), channel_id=1, source_target_pairs={{0,24},{4,28},{8,0},{12,4},{16,8},{20,12},{24,16},{28,20},{1,25},{... | collective-permute-start | bytes 589832 | tf_op jit(solution)/shard_map/upper_1_doc_shift_2/ppermute | solution.py:200
  59.5 1.4 %collective-permute-done.17.refs_4_ = bf16[128,768]{1,0:T(8,128)(2,1)S(1)} collective-permute-done((bf16[128,768]{1,0:T(8,128)(2,1)S(1)}, bf16[128,768]{1,0:T(8,128)(2,1)S(1)}, u32[]{:S(2)}, u32[]{:S(2)}) %collective-permute-start.17) | collective-permute-done | bytes 196640 | tf_op jit(solution)/shard_map/part_1_lab_hop_2/ppermute | solution.py:200
  61.1 3.6 %collective-permute-done.23.refs_5_ = bf16[128,768]{1,0:T(8,128)(2,1)S(1)} collective-permute-done((bf16[128,768]{1,0:T(8,128)(2,1)S(1)}, bf16[128,768]{1,0:T(8,128)(2,1)S(1)}, u32[]{:S(2)}, u32[]{:S(2)}) %collective-permute-start.23) | collective-permute-done | bytes 196640 | tf_op jit(solution)/shard_map/part_0_lab_hop_3/ppermute | solution.py:200
  64.7 1.6 %update_block.4 = (f32[256,768]{1,0:T(8,128)S(1)}, f32[256,768]{1,0:T(8,128)S(1)}) custom-call(bf16[144,768]{1,0:T(8,128)(2,1)S(1)} %get-tuple-element.54.refs_0_, bf16[128,768]{1,0:T(8,128)(2,1)S(1)} %get-tuple-element.67.refs_1_, bf16[128,768]{1,0:T(8,128)(2,1)S(1)} %constant_dynamic-update-slice_fusion.2.refs_2_, ...), custom_call_target="tpu_custom_call" | custom-call | flops 805306368 | bytes 3932160 | tf_op jit(solution)/shard_map/update_block/pallas_call | solution.py:177
  66.3 1.6 %update_block.5 = (f32[256,768]{1,0:T(8,128)S(1)}, f32[256,768]{1,0:T(8,128)S(1)}) custom-call(bf16[144,768]{1,0:T(8,128)(2,1)S(1)} %collective-permute-done.16.refs_0_, bf16[128,768]{1,0:T(8,128)(2,1)S(1)} %collective-permute-done.20.refs_1_, bf16[128,768]{1,0:T(8,128)(2,1)S(1)} %constant_dynamic-update-slice_fusion.2.refs_2_, ...), custom_call_target="tpu_custom_call" | custom-call | flops 805306368 | bytes 3932160 | tf_op jit(solution)/shard_map/update_block/pallas_call | solution.py:177
  68.3 1.6 %update_block.6 = (f32[256,768]{1,0:T(8,128)S(1)}, f32[256,768]{1,0:T(8,128)S(1)}) custom-call(bf16[144,768]{1,0:T(8,128)(2,1)S(1)} %collective-permute-done.10.refs_0_, bf16[128,768]{1,0:T(8,128)(2,1)S(1)} %collective-permute-done.19.refs_1_, bf16[128,768]{1,0:T(8,128)(2,1)S(1)} %constant_dynamic-update-slice_fusion.refs_2_, ...), custom_call_target="tpu_custom_call" | custom-call | flops 805306368 | bytes 3932160 | tf_op jit(solution)/shard_map/update_block/pallas_call | solution.py:177
  69.9 2.6 %update_block.7 = (f32[256,768]{1,0:T(8,128)}, f32[256,768]{1,0:T(8,128)}) custom-call(bf16[144,768]{1,0:T(8,128)(2,1)S(1)} %collective-permute-done.9.refs_0_, bf16[128,768]{1,0:T(8,128)(2,1)S(1)} %collective-permute-done.14.refs_1_, bf16[128,768]{1,0:T(8,128)(2,1)S(1)} %constant_dynamic-update-slice_fusion.refs_2_, ...), custom_call_target="tpu_custom_call" | custom-call | flops 805306368 | bytes 3932160 | tf_op jit(solution)/shard_map/update_block/pallas_call | solution.py:177
  (72 shorter events, 10.1 us)
Async XLA Ops:
  1.8 13.8 %collective-permute-start.1 = (bf16[64,768]{1,0:T(8,128)(2,1)S(1)}, bf16[64,768]{1,0:T(8,128)(2,1)S(1)}, u32[]{:S(2)}, u32[]{:S(2)}) collective-permute-start(bf16[64,768]{1,0:T(8,128)(2,1)S(1)} %get-tuple-element.40), channel_id=1, source_target_pairs={{0,1},{1,2},{2,3},{3,0},{4,5},{5,6},{6,7},{7,4},{8,9},{9,10},{10,1... | collective-permute-start | bytes 294920 | tf_op jit(solution)/shard_map/lower_lab_shift_1/ppermute | solution.py:200
  4.9 10.7 %collective-permute-start.2 = (bf16[64,768]{1,0:T(8,128)(2,1)S(1)}, bf16[64,768]{1,0:T(8,128)(2,1)S(1)}, u32[]{:S(2)}, u32[]{:S(2)}) collective-permute-start(bf16[64,768]{1,0:T(8,128)(2,1)S(1)} %get-tuple-element.41), channel_id=1, source_target_pairs={{0,2},{1,3},{2,0},{3,1},{4,6},{5,7},{6,4},{7,5},{8,10},{9,11},{10,... | collective-permute-start | bytes 294920 | tf_op jit(solution)/shard_map/lower_lab_shift_2/ppermute | solution.py:200
  7.5 8.2 %collective-permute-start.3 = (bf16[64,768]{1,0:T(8,128)(2,1)S(1)}, bf16[64,768]{1,0:T(8,128)(2,1)S(1)}, u32[]{:S(2)}, u32[]{:S(2)}) collective-permute-start(bf16[64,768]{1,0:T(8,128)(2,1)S(1)} %get-tuple-element.42), channel_id=1, source_target_pairs={{0,3},{1,0},{2,1},{3,2},{4,7},{5,4},{6,5},{7,6},{8,11},{9,8},{10,9... | collective-permute-start | bytes 294920 | tf_op jit(solution)/shard_map/lower_lab_shift_3/ppermute | solution.py:200
  9.0 12.0 %collective-permute-start = (bf16[144,768]{1,0:T(8,128)(2,1)S(1)}, bf16[144,768]{1,0:T(8,128)(2,1)S(1)}, u32[]{:S(2)}, u32[]{:S(2)}) collective-permute-start(bf16[144,768]{1,0:T(8,128)(2,1)S(1)} %fusion.2.refs_0_), channel_id=1, source_target_pairs={{0,1},{1,3},{3,2},{2,0},{4,5},{5,7},{7,6},{6,4},{8,9},{9,11},{11,1... | collective-permute-start | bytes 663560 | tf_op jit(solution)/shard_map/upper_0_lab_hop_1/ppermute | solution.py:200
  9.7 23.8 %collective-permute-start.11 = (bf16[128,768]{1,0:T(8,128)(2,1)S(1)}, bf16[128,768]{1,0:T(8,128)(2,1)S(1)}, u32[]{:S(2)}, u32[]{:S(2)}) collective-permute-start(bf16[128,768]{1,0:T(8,128)(2,1)S(1)} %get-tuple-element.52.refs_0_), channel_id=1, source_target_pairs={{0,1},{1,3},{3,2},{2,0},{4,5},{5,7},{7,6},{6,4},{8,9},{9,11},{11,1... | collective-permute-start | bytes 589832 | tf_op jit(solution)/shard_map/upper_1_lab_hop_1/ppermute | solution.py:200
  15.9 5.1 %collective-permute-start.5 = (bf16[64,768]{1,0:T(8,128)(2,1)S(1)}, bf16[64,768]{1,0:T(8,128)(2,1)S(1)}, u32[]{:S(2)}, u32[]{:S(2)}) collective-permute-start(bf16[64,768]{1,0:T(8,128)(2,1)S(1)} %get-tuple-element.45), channel_id=1, source_target_pairs={{0,28},{4,0},{8,4},{12,8},{16,12},{20,16},{24,20},{28,24},{1,29},{... | collective-permute-start | bytes 294920 | tf_op jit(solution)/shard_map/lower_doc_shift_1/ppermute | solution.py:200
  16.7 6.1 %collective-permute-start.6 = (bf16[64,768]{1,0:T(8,128)(2,1)S(1)}, bf16[64,768]{1,0:T(8,128)(2,1)S(1)}, u32[]{:S(2)}, u32[]{:S(2)}) collective-permute-start(bf16[64,768]{1,0:T(8,128)(2,1)S(1)} %get-tuple-element.46), channel_id=1, source_target_pairs={{0,24},{4,28},{8,0},{12,4},{16,8},{20,12},{24,16},{28,20},{1,25},{... | collective-permute-start | bytes 294920 | tf_op jit(solution)/shard_map/lower_doc_shift_2/ppermute | solution.py:200
  18.4 4.7 %collective-permute-start.7 = (bf16[64,768]{1,0:T(8,128)(2,1)S(1)}, bf16[64,768]{1,0:T(8,128)(2,1)S(1)}, u32[]{:S(2)}, u32[]{:S(2)}) collective-permute-start(bf16[64,768]{1,0:T(8,128)(2,1)S(1)} %get-tuple-element.47), channel_id=1, source_target_pairs={{0,20},{4,24},{8,28},{12,0},{16,4},{20,8},{24,12},{28,16},{1,21},{... | collective-permute-start | bytes 294920 | tf_op jit(solution)/shard_map/lower_doc_shift_3/ppermute | solution.py:200
  21.0 9.3 %collective-permute-start.4 = (bf16[144,768]{1,0:T(8,128)(2,1)S(1)}, bf16[144,768]{1,0:T(8,128)(2,1)S(1)}, u32[]{:S(2)}, u32[]{:S(2)}) collective-permute-start(bf16[144,768]{1,0:T(8,128)(2,1)S(1)} %collective-permute-done.refs_1_), channel_id=1, source_target_pairs={{0,1},{1,3},{3,2},{2,0},{4,5},{5,7},{7,6},{6,4},{8,9},{9,11},{11,1... | collective-permute-start | bytes 663560 | tf_op jit(solution)/shard_map/upper_0_lab_hop_2/ppermute | solution.py:200
  23.2 17.5 %collective-permute-start.21 = (bf16[128,768]{1,0:T(8,128)(2,1)S(1)}, bf16[128,768]{1,0:T(8,128)(2,1)S(1)}, u32[]{:S(2)}, u32[]{:S(2)}) collective-permute-start(bf16[128,768]{1,0:T(8,128)(2,1)S(1)} %constant_dynamic-update-slice_fusion.2.refs_2_), channel_id=1, source_target_pairs={{0,1},{1,3},{3,2},{2,0},{4,5},{5,7},{7,6},{6,4},{8,9},{9,11},{11,1... | collective-permute-start | bytes 589832 | tf_op jit(solution)/shard_map/part_0_lab_hop_1/ppermute | solution.py:200
  30.2 9.3 %collective-permute-start.8 = (bf16[144,768]{1,0:T(8,128)(2,1)S(1)}, bf16[144,768]{1,0:T(8,128)(2,1)S(1)}, u32[]{:S(2)}, u32[]{:S(2)}) collective-permute-start(bf16[144,768]{1,0:T(8,128)(2,1)S(1)} %collective-permute-done.4.refs_2_), channel_id=1, source_target_pairs={{0,1},{1,3},{3,2},{2,0},{4,5},{5,7},{7,6},{6,4},{8,9},{9,11},{11,1... | collective-permute-start | bytes 663560 | tf_op jit(solution)/shard_map/upper_0_lab_hop_3/ppermute | solution.py:200
  30.3 17.7 %collective-permute-start.15 = (bf16[128,768]{1,0:T(8,128)(2,1)S(1)}, bf16[128,768]{1,0:T(8,128)(2,1)S(1)}, u32[]{:S(2)}, u32[]{:S(2)}) collective-permute-start(bf16[128,768]{1,0:T(8,128)(2,1)S(1)} %constant_dynamic-update-slice_fusion.refs_2_), channel_id=1, source_target_pairs={{0,1},{1,3},{3,2},{2,0},{4,5},{5,7},{7,6},{6,4},{8,9},{9,11},{11,1... | collective-permute-start | bytes 589832 | tf_op jit(solution)/shard_map/part_1_lab_hop_1/ppermute | solution.py:200
  33.5 14.4 %collective-permute-start.12 = (bf16[128,768]{1,0:T(8,128)(2,1)S(1)}, bf16[128,768]{1,0:T(8,128)(2,1)S(1)}, u32[]{:S(2)}, u32[]{:S(2)}) collective-permute-start(bf16[128,768]{1,0:T(8,128)(2,1)S(1)} %collective-permute-done.11.refs_1_), channel_id=1, source_target_pairs={{0,1},{1,3},{3,2},{2,0},{4,5},{5,7},{7,6},{6,4},{8,9},{9,11},{11,1... | collective-permute-start | bytes 589832 | tf_op jit(solution)/shard_map/upper_1_lab_hop_2/ppermute | solution.py:200
  39.8 8.2 %collective-permute-start.16 = (bf16[144,768]{1,0:T(8,128)(2,1)S(1)}, bf16[144,768]{1,0:T(8,128)(2,1)S(1)}, u32[]{:S(2)}, u32[]{:S(2)}) collective-permute-start(bf16[144,768]{1,0:T(8,128)(2,1)S(1)} %get-tuple-element.58), channel_id=1, source_target_pairs={{0,28},{4,0},{8,4},{12,8},{16,12},{20,16},{24,20},{28,24},{1,29},{... | collective-permute-start | bytes 663560 | tf_op jit(solution)/shard_map/upper_0_doc_shift_1/ppermute | solution.py:200
  40.7 11.4 %collective-permute-start.22 = (bf16[128,768]{1,0:T(8,128)(2,1)S(1)}, bf16[128,768]{1,0:T(8,128)(2,1)S(1)}, u32[]{:S(2)}, u32[]{:S(2)}) collective-permute-start(bf16[128,768]{1,0:T(8,128)(2,1)S(1)} %collective-permute-done.21.refs_3_), channel_id=1, source_target_pairs={{0,1},{1,3},{3,2},{2,0},{4,5},{5,7},{7,6},{6,4},{8,9},{9,11},{11,1... | collective-permute-start | bytes 589832 | tf_op jit(solution)/shard_map/part_0_lab_hop_2/ppermute | solution.py:200
  40.8 11.4 %collective-permute-start.10 = (bf16[144,768]{1,0:T(8,128)(2,1)S(1)}, bf16[144,768]{1,0:T(8,128)(2,1)S(1)}, u32[]{:S(2)}, u32[]{:S(2)}) collective-permute-start(bf16[144,768]{1,0:T(8,128)(2,1)S(1)} %get-tuple-element.50), channel_id=1, source_target_pairs={{0,24},{4,28},{8,0},{12,4},{16,8},{20,12},{24,16},{28,20},{1,25},{... | collective-permute-start | bytes 663560 | tf_op jit(solution)/shard_map/upper_0_doc_shift_2/ppermute | solution.py:200
  47.9 8.7 %collective-permute-start.13 = (bf16[128,768]{1,0:T(8,128)(2,1)S(1)}, bf16[128,768]{1,0:T(8,128)(2,1)S(1)}, u32[]{:S(2)}, u32[]{:S(2)}) collective-permute-start(bf16[128,768]{1,0:T(8,128)(2,1)S(1)} %collective-permute-done.12.refs_2_), channel_id=1, source_target_pairs={{0,1},{1,3},{3,2},{2,0},{4,5},{5,7},{7,6},{6,4},{8,9},{9,11},{11,1... | collective-permute-start | bytes 589832 | tf_op jit(solution)/shard_map/upper_1_lab_hop_3/ppermute | solution.py:200
  48.0 12.9 %collective-permute-start.17 = (bf16[128,768]{1,0:T(8,128)(2,1)S(1)}, bf16[128,768]{1,0:T(8,128)(2,1)S(1)}, u32[]{:S(2)}, u32[]{:S(2)}) collective-permute-start(bf16[128,768]{1,0:T(8,128)(2,1)S(1)} %collective-permute-done.15.refs_3_), channel_id=1, source_target_pairs={{0,1},{1,3},{3,2},{2,0},{4,5},{5,7},{7,6},{6,4},{8,9},{9,11},{11,1... | collective-permute-start | bytes 589832 | tf_op jit(solution)/shard_map/part_1_lab_hop_2/ppermute | solution.py:200
  51.3 9.7 %collective-permute-start.9 = (bf16[144,768]{1,0:T(8,128)(2,1)S(1)}, bf16[144,768]{1,0:T(8,128)(2,1)S(1)}, u32[]{:S(2)}, u32[]{:S(2)}) collective-permute-start(bf16[144,768]{1,0:T(8,128)(2,1)S(1)} %get-tuple-element.49), channel_id=1, source_target_pairs={{0,20},{4,24},{8,28},{12,0},{16,4},{20,8},{24,12},{28,16},{1,21},{... | collective-permute-start | bytes 663560 | tf_op jit(solution)/shard_map/upper_0_doc_shift_3/ppermute | solution.py:200
  52.2 12.5 %collective-permute-start.23 = (bf16[128,768]{1,0:T(8,128)(2,1)S(1)}, bf16[128,768]{1,0:T(8,128)(2,1)S(1)}, u32[]{:S(2)}, u32[]{:S(2)}) collective-permute-start(bf16[128,768]{1,0:T(8,128)(2,1)S(1)} %collective-permute-done.22.refs_4_), channel_id=1, source_target_pairs={{0,1},{1,3},{3,2},{2,0},{4,5},{5,7},{7,6},{6,4},{8,9},{9,11},{11,1... | collective-permute-start | bytes 589832 | tf_op jit(solution)/shard_map/part_0_lab_hop_3/ppermute | solution.py:200
  56.9 9.4 %collective-permute-start.20 = (bf16[128,768]{1,0:T(8,128)(2,1)S(1)}, bf16[128,768]{1,0:T(8,128)(2,1)S(1)}, u32[]{:S(2)}, u32[]{:S(2)}) collective-permute-start(bf16[128,768]{1,0:T(8,128)(2,1)S(1)} %get-tuple-element.64), channel_id=1, source_target_pairs={{0,28},{4,0},{8,4},{12,8},{16,12},{20,16},{24,20},{28,24},{1,29},{... | collective-permute-start | bytes 589832 | tf_op jit(solution)/shard_map/upper_1_doc_shift_1/ppermute | solution.py:200
  57.0 11.3 %collective-permute-start.19 = (bf16[128,768]{1,0:T(8,128)(2,1)S(1)}, bf16[128,768]{1,0:T(8,128)(2,1)S(1)}, u32[]{:S(2)}, u32[]{:S(2)}) collective-permute-start(bf16[128,768]{1,0:T(8,128)(2,1)S(1)} %get-tuple-element.62), channel_id=1, source_target_pairs={{0,24},{4,28},{8,0},{12,4},{16,8},{20,12},{24,16},{28,20},{1,25},{... | collective-permute-start | bytes 589832 | tf_op jit(solution)/shard_map/upper_1_doc_shift_2/ppermute | solution.py:200
  60.9 7.4 %collective-permute-start.18 = (bf16[128,768]{1,0:T(8,128)(2,1)S(1)}, bf16[128,768]{1,0:T(8,128)(2,1)S(1)}, u32[]{:S(2)}, u32[]{:S(2)}) collective-permute-start(bf16[128,768]{1,0:T(8,128)(2,1)S(1)} %collective-permute-done.17.refs_4_), channel_id=1, source_target_pairs={{0,1},{1,3},{3,2},{2,0},{4,5},{5,7},{7,6},{6,4},{8,9},{9,11},{11,1... | collective-permute-start | bytes 589832 | tf_op jit(solution)/shard_map/part_1_lab_hop_3/ppermute | solution.py:200
  61.0 8.9 %collective-permute-start.14 = (bf16[128,768]{1,0:T(8,128)(2,1)S(1)}, bf16[128,768]{1,0:T(8,128)(2,1)S(1)}, u32[]{:S(2)}, u32[]{:S(2)}) collective-permute-start(bf16[128,768]{1,0:T(8,128)(2,1)S(1)} %get-tuple-element.57), channel_id=1, source_target_pairs={{0,20},{4,24},{8,28},{12,0},{16,4},{20,8},{24,12},{28,16},{1,21},{... | collective-permute-start | bytes 589832 | tf_op jit(solution)/shard_map/upper_1_doc_shift_3/ppermute | solution.py:200
  (7 other events, 85.9 us)

commit v9 on v8

--- a/solution.py
+++ b/solution.py
@@ -269,7 +269,7 @@
     ahead = select(which_upper, held[0])
     panels = [[ahead[0]]] + [[shift("upper_0", s, ahead[s])] for s in range(1, STEPS)]
     for r in range(3, lab_count):
-        hop("upper_1", held[1], ahead[0])
+        hop("upper_1", held[1], panels[1][0])
     hop("part_1", parts[1])
     found = select(which_upper, [after(held[1][0], panels[2][0]), *held[1][1:]])
     panels[0].append(found[0])

time: 72.8 us -> 72.8 us (level)
  no operation moved by 1% of the time
where the time goes in v9:
time: 72.8 us; the launch traced here: 72.5 us
  waiting for transfers between devices  31.8 us (44%)
  starting transfers between devices  24.5 us (34%)
  Pallas kernels  9.18 us (13%)
  local copies, waits for them, and re-layouts  4.68 us (6%)
  other arithmetic  1.42 us (2%)
  between operations  0.91 us (1%)
    ppermute x24, waiting for transfers between devices, send(): return lax.ppermute(value, axis, pairs)  31.8 us
    ppermute x24, starting transfers between devices, send(): return lax.ppermute(value, axis, pairs)  24.5 us
    pallas_call x4, Pallas kernels, update(): pl.pallas_call(functools.partial(update_kernel, first, last, len(pieces),...  7.38 us
    unnamed x16, local copies, waits for them, and re-layouts  2.04 us
  transfers between devices with their start and end apart: 24, of which 11 were waited for; matrix products, arithmetic and copies ran while one was open for 6% of the time, Pallas kernels for 8%

profile of v9, /device:TPU:0, one launch (start us, length us, event | category | flops | bytes accessed | tf_op | source)
XLA Modules:
  0.0 72.5 jit_solution(7368210292904602149)
XLA Ops:
  0.7 1.2 %pack_pieces.1 = (bf16[64,768]{1,0:T(8,128)(2,1)S(1)}, bf16[64,768]{1,0:T(8,128)(2,1)S(1)}, bf16[64,768]{1,0:T(8,128)(2,1)S(1)}, bf16[64,768]{1,0:T(8,128)(2,1)S(1)}) custom-call(bf16[512,768]{1,0:T(8,128)(2,1)} %source.1), custom_call_target="tpu_custom_call" | custom-call | tf_op jit(solution)/shard_map/pack_pieces/pallas_call | solution.py:74
  1.8 3.1 %collective-permute-start.1 = (bf16[64,768]{1,0:T(8,128)(2,1)S(1)}, bf16[64,768]{1,0:T(8,128)(2,1)S(1)}, u32[]{:S(2)}, u32[]{:S(2)}) collective-permute-start(bf16[64,768]{1,0:T(8,128)(2,1)S(1)} %get-tuple-element.40), channel_id=1, source_target_pairs={{0,1},{1,2},{2,3},{3,0},{4,5},{5,6},{6,7},{7,4},{8,9},{9,10},{10,1... | collective-permute-start | bytes 294920 | tf_op jit(solution)/shard_map/lower_lab_shift_1/ppermute | solution.py:200
  4.9 2.6 %collective-permute-start.2 = (bf16[64,768]{1,0:T(8,128)(2,1)S(1)}, bf16[64,768]{1,0:T(8,128)(2,1)S(1)}, u32[]{:S(2)}, u32[]{:S(2)}) collective-permute-start(bf16[64,768]{1,0:T(8,128)(2,1)S(1)} %get-tuple-element.41), channel_id=1, source_target_pairs={{0,2},{1,3},{2,0},{3,1},{4,6},{5,7},{6,4},{7,5},{8,10},{9,11},{10,... | collective-permute-start | bytes 294920 | tf_op jit(solution)/shard_map/lower_lab_shift_2/ppermute | solution.py:200
  7.5 1.3 %collective-permute-start.3 = (bf16[64,768]{1,0:T(8,128)(2,1)S(1)}, bf16[64,768]{1,0:T(8,128)(2,1)S(1)}, u32[]{:S(2)}, u32[]{:S(2)}) collective-permute-start(bf16[64,768]{1,0:T(8,128)(2,1)S(1)} %get-tuple-element.42), channel_id=1, source_target_pairs={{0,3},{1,0},{2,1},{3,2},{4,7},{5,4},{6,5},{7,6},{8,11},{9,8},{10,9... | collective-permute-start | bytes 294920 | tf_op jit(solution)/shard_map/lower_lab_shift_3/ppermute | solution.py:200
  10.3 0.8 %dynamic_slice.25 = s32[256]{0:T(256)S(1)} dynamic-slice(s32[8192]{0:T(1024)} %param.11, s32[]{:T(128)S(6)} %select_n.137), dynamic_slice_sizes={256} | dynamic-slice | bytes 2052 | tf_op jit(solution)/shard_map/dynamic_slice | solution.py:239
  15.9 0.8 %collective-permute-start.5 = (bf16[64,768]{1,0:T(8,128)(2,1)S(1)}, bf16[64,768]{1,0:T(8,128)(2,1)S(1)}, u32[]{:S(2)}, u32[]{:S(2)}) collective-permute-start(bf16[64,768]{1,0:T(8,128)(2,1)S(1)} %get-tuple-element.45), channel_id=1, source_target_pairs={{0,28},{4,0},{8,4},{12,8},{16,12},{20,16},{24,20},{28,24},{1,29},{... | collective-permute-start | bytes 294920 | tf_op jit(solution)/shard_map/lower_doc_shift_1/ppermute | solution.py:200
  16.7 1.7 %collective-permute-start.6 = (bf16[64,768]{1,0:T(8,128)(2,1)S(1)}, bf16[64,768]{1,0:T(8,128)(2,1)S(1)}, u32[]{:S(2)}, u32[]{:S(2)}) collective-permute-start(bf16[64,768]{1,0:T(8,128)(2,1)S(1)} %get-tuple-element.46), channel_id=1, source_target_pairs={{0,24},{4,28},{8,0},{12,4},{16,8},{20,12},{24,16},{28,20},{1,25},{... | collective-permute-start | bytes 294920 | tf_op jit(solution)/shard_map/lower_doc_shift_2/ppermute | solution.py:200
  18.7 2.2 %collective-permute-done.refs_1_ = bf16[144,768]{1,0:T(8,128)(2,1)S(1)} collective-permute-done((bf16[144,768]{1,0:T(8,128)(2,1)S(1)}, bf16[144,768]{1,0:T(8,128)(2,1)S(1)}, u32[]{:S(2)}, u32[]{:S(2)}) %collective-permute-start) | collective-permute-done | bytes 221216 | tf_op jit(solution)/shard_map/upper_0_lab_hop_1/ppermute | solution.py:200
  21.0 1.7 %collective-permute-done.6 = bf16[64,768]{1,0:T(8,128)(2,1)S(1)} collective-permute-done((bf16[64,768]{1,0:T(8,128)(2,1)S(1)}, bf16[64,768]{1,0:T(8,128)(2,1)S(1)}, u32[]{:S(2)}, u32[]{:S(2)}) %collective-permute-start.6) | collective-permute-done | bytes 98336 | tf_op jit(solution)/shard_map/lower_doc_shift_2/ppermute | solution.py:200
  23.2 1.5 %collective-permute-start.21 = (bf16[128,768]{1,0:T(8,128)(2,1)S(1)}, bf16[128,768]{1,0:T(8,128)(2,1)S(1)}, u32[]{:S(2)}, u32[]{:S(2)}) collective-permute-start(bf16[128,768]{1,0:T(8,128)(2,1)S(1)} %constant_dynamic-update-slice_fusion.2.refs_2_), channel_id=1, source_target_pairs={{0,1},{1,3},{3,2},{2,0},{4,5},{5,7},{7,6},{6,4},{8,9},{9,11},{11,1... | collective-permute-start | bytes 589832 | tf_op jit(solution)/shard_map/part_0_lab_hop_1/ppermute | solution.py:200
  24.6 5.6 %collective-permute-done.4.refs_2_ = bf16[144,768]{1,0:T(8,128)(2,1)S(1)} collective-permute-done((bf16[144,768]{1,0:T(8,128)(2,1)S(1)}, bf16[144,768]{1,0:T(8,128)(2,1)S(1)}, u32[]{:S(2)}, u32[]{:S(2)}) %collective-permute-start.4) | collective-permute-done | bytes 221216 | tf_op jit(solution)/shard_map/upper_0_lab_hop_2/ppermute | solution.py:200
  30.3 3.2 %collective-permute-start.16 = (bf16[128,768]{1,0:T(8,128)(2,1)S(1)}, bf16[128,768]{1,0:T(8,128)(2,1)S(1)}, u32[]{:S(2)}, u32[]{:S(2)}) collective-permute-start(bf16[128,768]{1,0:T(8,128)(2,1)S(1)} %constant_dynamic-update-slice_fusion.refs_2_), channel_id=1, source_target_pairs={{0,1},{1,3},{3,2},{2,0},{4,5},{5,7},{7,6},{6,4},{8,9},{9,11},{11,1... | collective-permute-start | bytes 589832 | tf_op jit(solution)/shard_map/part_1_lab_hop_1/ppermute | solution.py:200
  33.6 5.9 %collective-permute-done.8.refs_3_ = bf16[144,768]{1,0:T(8,128)(2,1)S(1)} collective-permute-done((bf16[144,768]{1,0:T(8,128)(2,1)S(1)}, bf16[144,768]{1,0:T(8,128)(2,1)S(1)}, u32[]{:S(2)}, u32[]{:S(2)}) %collective-permute-start.8) | collective-permute-done | bytes 221216 | tf_op jit(solution)/shard_map/upper_0_lab_hop_3/ppermute | solution.py:200
  40.8 1.9 %collective-permute-start.10 = (bf16[144,768]{1,0:T(8,128)(2,1)S(1)}, bf16[144,768]{1,0:T(8,128)(2,1)S(1)}, u32[]{:S(2)}, u32[]{:S(2)}) collective-permute-start(bf16[144,768]{1,0:T(8,128)(2,1)S(1)} %get-tuple-element.50), channel_id=1, source_target_pairs={{0,24},{4,28},{8,0},{12,4},{16,8},{20,12},{24,16},{28,20},{1,25},{... | collective-permute-start | bytes 663560 | tf_op jit(solution)/shard_map/upper_0_doc_shift_2/ppermute | solution.py:200
  42.7 5.2 %collective-permute-done.12.refs_2_ = bf16[128,768]{1,0:T(8,128)(2,1)S(1)} collective-permute-done((bf16[128,768]{1,0:T(8,128)(2,1)S(1)}, bf16[128,768]{1,0:T(8,128)(2,1)S(1)}, u32[]{:S(2)}, u32[]{:S(2)}) %collective-permute-start.12) | collective-permute-done | bytes 196640 | tf_op jit(solution)/shard_map/upper_1_lab_hop_2/ppermute | solution.py:200
  48.0 3.2 %collective-permute-start.17 = (bf16[128,768]{1,0:T(8,128)(2,1)S(1)}, bf16[128,768]{1,0:T(8,128)(2,1)S(1)}, u32[]{:S(2)}, u32[]{:S(2)}) collective-permute-start(bf16[128,768]{1,0:T(8,128)(2,1)S(1)} %collective-permute-done.16.refs_3_), channel_id=1, source_target_pairs={{0,1},{1,3},{3,2},{2,0},{4,5},{5,7},{7,6},{6,4},{8,9},{9,11},{11,1... | collective-permute-start | bytes 589832 | tf_op jit(solution)/shard_map/part_1_lab_hop_2/ppermute | solution.py:200
  52.0 4.7 %collective-permute-done.14.refs_3_ = bf16[128,768]{1,0:T(8,128)(2,1)S(1)} collective-permute-done((bf16[128,768]{1,0:T(8,128)(2,1)S(1)}, bf16[128,768]{1,0:T(8,128)(2,1)S(1)}, u32[]{:S(2)}, u32[]{:S(2)}) %collective-permute-start.14) | collective-permute-done | bytes 196640 | tf_op jit(solution)/shard_map/upper_1_lab_hop_3/ppermute | solution.py:200
  57.0 2.5 %collective-permute-start.19 = (bf16[128,768]{1,0:T(8,128)(2,1)S(1)}, bf16[128,768]{1,0:T(8,128)(2,1)S(1)}, u32[]{:S(2)}, u32[]{:S(2)}) collective-permute-start(bf16[128,768]{1,0:T(8,128)(2,1)S(1)} %get-tuple-element.61), channel_id=1, source_target_pairs={{0,24},{4,28},{8,0},{12,4},{16,8},{20,12},{24,16},{28,20},{1,25},{... | collective-permute-start | bytes 589832 | tf_op jit(solution)/shard_map/upper_1_doc_shift_2/ppermute | solution.py:200
  59.5 1.4 %collective-permute-done.17.refs_4_ = bf16[128,768]{1,0:T(8,128)(2,1)S(1)} collective-permute-done((bf16[128,768]{1,0:T(8,128)(2,1)S(1)}, bf16[128,768]{1,0:T(8,128)(2,1)S(1)}, u32[]{:S(2)}, u32[]{:S(2)}) %collective-permute-start.17) | collective-permute-done | bytes 196640 | tf_op jit(solution)/shard_map/part_1_lab_hop_2/ppermute | solution.py:200
  61.1 3.6 %collective-permute-done.23.refs_5_ = bf16[128,768]{1,0:T(8,128)(2,1)S(1)} collective-permute-done((bf16[128,768]{1,0:T(8,128)(2,1)S(1)}, bf16[128,768]{1,0:T(8,128)(2,1)S(1)}, u32[]{:S(2)}, u32[]{:S(2)}) %collective-permute-start.23) | collective-permute-done | bytes 196640 | tf_op jit(solution)/shard_map/part_0_lab_hop_3/ppermute | solution.py:200
  64.7 1.6 %update_block.4 = (f32[256,768]{1,0:T(8,128)S(1)}, f32[256,768]{1,0:T(8,128)S(1)}) custom-call(bf16[144,768]{1,0:T(8,128)(2,1)S(1)} %get-tuple-element.66.refs_0_, bf16[128,768]{1,0:T(8,128)(2,1)S(1)} %get-tuple-element.67.refs_1_, bf16[128,768]{1,0:T(8,128)(2,1)S(1)} %constant_dynamic-update-slice_fusion.2.refs_2_, ...), custom_call_target="tpu_custom_call" | custom-call | flops 805306368 | bytes 3932160 | tf_op jit(solution)/shard_map/update_block/pallas_call | solution.py:177
  66.3 1.6 %update_block.5 = (f32[256,768]{1,0:T(8,128)S(1)}, f32[256,768]{1,0:T(8,128)S(1)}) custom-call(bf16[144,768]{1,0:T(8,128)(2,1)S(1)} %collective-permute-done.13.refs_0_, bf16[128,768]{1,0:T(8,128)(2,1)S(1)} %collective-permute-done.20.refs_1_, bf16[128,768]{1,0:T(8,128)(2,1)S(1)} %constant_dynamic-update-slice_fusion.2.refs_2_, ...), custom_call_target="tpu_custom_call" | custom-call | flops 805306368 | bytes 3932160 | tf_op jit(solution)/shard_map/update_block/pallas_call | solution.py:177
  68.3 1.6 %update_block.6 = (f32[256,768]{1,0:T(8,128)S(1)}, f32[256,768]{1,0:T(8,128)S(1)}) custom-call(bf16[144,768]{1,0:T(8,128)(2,1)S(1)} %collective-permute-done.10.refs_0_, bf16[128,768]{1,0:T(8,128)(2,1)S(1)} %collective-permute-done.19.refs_1_, bf16[128,768]{1,0:T(8,128)(2,1)S(1)} %constant_dynamic-update-slice_fusion.refs_2_, ...), custom_call_target="tpu_custom_call" | custom-call | flops 805306368 | bytes 3932160 | tf_op jit(solution)/shard_map/update_block/pallas_call | solution.py:177
  69.9 2.6 %update_block.7 = (f32[256,768]{1,0:T(8,128)}, f32[256,768]{1,0:T(8,128)}) custom-call(bf16[144,768]{1,0:T(8,128)(2,1)S(1)} %collective-permute-done.9.refs_0_, bf16[128,768]{1,0:T(8,128)(2,1)S(1)} %collective-permute-done.15.refs_1_, bf16[128,768]{1,0:T(8,128)(2,1)S(1)} %constant_dynamic-update-slice_fusion.refs_2_, ...), custom_call_target="tpu_custom_call" | custom-call | flops 805306368 | bytes 3932160 | tf_op jit(solution)/shard_map/update_block/pallas_call | solution.py:177
  (72 shorter events, 10.0 us)
Async XLA Ops:
  1.8 13.8 %collective-permute-start.1 = (bf16[64,768]{1,0:T(8,128)(2,1)S(1)}, bf16[64,768]{1,0:T(8,128)(2,1)S(1)}, u32[]{:S(2)}, u32[]{:S(2)}) collective-permute-start(bf16[64,768]{1,0:T(8,128)(2,1)S(1)} %get-tuple-element.40), channel_id=1, source_target_pairs={{0,1},{1,2},{2,3},{3,0},{4,5},{5,6},{6,7},{7,4},{8,9},{9,10},{10,1... | collective-permute-start | bytes 294920 | tf_op jit(solution)/shard_map/lower_lab_shift_1/ppermute | solution.py:200
  4.9 10.7 %collective-permute-start.2 = (bf16[64,768]{1,0:T(8,128)(2,1)S(1)}, bf16[64,768]{1,0:T(8,128)(2,1)S(1)}, u32[]{:S(2)}, u32[]{:S(2)}) collective-permute-start(bf16[64,768]{1,0:T(8,128)(2,1)S(1)} %get-tuple-element.41), channel_id=1, source_target_pairs={{0,2},{1,3},{2,0},{3,1},{4,6},{5,7},{6,4},{7,5},{8,10},{9,11},{10,... | collective-permute-start | bytes 294920 | tf_op jit(solution)/shard_map/lower_lab_shift_2/ppermute | solution.py:200
  7.5 8.2 %collective-permute-start.3 = (bf16[64,768]{1,0:T(8,128)(2,1)S(1)}, bf16[64,768]{1,0:T(8,128)(2,1)S(1)}, u32[]{:S(2)}, u32[]{:S(2)}) collective-permute-start(bf16[64,768]{1,0:T(8,128)(2,1)S(1)} %get-tuple-element.42), channel_id=1, source_target_pairs={{0,3},{1,0},{2,1},{3,2},{4,7},{5,4},{6,5},{7,6},{8,11},{9,8},{10,9... | collective-permute-start | bytes 294920 | tf_op jit(solution)/shard_map/lower_lab_shift_3/ppermute | solution.py:200
  9.0 12.0 %collective-permute-start = (bf16[144,768]{1,0:T(8,128)(2,1)S(1)}, bf16[144,768]{1,0:T(8,128)(2,1)S(1)}, u32[]{:S(2)}, u32[]{:S(2)}) collective-permute-start(bf16[144,768]{1,0:T(8,128)(2,1)S(1)} %fusion.2.refs_0_), channel_id=1, source_target_pairs={{0,1},{1,3},{3,2},{2,0},{4,5},{5,7},{7,6},{6,4},{8,9},{9,11},{11,1... | collective-permute-start | bytes 663560 | tf_op jit(solution)/shard_map/upper_0_lab_hop_1/ppermute | solution.py:200
  9.7 23.8 %collective-permute-start.11 = (bf16[128,768]{1,0:T(8,128)(2,1)S(1)}, bf16[128,768]{1,0:T(8,128)(2,1)S(1)}, u32[]{:S(2)}, u32[]{:S(2)}) collective-permute-start(bf16[128,768]{1,0:T(8,128)(2,1)S(1)} %get-tuple-element.52.refs_0_), channel_id=1, source_target_pairs={{0,1},{1,3},{3,2},{2,0},{4,5},{5,7},{7,6},{6,4},{8,9},{9,11},{11,1... | collective-permute-start | bytes 589832 | tf_op jit(solution)/shard_map/upper_1_lab_hop_1/ppermute | solution.py:200
  15.9 5.1 %collective-permute-start.5 = (bf16[64,768]{1,0:T(8,128)(2,1)S(1)}, bf16[64,768]{1,0:T(8,128)(2,1)S(1)}, u32[]{:S(2)}, u32[]{:S(2)}) collective-permute-start(bf16[64,768]{1,0:T(8,128)(2,1)S(1)} %get-tuple-element.45), channel_id=1, source_target_pairs={{0,28},{4,0},{8,4},{12,8},{16,12},{20,16},{24,20},{28,24},{1,29},{... | collective-permute-start | bytes 294920 | tf_op jit(solution)/shard_map/lower_doc_shift_1/ppermute | solution.py:200
  16.7 6.1 %collective-permute-start.6 = (bf16[64,768]{1,0:T(8,128)(2,1)S(1)}, bf16[64,768]{1,0:T(8,128)(2,1)S(1)}, u32[]{:S(2)}, u32[]{:S(2)}) collective-permute-start(bf16[64,768]{1,0:T(8,128)(2,1)S(1)} %get-tuple-element.46), channel_id=1, source_target_pairs={{0,24},{4,28},{8,0},{12,4},{16,8},{20,12},{24,16},{28,20},{1,25},{... | collective-permute-start | bytes 294920 | tf_op jit(solution)/shard_map/lower_doc_shift_2/ppermute | solution.py:200
  18.4 4.7 %collective-permute-start.7 = (bf16[64,768]{1,0:T(8,128)(2,1)S(1)}, bf16[64,768]{1,0:T(8,128)(2,1)S(1)}, u32[]{:S(2)}, u32[]{:S(2)}) collective-permute-start(bf16[64,768]{1,0:T(8,128)(2,1)S(1)} %get-tuple-element.47), channel_id=1, source_target_pairs={{0,20},{4,24},{8,28},{12,0},{16,4},{20,8},{24,12},{28,16},{1,21},{... | collective-permute-start | bytes 294920 | tf_op jit(solution)/shard_map/lower_doc_shift_3/ppermute | solution.py:200
  21.0 9.3 %collective-permute-start.4 = (bf16[144,768]{1,0:T(8,128)(2,1)S(1)}, bf16[144,768]{1,0:T(8,128)(2,1)S(1)}, u32[]{:S(2)}, u32[]{:S(2)}) collective-permute-start(bf16[144,768]{1,0:T(8,128)(2,1)S(1)} %collective-permute-done.refs_1_), channel_id=1, source_target_pairs={{0,1},{1,3},{3,2},{2,0},{4,5},{5,7},{7,6},{6,4},{8,9},{9,11},{11,1... | collective-permute-start | bytes 663560 | tf_op jit(solution)/shard_map/upper_0_lab_hop_2/ppermute | solution.py:200
  23.2 17.5 %collective-permute-start.21 = (bf16[128,768]{1,0:T(8,128)(2,1)S(1)}, bf16[128,768]{1,0:T(8,128)(2,1)S(1)}, u32[]{:S(2)}, u32[]{:S(2)}) collective-permute-start(bf16[128,768]{1,0:T(8,128)(2,1)S(1)} %constant_dynamic-update-slice_fusion.2.refs_2_), channel_id=1, source_target_pairs={{0,1},{1,3},{3,2},{2,0},{4,5},{5,7},{7,6},{6,4},{8,9},{9,11},{11,1... | collective-permute-start | bytes 589832 | tf_op jit(solution)/shard_map/part_0_lab_hop_1/ppermute | solution.py:200
  30.2 9.3 %collective-permute-start.8 = (bf16[144,768]{1,0:T(8,128)(2,1)S(1)}, bf16[144,768]{1,0:T(8,128)(2,1)S(1)}, u32[]{:S(2)}, u32[]{:S(2)}) collective-permute-start(bf16[144,768]{1,0:T(8,128)(2,1)S(1)} %collective-permute-done.4.refs_2_), channel_id=1, source_target_pairs={{0,1},{1,3},{3,2},{2,0},{4,5},{5,7},{7,6},{6,4},{8,9},{9,11},{11,1... | collective-permute-start | bytes 663560 | tf_op jit(solution)/shard_map/upper_0_lab_hop_3/ppermute | solution.py:200
  30.3 17.7 %collective-permute-start.16 = (bf16[128,768]{1,0:T(8,128)(2,1)S(1)}, bf16[128,768]{1,0:T(8,128)(2,1)S(1)}, u32[]{:S(2)}, u32[]{:S(2)}) collective-permute-start(bf16[128,768]{1,0:T(8,128)(2,1)S(1)} %constant_dynamic-update-slice_fusion.refs_2_), channel_id=1, source_target_pairs={{0,1},{1,3},{3,2},{2,0},{4,5},{5,7},{7,6},{6,4},{8,9},{9,11},{11,1... | collective-permute-start | bytes 589832 | tf_op jit(solution)/shard_map/part_1_lab_hop_1/ppermute | solution.py:200
  33.5 14.4 %collective-permute-start.12 = (bf16[128,768]{1,0:T(8,128)(2,1)S(1)}, bf16[128,768]{1,0:T(8,128)(2,1)S(1)}, u32[]{:S(2)}, u32[]{:S(2)}) collective-permute-start(bf16[128,768]{1,0:T(8,128)(2,1)S(1)} %collective-permute-done.11.refs_1_), channel_id=1, source_target_pairs={{0,1},{1,3},{3,2},{2,0},{4,5},{5,7},{7,6},{6,4},{8,9},{9,11},{11,1... | collective-permute-start | bytes 589832 | tf_op jit(solution)/shard_map/upper_1_lab_hop_2/ppermute | solution.py:200
  39.8 8.2 %collective-permute-start.13 = (bf16[144,768]{1,0:T(8,128)(2,1)S(1)}, bf16[144,768]{1,0:T(8,128)(2,1)S(1)}, u32[]{:S(2)}, u32[]{:S(2)}) collective-permute-start(bf16[144,768]{1,0:T(8,128)(2,1)S(1)} %get-tuple-element.54), channel_id=1, source_target_pairs={{0,28},{4,0},{8,4},{12,8},{16,12},{20,16},{24,20},{28,24},{1,29},{... | collective-permute-start | bytes 663560 | tf_op jit(solution)/shard_map/upper_0_doc_shift_1/ppermute | solution.py:200
  40.7 11.2 %collective-permute-start.22 = (bf16[128,768]{1,0:T(8,128)(2,1)S(1)}, bf16[128,768]{1,0:T(8,128)(2,1)S(1)}, u32[]{:S(2)}, u32[]{:S(2)}) collective-permute-start(bf16[128,768]{1,0:T(8,128)(2,1)S(1)} %collective-permute-done.21.refs_3_), channel_id=1, source_target_pairs={{0,1},{1,3},{3,2},{2,0},{4,5},{5,7},{7,6},{6,4},{8,9},{9,11},{11,1... | collective-permute-start | bytes 589832 | tf_op jit(solution)/shard_map/part_0_lab_hop_2/ppermute | solution.py:200
  40.8 11.1 %collective-permute-start.10 = (bf16[144,768]{1,0:T(8,128)(2,1)S(1)}, bf16[144,768]{1,0:T(8,128)(2,1)S(1)}, u32[]{:S(2)}, u32[]{:S(2)}) collective-permute-start(bf16[144,768]{1,0:T(8,128)(2,1)S(1)} %get-tuple-element.50), channel_id=1, source_target_pairs={{0,24},{4,28},{8,0},{12,4},{16,8},{20,12},{24,16},{28,20},{1,25},{... | collective-permute-start | bytes 663560 | tf_op jit(solution)/shard_map/upper_0_doc_shift_2/ppermute | solution.py:200
  47.9 8.7 %collective-permute-start.14 = (bf16[128,768]{1,0:T(8,128)(2,1)S(1)}, bf16[128,768]{1,0:T(8,128)(2,1)S(1)}, u32[]{:S(2)}, u32[]{:S(2)}) collective-permute-start(bf16[128,768]{1,0:T(8,128)(2,1)S(1)} %collective-permute-done.12.refs_2_), channel_id=1, source_target_pairs={{0,1},{1,3},{3,2},{2,0},{4,5},{5,7},{7,6},{6,4},{8,9},{9,11},{11,1... | collective-permute-start | bytes 589832 | tf_op jit(solution)/shard_map/upper_1_lab_hop_3/ppermute | solution.py:200
  48.0 12.9 %collective-permute-start.17 = (bf16[128,768]{1,0:T(8,128)(2,1)S(1)}, bf16[128,768]{1,0:T(8,128)(2,1)S(1)}, u32[]{:S(2)}, u32[]{:S(2)}) collective-permute-start(bf16[128,768]{1,0:T(8,128)(2,1)S(1)} %collective-permute-done.16.refs_3_), channel_id=1, source_target_pairs={{0,1},{1,3},{3,2},{2,0},{4,5},{5,7},{7,6},{6,4},{8,9},{9,11},{11,1... | collective-permute-start | bytes 589832 | tf_op jit(solution)/shard_map/part_1_lab_hop_2/ppermute | solution.py:200
  51.2 9.8 %collective-permute-start.9 = (bf16[144,768]{1,0:T(8,128)(2,1)S(1)}, bf16[144,768]{1,0:T(8,128)(2,1)S(1)}, u32[]{:S(2)}, u32[]{:S(2)}) collective-permute-start(bf16[144,768]{1,0:T(8,128)(2,1)S(1)} %get-tuple-element.49), channel_id=1, source_target_pairs={{0,20},{4,24},{8,28},{12,0},{16,4},{20,8},{24,12},{28,16},{1,21},{... | collective-permute-start | bytes 663560 | tf_op jit(solution)/shard_map/upper_0_doc_shift_3/ppermute | solution.py:200
  51.9 12.8 %collective-permute-start.23 = (bf16[128,768]{1,0:T(8,128)(2,1)S(1)}, bf16[128,768]{1,0:T(8,128)(2,1)S(1)}, u32[]{:S(2)}, u32[]{:S(2)}) collective-permute-start(bf16[128,768]{1,0:T(8,128)(2,1)S(1)} %collective-permute-done.22.refs_4_), channel_id=1, source_target_pairs={{0,1},{1,3},{3,2},{2,0},{4,5},{5,7},{7,6},{6,4},{8,9},{9,11},{11,1... | collective-permute-start | bytes 589832 | tf_op jit(solution)/shard_map/part_0_lab_hop_3/ppermute | solution.py:200
  56.9 9.3 %collective-permute-start.20 = (bf16[128,768]{1,0:T(8,128)(2,1)S(1)}, bf16[128,768]{1,0:T(8,128)(2,1)S(1)}, u32[]{:S(2)}, u32[]{:S(2)}) collective-permute-start(bf16[128,768]{1,0:T(8,128)(2,1)S(1)} %get-tuple-element.63), channel_id=1, source_target_pairs={{0,28},{4,0},{8,4},{12,8},{16,12},{20,16},{24,20},{28,24},{1,29},{... | collective-permute-start | bytes 589832 | tf_op jit(solution)/shard_map/upper_1_doc_shift_1/ppermute | solution.py:200
  57.0 11.3 %collective-permute-start.19 = (bf16[128,768]{1,0:T(8,128)(2,1)S(1)}, bf16[128,768]{1,0:T(8,128)(2,1)S(1)}, u32[]{:S(2)}, u32[]{:S(2)}) collective-permute-start(bf16[128,768]{1,0:T(8,128)(2,1)S(1)} %get-tuple-element.61), channel_id=1, source_target_pairs={{0,24},{4,28},{8,0},{12,4},{16,8},{20,12},{24,16},{28,20},{1,25},{... | collective-permute-start | bytes 589832 | tf_op jit(solution)/shard_map/upper_1_doc_shift_2/ppermute | solution.py:200
  60.9 7.4 %collective-permute-start.18 = (bf16[128,768]{1,0:T(8,128)(2,1)S(1)}, bf16[128,768]{1,0:T(8,128)(2,1)S(1)}, u32[]{:S(2)}, u32[]{:S(2)}) collective-permute-start(bf16[128,768]{1,0:T(8,128)(2,1)S(1)} %collective-permute-done.17.refs_4_), channel_id=1, source_target_pairs={{0,1},{1,3},{3,2},{2,0},{4,5},{5,7},{7,6},{6,4},{8,9},{9,11},{11,1... | collective-permute-start | bytes 589832 | tf_op jit(solution)/shard_map/part_1_lab_hop_3/ppermute | solution.py:200
  61.0 8.9 %collective-permute-start.15 = (bf16[128,768]{1,0:T(8,128)(2,1)S(1)}, bf16[128,768]{1,0:T(8,128)(2,1)S(1)}, u32[]{:S(2)}, u32[]{:S(2)}) collective-permute-start(bf16[128,768]{1,0:T(8,128)(2,1)S(1)} %get-tuple-element.57), channel_id=1, source_target_pairs={{0,20},{4,24},{8,28},{12,0},{16,4},{20,8},{24,12},{28,16},{1,21},{... | collective-permute-start | bytes 589832 | tf_op jit(solution)/shard_map/upper_1_doc_shift_3/ppermute | solution.py:200
  (7 other events, 85.9 us)
